TPU v7x, 256 devices: a whole 4x4x8 slice. The times are simulated.
256 devices in a mesh: chan: 4 (over x_hi, core), wide: 64 (over z, y, x_lo).
Axes of the slice: x: 4 (x_hi: 2, x_lo: 2; x = x_hi * 2 + x_lo), y: 4, z: 8, core: 2. Of those that a mesh axis runs over, the one named last changes fastest.
Arguments:
- echoes: float32 [2, 4, 1024, 8192], P(None, 'chan', 'wide'), may hold values from -6 to 6
- range_chirp: float32 [2, 4, 512], P(None, 'chan'), may hold values from -0.1875 to 0.1875
- azimuth_filter: float32 [2, 4, 1024], P(None, 'chan'), may hold values from -0.125 to 0.125
- pairing: int32 [4], replicated, may hold values from 0 to 3, each once
- offsets: int32 [8, 2], replicated, may hold values from -4 to 4, as said below
Outputs:
- coherence: float32 [2, 1024, 8192], P(None, 'chan', 'wide')
Inputs may be any that keep to these rules, and one draw needn't show every extreme that they name: `pairing`: each receiver appears once. both -4 and 4 appear among the offsets.
All inputs are finite; a program needn't handle non-finite values.
Results may differ from a plain program's by a relative error of at most 0.00012.
Values sent between devices are 32-bit elements; how exact they have to be, the bound alone decides.
No kernel may reach another device: no remote copies, remote signals or barrier semaphores. Data moves between devices by JAX's collectives and lax.ppermute only.
A program may use at most 128 MiB of HBM per device.

v0:
```python
import jax
import jax.numpy as jnp
from jax import lax
from jax.sharding import PartitionSpec as P

RADIUS = 4


def extended_2(shard, sides, width):
    for axis, dim in sides:
        devices, length = (lax.axis_size(axis), shard.shape[dim])
        up = [(i, (i + 1) % devices) for i in range(devices - 1)]
        down = [(j, i) for i, j in up]
        last = lax.slice_in_dim(shard, length - width, length, axis=dim)
        first = lax.slice_in_dim(shard, 0, width, axis=dim)
        before = lax.ppermute(last, axis, up)
        after = lax.ppermute(first, axis, down)
        shard = jnp.concatenate([before, shard, after], axis=dim)
    return shard


def band(filter_taps, out_count, in_width):
    tap_count = filter_taps.shape[0]
    padded_line = jnp.concatenate(
        [filter_taps, jnp.zeros((in_width + 1 - tap_count,), jnp.float32)]
    )
    tiled = jnp.tile(padded_line, out_count)[: out_count * in_width]
    return tiled.reshape(out_count, in_width)


def range_matrix(chirp, range_block):
    in_width = range_block + chirp.shape[1]
    real_part = band(chirp[0], range_block, in_width).T
    imag_part = band(chirp[1], range_block, in_width).T
    upper_rows = jnp.concatenate([real_part, imag_part], 1)
    lower_rows = jnp.concatenate([-imag_part, real_part], 1)
    return jnp.concatenate([upper_rows, lower_rows], 0)


def azimuth_matrix(filter_taps, az_block):
    in_width = az_block + filter_taps.shape[1]
    real_part = band(filter_taps[0], az_block, in_width)
    imag_part = band(filter_taps[1], az_block, in_width)
    upper_rows = jnp.concatenate([real_part, -imag_part], 1)
    lower_rows = jnp.concatenate([imag_part, real_part], 1)
    return jnp.concatenate([upper_rows, lower_rows], 0)


def compress_range(signal, chirp):
    tap_count = chirp.shape[1]
    row_count = signal.shape[1]
    bins = signal.shape[2]
    range_block = min(512, bins)
    in_width = range_block + tap_count
    matrix = range_matrix(chirp, range_block)
    padded = jnp.pad(signal, ((0, 0), (0, 0), (0, tap_count)))

    def one_block(block_index):
        window = lax.dynamic_slice_in_dim(padded, block_index * range_block, in_width, 2)
        stacked = jnp.concatenate([window[0], window[1]], 1)
        return jnp.dot(
            stacked, matrix, precision=lax.Precision.HIGHEST, preferred_element_type=jnp.float32
        )

    block_count = bins // range_block
    blocks = lax.map(one_block, jnp.arange(block_count, dtype=jnp.int32))
    blocks = blocks.reshape(block_count, row_count, 2, range_block).transpose(2, 1, 0, 3)
    return blocks.reshape(2, row_count, bins)


def compress_azimuth(signal, matrix):
    az_block = matrix.shape[0] // 2
    in_width = matrix.shape[1] // 2
    margin = (in_width - az_block) // 2
    pulses = signal.shape[1]
    columns = signal.shape[2]
    padded = jnp.pad(signal, ((0, 0), (margin, margin), (0, 0)))

    def one_block(block_index):
        window = lax.dynamic_slice_in_dim(padded, block_index * az_block, in_width, 1)
        stacked = window.reshape(2 * in_width, columns)
        return jnp.dot(
            matrix, stacked, precision=lax.Precision.HIGHEST, preferred_element_type=jnp.float32
        )

    block_count = pulses // az_block
    blocks = lax.map(one_block, jnp.arange(block_count, dtype=jnp.int32))
    blocks = blocks.reshape(block_count, 2, az_block, columns).transpose(1, 0, 2, 3)
    return blocks.reshape(2, pulses, columns)


def quantities(fore_re, fore_im, aft_re, aft_im):
    return jnp.stack(
        [
            fore_re * aft_re + fore_im * aft_im,
            fore_im * aft_re - fore_re * aft_im,
            fore_re * fore_re + fore_im * fore_im,
            aft_re * aft_re + aft_im * aft_im,
        ]
    )


def coherence_of(window_sums):
    scale = jnp.sqrt(jnp.maximum(window_sums[2], 1.0) * jnp.maximum(window_sums[3], 1.0))
    return jnp.stack([window_sums[0] / scale, window_sums[1] / scale])


def rows_with_margin(summed, channel, rows_quarter, reach):
    padded = jnp.pad(summed, ((0, 0), (reach, reach), (0, 0)))
    return lax.dynamic_slice_in_dim(padded, channel * rows_quarter, rows_quarter + 2 * reach, 1)


def body(echoes, range_chirp, azimuth_filter, pairing, offsets):
    signal = echoes[:, 0]
    pulses_dev = signal.shape[1]
    bins = signal.shape[2]
    wide_count = lax.axis_size("wide")
    chan_count = lax.axis_size("chan")
    shard_bins = bins // wide_count
    pulses = pulses_dev * wide_count
    compressed = compress_range(signal, range_chirp[:, 0])
    parted = compressed.reshape(2, pulses_dev, wide_count, shard_bins)
    az_matrix = azimuth_matrix(azimuth_filter[:, 0], min(512, pulses))
    turned = lax.all_to_all(parted, "wide", split_axis=2, concat_axis=1, tiled=True)
    focused = compress_azimuth(turned[:, :, 0, :], az_matrix)
    channel = lax.axis_index("chan")
    rows_quarter = pulses // chan_count
    reach = 2 * RADIUS
    fore_ids = pairing[: chan_count // 2]
    fore_weight = jnp.sum((fore_ids == channel).astype(jnp.int32)).astype(jnp.float32)
    aft_weight = 1.0 - fore_weight
    pair_terms = jnp.concatenate([focused * fore_weight, focused * aft_weight], 0)
    summed = lax.psum(pair_terms, "chan")
    rows_near = rows_with_margin(summed, channel, rows_quarter, reach)
    extended = extended_2(rows_near, (("wide", 2),), reach)
    products = quantities(extended[0], extended[1], extended[2], extended[3])
    group_count = offsets.shape[0]
    row_ids = channel * rows_quarter + jnp.arange(rows_quarter, dtype=jnp.int32)
    group_of = row_ids // (pulses // group_count)
    in_group = group_of[:, None] == jnp.arange(group_count, dtype=jnp.int32)[None, :]
    row_shift = jnp.sum(jnp.where(in_group, offsets[None, :, 0], 0), 1)
    col_shift = jnp.sum(jnp.where(in_group, offsets[None, :, 1], 0), 1)
    source_rows = jnp.arange(rows_quarter + 2 * reach, dtype=jnp.int32)
    distance = (
        source_rows[None, :]
        - jnp.arange(rows_quarter, dtype=jnp.int32)[:, None]
        - row_shift[:, None]
    )
    window_rows = ((distance >= RADIUS) & (distance <= 3 * RADIUS)).astype(jnp.float32)
    row_sums = jnp.einsum("ij,qjc->qic", window_rows, products, precision=lax.Precision.HIGHEST)
    col_windowed = row_sums[:, :, 0 : shard_bins + reach]
    for step in range(1, reach + 1):
        col_windowed = col_windowed + row_sums[:, :, step : step + shard_bins + reach]
    window_sums = jnp.zeros((4, rows_quarter, shard_bins), jnp.float32)
    for step in range(-RADIUS, RADIUS + 1):
        chosen = (col_shift == step)[None, :, None]
        window_sums = window_sums + jnp.where(
            chosen, col_windowed[:, :, RADIUS + step : RADIUS + step + shard_bins], 0.0
        )
    return coherence_of(window_sums)


def solution(mesh):
    placed = (P(None, "chan", "wide", None), P(None, "chan", None), P(None, "chan", None), P(), P())
    return jax.shard_map(
        body, mesh=mesh, in_specs=placed, out_specs=P(None, "chan", "wide"), check_vma=False
    )
```

profile of v0, /device:TPU:26, one launch (start us, length us, event | category | flops | bytes accessed | tf_op | source)
XLA Modules:
  0.0 341.9 jit_solution(16098929987159809836)
XLA Ops:
  6.5 0.7 fusion.36
  7.2 1.3 pad.16
  8.7 2.3 tile.17
  11.0 1.6 slice-done.1
  12.6 1.5 reshape.94
  14.3 2.3 tile.19
  16.6 3.1 slice.167
  19.7 1.7 reshape.95
  21.4 1.5 bitcast_negate_fusion
  22.9 7.2 %maximum_maximum_fusion.1 = f32[2048,1024]{0,1:T(8,128)} fusion(f32[1024,512]{0,1:T(8,128)} %bitcast.81, f32[1024,512]{0,1:T(8,128)} %bitcast_negate_fusion, f32[1024,512]{0,1:T(8,128)S(1)} %bitcast.80), kind=kLoop, calls=%fused_computation.12 | loop fusion | flops 6291456 | bytes 14680064 | tf_op jit(solution)/shard_map/concatenate | solution.py:37
  30.1 9.4 %copy.27 = f32[2048,1024]{1,0:T(8,128)} copy(f32[2048,1024]{0,1:T(8,128)} %maximum_maximum_fusion.1) | data formatting | bytes 16777216 | tf_op jit(solution)/shard_map/while | solution.py:66
  39.5 122.4 %while.20 = (s32[]{:T(128)}, f32[16,16,1024]{2,1,0:T(8,128)S(1)}, s32[16]{0:T(128)S(1)}, f32[2,16,8704]{2,1,0:T(8,128)S(1)}, f32[2048,1024]{1,0:T(8,128)}, /*ind...) while((s32[]{:T(128)}, f32[16,16,1024]{2,1,0:T(8,128)S(1)}, s32[16]{0:T(128)S(1)}, ...), condition=%wide.region_2.3_spmd, body=%wide.region_1.2_spmd.sunk | while | flops 402685952 | bytes 8847551 | solution.py:66
  40.7 6.4 %fusion.48 = f32[16,16,1024]{2,1,0:T(8,128)S(1)} fusion(f32[16,16,1024]{2,1,0:T(8,128)S(1)} %get-tuple-element.207, s32[]{:T(128)S(6)} %copy.44, f32[2048,1024]{1,0:T(8,128)} %get-tuple-element.220, f32[16,1024]{1,0:T(8,128)S(1)} %get-tuple-element.189, f32[16,1024]{1,0:T(8,128)S(1)} %get-tuple-element.190), kind=kOutput, calls=%fused_computation.1.clone.1 | convolution fusion | flops 402685952 | bytes 8585220 | tf_op jit(solution)/shard_map/while/body/eval_jaxpr/dot_general | solution.py:61
  48.4 6.4 %fusion.48 = f32[16,16,1024]{2,1,0:T(8,128)S(1)} fusion(f32[16,16,1024]{2,1,0:T(8,128)S(1)} %get-tuple-element.207, s32[]{:T(128)S(6)} %copy.44, f32[2048,1024]{1,0:T(8,128)} %get-tuple-element.220, f32[16,1024]{1,0:T(8,128)S(1)} %get-tuple-element.189, f32[16,1024]{1,0:T(8,128)S(1)} %get-tuple-element.190), kind=kOutput, calls=%fused_computation.1.clone.1 | convolution fusion | flops 402685952 | bytes 8585220 | tf_op jit(solution)/shard_map/while/body/eval_jaxpr/dot_general | solution.py:61
  56.0 6.4 %fusion.48 = f32[16,16,1024]{2,1,0:T(8,128)S(1)} fusion(f32[16,16,1024]{2,1,0:T(8,128)S(1)} %get-tuple-element.207, s32[]{:T(128)S(6)} %copy.44, f32[2048,1024]{1,0:T(8,128)} %get-tuple-element.220, f32[16,1024]{1,0:T(8,128)S(1)} %get-tuple-element.189, f32[16,1024]{1,0:T(8,128)S(1)} %get-tuple-element.190), kind=kOutput, calls=%fused_computation.1.clone.1 | convolution fusion | flops 402685952 | bytes 8585220 | tf_op jit(solution)/shard_map/while/body/eval_jaxpr/dot_general | solution.py:61
  63.7 6.4 %fusion.48 = f32[16,16,1024]{2,1,0:T(8,128)S(1)} fusion(f32[16,16,1024]{2,1,0:T(8,128)S(1)} %get-tuple-element.207, s32[]{:T(128)S(6)} %copy.44, f32[2048,1024]{1,0:T(8,128)} %get-tuple-element.220, f32[16,1024]{1,0:T(8,128)S(1)} %get-tuple-element.189, f32[16,1024]{1,0:T(8,128)S(1)} %get-tuple-element.190), kind=kOutput, calls=%fused_computation.1.clone.1 | convolution fusion | flops 402685952 | bytes 8585220 | tf_op jit(solution)/shard_map/while/body/eval_jaxpr/dot_general | solution.py:61
  71.3 6.4 %fusion.48 = f32[16,16,1024]{2,1,0:T(8,128)S(1)} fusion(f32[16,16,1024]{2,1,0:T(8,128)S(1)} %get-tuple-element.207, s32[]{:T(128)S(6)} %copy.44, f32[2048,1024]{1,0:T(8,128)} %get-tuple-element.220, f32[16,1024]{1,0:T(8,128)S(1)} %get-tuple-element.189, f32[16,1024]{1,0:T(8,128)S(1)} %get-tuple-element.190), kind=kOutput, calls=%fused_computation.1.clone.1 | convolution fusion | flops 402685952 | bytes 8585220 | tf_op jit(solution)/shard_map/while/body/eval_jaxpr/dot_general | solution.py:61
  77.7 0.6 dynamic_slice.23
  79.0 6.4 %fusion.48 = f32[16,16,1024]{2,1,0:T(8,128)S(1)} fusion(f32[16,16,1024]{2,1,0:T(8,128)S(1)} %get-tuple-element.207, s32[]{:T(128)S(6)} %copy.44, f32[2048,1024]{1,0:T(8,128)} %get-tuple-element.220, f32[16,1024]{1,0:T(8,128)S(1)} %get-tuple-element.189, f32[16,1024]{1,0:T(8,128)S(1)} %get-tuple-element.190), kind=kOutput, calls=%fused_computation.1.clone.1 | convolution fusion | flops 402685952 | bytes 8585220 | tf_op jit(solution)/shard_map/while/body/eval_jaxpr/dot_general | solution.py:61
  86.6 6.4 %fusion.48 = f32[16,16,1024]{2,1,0:T(8,128)S(1)} fusion(f32[16,16,1024]{2,1,0:T(8,128)S(1)} %get-tuple-element.207, s32[]{:T(128)S(6)} %copy.44, f32[2048,1024]{1,0:T(8,128)} %get-tuple-element.220, f32[16,1024]{1,0:T(8,128)S(1)} %get-tuple-element.189, f32[16,1024]{1,0:T(8,128)S(1)} %get-tuple-element.190), kind=kOutput, calls=%fused_computation.1.clone.1 | convolution fusion | flops 402685952 | bytes 8585220 | tf_op jit(solution)/shard_map/while/body/eval_jaxpr/dot_general | solution.py:61
  94.2 6.4 %fusion.48 = f32[16,16,1024]{2,1,0:T(8,128)S(1)} fusion(f32[16,16,1024]{2,1,0:T(8,128)S(1)} %get-tuple-element.207, s32[]{:T(128)S(6)} %copy.44, f32[2048,1024]{1,0:T(8,128)} %get-tuple-element.220, f32[16,1024]{1,0:T(8,128)S(1)} %get-tuple-element.189, f32[16,1024]{1,0:T(8,128)S(1)} %get-tuple-element.190), kind=kOutput, calls=%fused_computation.1.clone.1 | convolution fusion | flops 402685952 | bytes 8585220 | tf_op jit(solution)/shard_map/while/body/eval_jaxpr/dot_general | solution.py:61
  101.9 6.4 %fusion.48 = f32[16,16,1024]{2,1,0:T(8,128)S(1)} fusion(f32[16,16,1024]{2,1,0:T(8,128)S(1)} %get-tuple-element.207, s32[]{:T(128)S(6)} %copy.44, f32[2048,1024]{1,0:T(8,128)} %get-tuple-element.220, f32[16,1024]{1,0:T(8,128)S(1)} %get-tuple-element.189, f32[16,1024]{1,0:T(8,128)S(1)} %get-tuple-element.190), kind=kOutput, calls=%fused_computation.1.clone.1 | convolution fusion | flops 402685952 | bytes 8585220 | tf_op jit(solution)/shard_map/while/body/eval_jaxpr/dot_general | solution.py:61
  109.5 6.4 %fusion.48 = f32[16,16,1024]{2,1,0:T(8,128)S(1)} fusion(f32[16,16,1024]{2,1,0:T(8,128)S(1)} %get-tuple-element.207, s32[]{:T(128)S(6)} %copy.44, f32[2048,1024]{1,0:T(8,128)} %get-tuple-element.220, f32[16,1024]{1,0:T(8,128)S(1)} %get-tuple-element.189, f32[16,1024]{1,0:T(8,128)S(1)} %get-tuple-element.190), kind=kOutput, calls=%fused_computation.1.clone.1 | convolution fusion | flops 402685952 | bytes 8585220 | tf_op jit(solution)/shard_map/while/body/eval_jaxpr/dot_general | solution.py:61
  115.9 0.6 dynamic_slice.23
  117.2 6.4 %fusion.48 = f32[16,16,1024]{2,1,0:T(8,128)S(1)} fusion(f32[16,16,1024]{2,1,0:T(8,128)S(1)} %get-tuple-element.207, s32[]{:T(128)S(6)} %copy.44, f32[2048,1024]{1,0:T(8,128)} %get-tuple-element.220, f32[16,1024]{1,0:T(8,128)S(1)} %get-tuple-element.189, f32[16,1024]{1,0:T(8,128)S(1)} %get-tuple-element.190), kind=kOutput, calls=%fused_computation.1.clone.1 | convolution fusion | flops 402685952 | bytes 8585220 | tf_op jit(solution)/shard_map/while/body/eval_jaxpr/dot_general | solution.py:61
  124.8 6.4 %fusion.48 = f32[16,16,1024]{2,1,0:T(8,128)S(1)} fusion(f32[16,16,1024]{2,1,0:T(8,128)S(1)} %get-tuple-element.207, s32[]{:T(128)S(6)} %copy.44, f32[2048,1024]{1,0:T(8,128)} %get-tuple-element.220, f32[16,1024]{1,0:T(8,128)S(1)} %get-tuple-element.189, f32[16,1024]{1,0:T(8,128)S(1)} %get-tuple-element.190), kind=kOutput, calls=%fused_computation.1.clone.1 | convolution fusion | flops 402685952 | bytes 8585220 | tf_op jit(solution)/shard_map/while/body/eval_jaxpr/dot_general | solution.py:61
  131.2 0.6 dynamic_slice.23
  132.5 6.4 %fusion.48 = f32[16,16,1024]{2,1,0:T(8,128)S(1)} fusion(f32[16,16,1024]{2,1,0:T(8,128)S(1)} %get-tuple-element.207, s32[]{:T(128)S(6)} %copy.44, f32[2048,1024]{1,0:T(8,128)} %get-tuple-element.220, f32[16,1024]{1,0:T(8,128)S(1)} %get-tuple-element.189, f32[16,1024]{1,0:T(8,128)S(1)} %get-tuple-element.190), kind=kOutput, calls=%fused_computation.1.clone.1 | convolution fusion | flops 402685952 | bytes 8585220 | tf_op jit(solution)/shard_map/while/body/eval_jaxpr/dot_general | solution.py:61
  140.1 6.4 %fusion.48 = f32[16,16,1024]{2,1,0:T(8,128)S(1)} fusion(f32[16,16,1024]{2,1,0:T(8,128)S(1)} %get-tuple-element.207, s32[]{:T(128)S(6)} %copy.44, f32[2048,1024]{1,0:T(8,128)} %get-tuple-element.220, f32[16,1024]{1,0:T(8,128)S(1)} %get-tuple-element.189, f32[16,1024]{1,0:T(8,128)S(1)} %get-tuple-element.190), kind=kOutput, calls=%fused_computation.1.clone.1 | convolution fusion | flops 402685952 | bytes 8585220 | tf_op jit(solution)/shard_map/while/body/eval_jaxpr/dot_general | solution.py:61
  147.8 6.4 %fusion.48 = f32[16,16,1024]{2,1,0:T(8,128)S(1)} fusion(f32[16,16,1024]{2,1,0:T(8,128)S(1)} %get-tuple-element.207, s32[]{:T(128)S(6)} %copy.44, f32[2048,1024]{1,0:T(8,128)} %get-tuple-element.220, f32[16,1024]{1,0:T(8,128)S(1)} %get-tuple-element.189, f32[16,1024]{1,0:T(8,128)S(1)} %get-tuple-element.190), kind=kOutput, calls=%fused_computation.1.clone.1 | convolution fusion | flops 402685952 | bytes 8585220 | tf_op jit(solution)/shard_map/while/body/eval_jaxpr/dot_general | solution.py:61
  155.4 6.4 %fusion.48 = f32[16,16,1024]{2,1,0:T(8,128)S(1)} fusion(f32[16,16,1024]{2,1,0:T(8,128)S(1)} %get-tuple-element.207, s32[]{:T(128)S(6)} %copy.44, f32[2048,1024]{1,0:T(8,128)} %get-tuple-element.220, f32[16,1024]{1,0:T(8,128)S(1)} %get-tuple-element.189, f32[16,1024]{1,0:T(8,128)S(1)} %get-tuple-element.190), kind=kOutput, calls=%fused_computation.1.clone.1 | convolution fusion | flops 402685952 | bytes 8585220 | tf_op jit(solution)/shard_map/while/body/eval_jaxpr/dot_general | solution.py:61
  161.8 0.9 reshape.96
  162.7 0.6 copy.39
  163.4 1.6 copy.29
  165.0 13.0 %all-to-all-start = ((f32[2,16,64,128]{3,1,0,2:T(8,128)}), f32[2,16,64,128]{3,1,0,2:T(8,128)}, u32[]{:S(2)}, u32[]{:S(2)}) async-start(f32[2,16,64,128]{3,1,0,2:T(8,128)} %copy.29), calls=%async_computation | async-start | bytes 2097152 | tf_op jit(solution)/shard_map/all_to_all | solution.py:124
  178.5 3.9 %tile.41 = f32[786944]{0:T(1024)} reshape(f32[512,1537]{1,0:T(8,128)S(1)} %tile.40) | data formatting | bytes 6295552 | tf_op jit(solution)/shard_map/tile | solution.py:27
  182.4 1.9 slice-done
  184.3 1.9 reshape.97
  186.4 3.9 %tile.43 = f32[786944]{0:T(1024)} reshape(f32[512,1537]{1,0:T(8,128)S(1)} %tile.42) | data formatting | bytes 6295552 | tf_op jit(solution)/shard_map/tile | solution.py:27
  190.2 3.8 %slice.169 = f32[786432]{0:T(1024)} slice(f32[786944]{0:T(1024)} %tile.43), slice={[0:786432]} | slice | bytes 6291456 | tf_op jit(solution)/shard_map/slice | solution.py:27
  194.0 2.8 reshape.98
  196.8 1.9 neg.7
  198.8 0.6 fusion.31
  199.9 11.9 %maximum_maximum_fusion = f32[1024,3072]{1,0:T(8,128)} fusion(f32[512,1536]{1,0:T(8,128)} %reshape.97, f32[512,1536]{1,0:T(8,128)S(1)} %reshape.98, f32[512,1536]{1,0:T(8,128)} %neg.7), kind=kLoop, calls=%fused_computation.11 | loop fusion | flops 9437184 | bytes 22020096 | tf_op jit(solution)/shard_map/concatenate | solution.py:46
  211.8 1.4 copy.30
  213.4 36.1 %while.21 = (s32[]{:T(128)}, f32[2,1024,128]{1,2,0:T(8,128)S(1)}, s32[2]{0:T(128)S(1)}, f32[2,2048,128]{2,1,0:T(8,128)S(1)}, f32[1024,3072]{1,0:T(8,128)}, /*index=5*/s32[]{:T(128)}, s32[1]{0:T(128)}, s32[]{:T(128)}, s32[]{:T(128)}) while((s32[]{:T(128)}, f32[2,1024,128]{1,2,0:T(8,128)S(1)}, s32[2]{0:T(128)S(1)}, ...), condition=%wide.region_4.5_spmd, body=%wide.region_3.4_spmd.sunk | while | flops 4831838208 | bytes 17825960 | solution.py:87
  213.4 0.7 dynamic_slice.25
  214.9 16.4 %fusion.51 = f32[2,1024,128]{1,2,0:T(8,128)S(1)} fusion(f32[2,1024,128]{1,2,0:T(8,128)S(1)} %get-tuple-element.236, s32[]{:T(128)S(6)} %copy.50, f32[3072,128]{1,0:T(8,128)S(1)} %bitcast.79, f32[1024,3072]{1,0:T(8,128)} %get-tuple-element.248), kind=kOutput, calls=%fused_computation.9.clone.1 | convolution fusion | flops 4831838208 | bytes 14680068 | tf_op jit(solution)/shard_map/while/body/eval_jaxpr/dot_general | solution.py:82
  231.3 0.7 dynamic_slice.25
  232.8 16.4 %fusion.51 = f32[2,1024,128]{1,2,0:T(8,128)S(1)} fusion(f32[2,1024,128]{1,2,0:T(8,128)S(1)} %get-tuple-element.236, s32[]{:T(128)S(6)} %copy.50, f32[3072,128]{1,0:T(8,128)S(1)} %bitcast.79, f32[1024,3072]{1,0:T(8,128)} %get-tuple-element.248), kind=kOutput, calls=%fused_computation.9.clone.1 | convolution fusion | flops 4831838208 | bytes 14680068 | tf_op jit(solution)/shard_map/while/body/eval_jaxpr/dot_general | solution.py:82
  249.7 0.9 mul.91
  250.6 0.8 copy.37
  251.5 0.9 mul.93
  252.4 0.9 mul.86
  253.3 0.8 copy.38
  254.1 0.9 mul.88
  255.0 1.5 pad_maximum_fusion
  256.6 63.9 %all-reduce.9.cloned.1.call-done = f32[4,1024,128]{1,2,0:T(8,128)} async-done(((f32[4,1024,128]{1,2,0:T(8,128)}), f32[4,1024,128]{1,2,0:T(8,128)}) %all-reduce.9.cloned.1.call-update) | async-done | bytes 2097168 | tf_op jit(solution)/shard_map/psum | solution.py:133
  320.6 1.1 pad_dynamic-slice_fusion.1
  321.7 3.4 collective-permute-start.1
  325.1 5.5 %collective-permute-start = (f32[4,272,8]{1,2,0:T(8,128)S(1)}, f32[4,272,8]{1,2,0:T(8,128)S(1)}, u32[]{:S(2)}, u32[]{:S(2)}) collective-permute-start(f32[4,272,8]{1,2,0:T(8,128)S(1)} %get-tuple-element.105), channel_id=1, source_target_pairs={{0,1},{1,2},{2,3},{3,4},{4,5},{5,6},{6,7},{7,8},{8,9},{9,10},{10,1... | collective-permute-start | bytes 104456 | tf_op jit(solution)/shard_map/ppermute | solution.py:16
  330.9 1.4 collective-permute-done
  332.5 0.7 convolution_bitcast_fusion.2
  334.2 0.8 copy.33
  (76 shorter events, 11.3 us)
Async XLA Ops:
  11.0 1.6 slice-start.1
  30.1 9.4 %copy-start.2 = (f32[16,16,1024]{2,1,0:T(8,128)S(1)}, f32[16,16,1024]{2,1,0:T(8,128)}, u32[]{:S(2)}) copy-start(f32[16,16,1024]{2,1,0:T(8,128)} %custom-call) | copy-start | bytes 3145732
  163.3 14.9 %copy-start.3 = (f32[2,1,1024]{2,1,0:T(1,128)S(1)}, f32[2,1,1024]{2,1,0:T(1,128)}, u32[]{:S(2)}) copy-start(f32[2,1,1024]{2,1,0:T(1,128)} %param.11) | copy-start | bytes 24580
  165.0 46.8 %all-to-all-start = ((f32[2,16,64,128]{3,1,0,2:T(8,128)}), f32[2,16,64,128]{3,1,0,2:T(8,128)}, u32[]{:S(2)}, u32[]{:S(2)}) async-start(f32[2,16,64,128]{3,1,0,2:T(8,128)} %copy.29), calls=%async_computation | async-start | bytes 2097152 | tf_op jit(solution)/shard_map/all_to_all | solution.py:124
  178.0 142.6 %all-reduce.9.cloned.1.call-start = ((), (), s32[]{:S(2)}) async-start(), calls=%async_computation.1 | async-start | bytes 4194304 | tf_op jit(solution)/shard_map/psum | solution.py:133
  182.4 1.9 slice-start
  196.8 1.9 copy-start.5
  211.8 1.5 copy-start.1
  255.0 1.5 copy-start.4
  320.6 10.0 %copy-start = (f32[4,1024,128]{1,2,0:T(8,128)S(1)}, f32[4,1024,128]{1,2,0:T(8,128)}, u32[]{:S(2)}) copy-start(f32[4,1024,128]{1,2,0:T(8,128)} %all-reduce.9.cloned.1.call-done) | copy-start | bytes 6291460
  321.7 9.2 %collective-permute-start.1 = (f32[4,272,8]{1,2,0:T(8,128)S(1)}, f32[4,272,8]{1,2,0:T(8,128)S(1)}, u32[]{:S(2)}, u32[]{:S(2)}) collective-permute-start(f32[4,272,8]{1,2,0:T(8,128)S(1)} %get-tuple-element.106), channel_id=1, source_target_pairs={{1,0},{2,1},{3,2},{4,3},{5,4},{6,5},{7,6},{8,7},{9,8},{10,9},{11,1... | collective-permute-start | bytes 104456 | tf_op jit(solution)/shard_map/ppermute | solution.py:17
  325.1 7.2 %collective-permute-start = (f32[4,272,8]{1,2,0:T(8,128)S(1)}, f32[4,272,8]{1,2,0:T(8,128)S(1)}, u32[]{:S(2)}, u32[]{:S(2)}) collective-permute-start(f32[4,272,8]{1,2,0:T(8,128)S(1)} %get-tuple-element.105), channel_id=1, source_target_pairs={{0,1},{1,2},{2,3},{3,4},{4,5},{5,6},{6,7},{7,8},{8,9},{9,10},{10,1... | collective-permute-start | bytes 104456 | tf_op jit(solution)/shard_map/ppermute | solution.py:16
Sparse Core Ops, SparseCore 0:
  256.6 63.9 all-reduce.8
where the time goes:
time: 347 us; the launch traced here: 342 us
  matrix products  136 us (39%)
  local copies, waits for them, and re-layouts  66.2 us (19%)
  waiting for transfers between devices  65.4 us (19%)
  other arithmetic  26.1 us (8%)
  starting transfers between devices  22 us (6%)
  between operations  14.3 us (4%)
  loops' own time  11.9 us (3%)
    dot_general x16, matrix products, one_block(): jnp.dot(stacked, matrix, precision=lax.Precision.HIGHEST, preferred_eleme...  102 us
    psum x1, waiting for transfers between devices, body(): summed = lax.psum(pair_terms, 'chan')  63.9 us
    dot_general x2, matrix products, one_block(): jnp.dot(matrix, stacked, precision=lax.Precision.HIGHEST, preferred_eleme...  32.8 us
    another operation x8, local copies, waits for them, and re-layouts, band(): tiled = jnp.tile(padded_line, out_count)[:out_count * in_width]  13.1 us
    all_to_all x1, starting transfers between devices, body(): lax.all_to_all(parted, 'wide', split_axis=2, concat_axis=1, tiled=True)  13 us
    concatenate x1, other arithmetic, azimuth_matrix(): return jnp.concatenate([upper_rows, lower_rows], 0)  11.9 us
    slice x6, local copies, waits for them, and re-layouts, band(): tiled = jnp.tile(padded_line, out_count)[:out_count * in_width]  10.3 us
    another operation x1, loops' own time, compress_range(): blocks = lax.map(one_block, jnp.arange(block_count, dtype=jnp.int32))  10.2 us
  transfers between devices with their start and end apart: 4, of which 2 were waited for; matrix products, arithmetic and copies ran while one was open for 9% of the time, Pallas kernels for 0%

commit v1 on v0

v1 whole, which is shorter than its diff:
```python
import jax
import jax.numpy as jnp
from jax import lax
from jax.experimental import pallas as pl
from jax.experimental.pallas import tpu as pltpu
from jax.sharding import PartitionSpec as P

RADIUS = 4
REACH = 2 * RADIUS
F32 = jnp.float32
BF16 = jnp.bfloat16
VMEM_LIMIT = 48 * 1024 * 1024


def split(x):
    hi = x.astype(BF16)
    return hi, (x - hi.astype(F32)).astype(BF16)


def dot_nn(a, b):
    return lax.dot_general(a, b, (((1,), (0,)), ((), ())), preferred_element_type=F32)


def dot_nt(a, b):
    return lax.dot_general(a, b, (((1,), (1,)), ((), ())), preferred_element_type=F32)


def toeplitz(taps, rows, width):
    line = jnp.concatenate([taps, jnp.zeros((1, width - taps.shape[1]), F32)], 1)
    return pltpu.roll(jnp.broadcast_to(line, (rows, width)), 0, 1, stride=1, stride_axis=0)


def range_kernel(echo_ref, chirp_ref, out_ref, e_hi, e_lo, w_hi, w_lo):
    real = split(toeplitz(chirp_ref[0], 128, 640))
    imag = split(toeplitz(chirp_ref[1], 128, 640))
    for w_ref, re, im in ((w_hi, real[0], imag[0]), (w_lo, real[1], imag[1])):
        for j in range(5):
            cols = slice(128 * j, 128 * j + 128)
            w_ref[0:128, 256 * j:256 * j + 128] = re[:, cols]
            w_ref[0:128, 256 * j + 128:256 * j + 256] = -im[:, cols]
            w_ref[128:256, 256 * j:256 * j + 128] = im[:, cols]
            w_ref[128:256, 256 * j + 128:256 * j + 256] = re[:, cols]
    for n in range(64):
        for part in range(2):
            hi, lo = split(echo_ref[part, :, 128 * n:128 * n + 128])
            e_hi[16 * n:16 * n + 16, 128 * part:128 * part + 128] = hi
            e_lo[16 * n:16 * n + 16, 128 * part:128 * part + 128] = lo
    e_hi[1024:1088, :] = jnp.zeros((64, 256), BF16)
    e_lo[1024:1088, :] = jnp.zeros((64, 256), BF16)

    @pl.loop(0, 4)
    def _(m):
        starts = [pl.multiple_of(256 * m + 16 * j, 16) for j in range(5)]
        hi = jnp.concatenate([e_hi[pl.ds(s, 256), :] for s in starts], 1)
        lo = jnp.concatenate([e_lo[pl.ds(s, 256), :] for s in starts], 1)
        acc = dot_nt(hi, w_hi[...]) + dot_nt(hi, w_lo[...]) + dot_nt(lo, w_hi[...])
        out_ref[pl.ds(16 * m, 16), 0:16, :] = acc[:, 0:128].reshape(16, 16, 128)
        out_ref[pl.ds(16 * m, 16), 16:32, :] = acc[:, 128:256].reshape(16, 16, 128)


def taps_kernel(taps_ref, hi_ref, lo_ref):
    for part in range(2):
        hi, lo = split(toeplitz(taps_ref[part], 256, 1280))
        hi_ref[256 * part:256 * part + 256, :] = hi
        lo_ref[256 * part:256 * part + 256, :] = lo


def azimuth_kernel(x_ref, t_hi, t_lo, o0, o1, o2, o3, x_hi, x_lo, y_ref):
    for part in range(2):
        hi, lo = split(x_ref[:, 16 * part:16 * part + 16, :].reshape(1024, 128))
        x_hi[:, 128 * part:128 * part + 128] = hi
        x_lo[:, 128 * part:128 * part + 128] = lo
    for part in range(2):
        y_ref[part, 0:8, :] = jnp.zeros((8, 128), F32)
        y_ref[part, 1032:1040, :] = jnp.zeros((8, 128), F32)
    for q in range(4):
        first, last = max(q - 2, 0), min(q + 2, 3)
        taps = slice(256 * (first - q + 2), 256 * (last - q + 3))
        rows = slice(256 * first, 256 * last + 256)
        g = (
            dot_nn(t_hi[:, taps], x_hi[rows, :])
            + dot_nn(t_hi[:, taps], x_lo[rows, :])
            + dot_nn(t_lo[:, taps], x_hi[rows, :])
        )
        y_ref[0, 8 + 256 * q:264 + 256 * q, :] = g[0:256, 0:128] - g[256:512, 128:256]
        y_ref[1, 8 + 256 * q:264 + 256 * q, :] = g[0:256, 128:256] + g[256:512, 0:128]
    me = lax.axis_index("chan")
    for k, o_ref in enumerate((o0, o1, o2, o3)):
        start = pl.multiple_of(lax.rem(me + k, 4) * 256, 8)
        o_ref[...] = y_ref[:, pl.ds(start, 272), :]


def sum_kernel(pairing_ref, y0, y1, y2, y3, sums_ref, first_ref, last_ref):
    me = lax.axis_index("chan")
    first_ref[...] = jnp.zeros((32, 384), F32)
    last_ref[...] = jnp.zeros((32, 384), F32)
    member = []
    for k in range(4):
        channel = lax.rem(me + 4 - k, 4)
        member.append((pairing_ref[0] == channel) | (pairing_ref[1] == channel))
    for part in range(2):
        fore = jnp.zeros((272, 128), F32)
        aft = jnp.zeros((272, 128), F32)
        for k, y_ref in enumerate((y0, y1, y2, y3)):
            y = y_ref[part]
            fore = fore + jnp.where(member[k], y, 0.0)
            aft = aft + jnp.where(member[k], 0.0, y)
        for plane, value in ((part, fore), (2 + part, aft)):
            sums_ref[plane] = value
            turned = jnp.concatenate([value, jnp.zeros((112, 128), F32)], 0).T
            first_ref[8 * plane:8 * plane + 8, :] = turned[0:8]
            last_ref[8 * plane:8 * plane + 8, :] = turned[120:128]


def window_kernel(offsets_ref, sums_ref, before_ref, after_ref, out_ref, p_hi, p_lo):
    me = lax.axis_index("chan")
    halo = jnp.concatenate([before_ref[...], after_ref[...], jnp.zeros((64, 384), F32)], 0).T[0:272]
    main = [sums_ref[i] for i in range(4)]
    edge = [
        jnp.concatenate([halo[:, 8 * i:8 * i + 8], halo[:, 32 + 8 * i:40 + 8 * i], jnp.zeros((272, 112), F32)], 1)
        for i in range(4)
    ]
    for col, (fr, fi, ar, ai) in ((0, main), (128, edge)):
        planes = (fr * ar + fi * ai, fi * ar - fr * ai, fr * fr + fi * fi, ar * ar + ai * ai)
        for q, value in enumerate(planes):
            hi, lo = split(value)
            p_hi[0:272, 256 * q + col:256 * q + col + 128] = hi
            p_lo[0:272, 256 * q + col:256 * q + col + 128] = lo
    p_hi[272:384, :] = jnp.zeros((112, 1024), BF16)
    p_lo[272:384, :] = jnp.zeros((112, 1024), BF16)
    for g in range(2):
        oa = offsets_ref[2 * me + g, 0]
        orr = offsets_ref[2 * me + g, 1]
        row = lax.broadcasted_iota(jnp.int32, (128, 256), 0)
        src = lax.broadcasted_iota(jnp.int32, (128, 256), 1)
        rows = jnp.where(jnp.abs(src - REACH - row - oa) <= RADIUS, 1.0, 0.0).astype(BF16)
        sums = dot_nn(rows, p_hi[128 * g:128 * g + 256, :]) + dot_nn(rows, p_lo[128 * g:128 * g + 256, :])
        lane = lax.broadcasted_iota(jnp.int32, (256, 128), 0)
        bin_out = lax.broadcasted_iota(jnp.int32, (256, 128), 1)
        at = jnp.where(lane < 128, lane, jnp.where(lane < 136, lane - 136, jnp.where(lane < 144, lane - 8, 4096)))
        cols = jnp.where(jnp.abs(at - bin_out - orr) <= RADIUS, 1.0, 0.0).astype(BF16)
        stacked = jnp.concatenate([sums[:, 256 * q:256 * q + 256] for q in range(4)], 0)
        hi, lo = split(stacked)
        window = dot_nn(hi, cols) + dot_nn(lo, cols)
        scale = jnp.sqrt(jnp.maximum(window[256:384], 1.0) * jnp.maximum(window[384:512], 1.0))
        out_ref[0, 128 * g:128 * g + 128, :] = window[0:128] / scale
        out_ref[1, 128 * g:128 * g + 128, :] = window[128:256] / scale


def call(kernel, name, out_shape, scratch, n_in, smem=(), flops=0, moved=0):
    specs = [pl.BlockSpec(memory_space=pltpu.SMEM if i in smem else pltpu.VMEM) for i in range(n_in)]
    return pl.pallas_call(
        kernel,
        out_shape=out_shape,
        in_specs=specs,
        out_specs=jax.tree.map(lambda _: pl.BlockSpec(memory_space=pltpu.VMEM), out_shape),
        scratch_shapes=scratch,
        compiler_params=pltpu.CompilerParams(vmem_limit_bytes=VMEM_LIMIT),
        cost_estimate=pl.CostEstimate(flops=flops, bytes_accessed=moved, transcendentals=0),
        name=name,
    )


def shape(*dims, dtype=F32):
    return jax.ShapeDtypeStruct(dims, dtype)


def body(echoes, range_chirp, azimuth_filter, pairing, offsets):
    signal = echoes[:, 0]
    chirp = range_chirp.reshape(2, 1, 512)
    taps = azimuth_filter.reshape(2, 1, 1024)
    parted = call(
        range_kernel, "range_filter", shape(64, 32, 128),
        [pltpu.VMEM((1088, 256), BF16)] * 2 + [pltpu.VMEM((256, 1280), BF16)] * 2,
        2, flops=2_000_000_000, moved=2 << 20,
    )(signal, chirp)
    t_hi, t_lo = call(
        taps_kernel, "azimuth_taps", (shape(512, 1280, dtype=BF16), shape(512, 1280, dtype=BF16)), [],
        1, flops=1_000_000_000, moved=8 << 20,
    )(taps)
    turned = lax.all_to_all(parted, "wide", split_axis=0, concat_axis=0, tiled=True)
    pieces = call(
        azimuth_kernel, "azimuth_filter", (shape(2, 272, 128),) * 4,
        [pltpu.VMEM((1024, 256), BF16)] * 2 + [pltpu.VMEM((2, 1040, 128), F32)],
        3, flops=3_000_000_000, moved=4 << 20,
    )(turned, t_hi, t_lo)
    got = [pieces[0]]
    for k in range(1, 4):
        got.append(lax.ppermute(pieces[k], "chan", [(i, (i + k) % 4) for i in range(4)]))
    sums, first, last = call(
        sum_kernel, "fore_aft", (shape(4, 272, 128), shape(32, 384), shape(32, 384)), [],
        5, smem=(0,), flops=1_000_000, moved=2 << 20,
    )(pairing, *got)
    up = [(i, i + 1) for i in range(63)]
    before = lax.ppermute(last, "wide", up)
    after = lax.ppermute(first, "wide", [(j, i) for i, j in up])
    return call(
        window_kernel, "coherence", shape(2, 256, 128),
        [pltpu.VMEM((384, 1024), BF16)] * 2,
        4, smem=(0,), flops=1_000_000_000, moved=1 << 20,
    )(offsets, sums, before, after)


def solution(mesh):
    placed = (P(None, "chan", "wide", None), P(None, "chan", None), P(None, "chan", None), P(), P())
    return jax.shard_map(
        body, mesh=mesh, in_specs=placed, out_specs=P(None, "chan", "wide"), check_vma=False
    )
```

time: 347 us -> 84.7 us (0.24); the launches traced: 342 us -> 84.2 us
  matrix products: 136 us -> 0 us
  local copies, waits for them, and re-layouts: 66.2 us -> 4.38 us
  other arithmetic: 26.1 us -> 0 us
  waiting for transfers between devices: 65.4 us -> 43.3 us
  between operations: 14.3 us -> 0.09 us
  loops' own time: 11.9 us -> 0 us
  Pallas kernels: 0 us -> 11.6 us
    dot_general x19 -> x0, matrix products: 136 us -> none  [the longest x16 102 us: one_block(): jnp.dot(stacked, matrix, precision=lax.Precision.HIGHEST, preferred_eleme...]
    psum x1 -> x0, waiting for transfers between devices: 63.9 us -> none  [body(): summed = lax.psum(pair_terms, 'chan')]
    all_to_all x1, waiting for transfers between devices: 0.01 us -> 26.5 us  [body(): lax.all_to_all(parted, 'wide', split_axis=0, concat_axis=0, tiled=True)]
    concatenate x4 -> x0, other arithmetic: 20.6 us -> none  [the longest x1 11.9 us: azimuth_matrix(): return jnp.concatenate([upper_rows, lower_rows], 0)]
    another operation x11 -> x0, local copies, waits for them, and re-layouts: 15.6 us -> none  [the longest x8 13.1 us: band(): tiled = jnp.tile(padded_line, out_count)[:out_count * in_width]]
    ppermute x2 -> x5, waiting for transfers between devices: 1.43 us -> 16.8 us  [the longest x3 9.47 us: body(): lax.ppermute(pieces[k], 'chan', [(i, (i + k) % 4) for i in range(4)])]
    slice x9 -> x0, local copies, waits for them, and re-layouts: 12.1 us -> none  [the longest x6 10.3 us: band(): tiled = jnp.tile(padded_line, out_count)[:out_count * in_width]]
    another operation x2 -> x0, loops' own time: 11.9 us -> none  [the longest x1 10.2 us: compress_range(): blocks = lax.map(one_block, jnp.arange(block_count, dtype=jnp.int32))]
  transfers between devices with their start and end apart: 4 -> 6, of which waited for: 2 -> 5; matrix products, arithmetic and copies ran while one was open for 9% -> 0% of each run, Pallas kernels for 0% -> 0%
where the time goes in v1:
time: 84.7 us; the launch traced here: 84.2 us
  waiting for transfers between devices  43.3 us (51%)
  starting transfers between devices  24.8 us (29%)
  Pallas kernels  11.6 us (14%)
  local copies, waits for them, and re-layouts  4.38 us (5%)
    all_to_all x1, waiting for transfers between devices, body(): lax.all_to_all(parted, 'wide', split_axis=0, concat_axis=0, tiled=True)  26.5 us
    all_to_all x1, starting transfers between devices, body(): lax.all_to_all(parted, 'wide', split_axis=0, concat_axis=0, tiled=True)  12.9 us
    ppermute x3, waiting for transfers between devices, body(): lax.ppermute(pieces[k], 'chan', [(i, (i + k) % 4) for i in range(4)])  9.47 us
    ppermute x1, waiting for transfers between devices, body(): after = lax.ppermute(first, 'wide', [(j, i) for i, j in up])  7.33 us
    ppermute x3, starting transfers between devices, body(): lax.ppermute(pieces[k], 'chan', [(i, (i + k) % 4) for i in range(4)])  5.17 us
    ppermute x1, starting transfers between devices, body(): before = lax.ppermute(last, 'wide', up)  4.81 us
    unnamed x15, local copies, waits for them, and re-layouts  4.38 us
    pallas_call x1, Pallas kernels, body(): call(range_kernel, 'range_filter', shape(64, 32, 128), [pltpu.VMEM((1088,...  4.25 us
  transfers between devices with their start and end apart: 6, of which 5 were waited for; matrix products, arithmetic and copies ran while one was open for 0% of the time, Pallas kernels for 0%

profile of v1, /device:TPU:26, one launch (start us, length us, event | category | flops | bytes accessed | tf_op | source)
XLA Modules:
  0.0 84.2 jit_solution(16638057472065152893)
XLA Ops:
  0.0 0.0 copy-start.1
  0.0 1.2 %copy-done.1 = f32[2,1,16,8192]{3,2,1,0:T(8,128)S(1)} copy-done((f32[2,1,16,8192]{3,2,1,0:T(8,128)S(1)}, f32[2,1,16,8192]{3,2,1,0:T(8,128)}, u32[]{:S(2)}) %copy-start.1) | copy-done | bytes 1048600
  1.2 0.0 copy-start.3
  1.2 0.7 copy-done.3
  1.9 4.3 %range_filter.1 = f32[64,32,128]{2,1,0:T(8,128)} custom-call(f32[2,16,8192]{2,1,0:T(8,128)S(1)} %bitcast.1, f32[2,1,512]{2,1,0:T(1,128)S(1)} %copy-done.3), custom_call_target="tpu_custom_call" | custom-call | flops 2000000000 | bytes 2097152 | tf_op jit(solution)/shard_map/range_filter/pallas_call | solution.py:172
  6.2 0.0 copy-start.2
  6.2 12.9 %all-to-all-start = ((f32[64,32,128]{2,1,0:T(8,128)}), f32[64,32,128]{2,1,0:T(8,128)S(1)}, u32[]{:S(2)}, u32[]{:S(2)}) async-start(f32[64,32,128]{2,1,0:T(8,128)} %range_filter.1), calls=%async_computation | async-start | bytes 2097152 | tf_op jit(solution)/shard_map/all_to_all | solution.py:181
  19.1 0.0 copy-done.2
  19.1 0.4 azimuth_taps.1
  19.5 0.0 copy-start.4
  19.5 1.1 %copy-done.4 = bf16[512,1280]{1,0:T(8,128)(2,1)} copy-done((bf16[512,1280]{1,0:T(8,128)(2,1)}, bf16[512,1280]{1,0:T(8,128)(2,1)S(1)}, u32[]{:S(2)}) %copy-start.4) | copy-done | bytes 1310744
  20.5 26.5 %all-to-all-done.x_ref = f32[64,32,128]{2,1,0:T(8,128)S(1)} async-done(((f32[64,32,128]{2,1,0:T(8,128)}), f32[64,32,128]{2,1,0:T(8,128)S(1)}, u32[]{:S(2)}, u32[]{:S(2)}) %all-to-all-start) | async-done | bytes 1048608 | tf_op jit(solution)/shard_map/all_to_all | solution.py:181
  47.0 0.0 copy-start.5
  47.0 1.3 %copy-done.5 = bf16[512,1280]{1,0:T(8,128)(2,1)S(1)} copy-done((bf16[512,1280]{1,0:T(8,128)(2,1)S(1)}, bf16[512,1280]{1,0:T(8,128)(2,1)}, u32[]{:S(2)}) %copy-start.5) | copy-done | bytes 1310744
  48.4 0.0 copy-start
  48.4 0.0 copy-start.6
  48.4 3.3 %azimuth_filter.1 = (f32[2,272,128]{2,1,0:T(8,128)S(1)}, f32[2,272,128]{2,1,0:T(8,128)S(1)}, f32[2,272,128]{2,1,0:T(8,128)S(1)}, f32[2,272,128]{2,1,0:T(8,128)S(1)}) custom-call(f32[64,32,128]{2,1,0:T(8,128)S(1)} %all-to-all-done.x_ref, bf16[512,1280]{1,0:T(8,128)(2,1)S(1)} %get-tuple-element.14.t_hi, bf16[512,1280]{1,0:T(8,128)(2,1)S(1)} %copy-done.5), custom_call_target="tpu_custom_call" | custom-call | flops 3000000000 | bytes 4194304 | tf_op jit(solution)/shard_map/azimuth_filter/pallas_call | solution.py:182
  51.7 0.1 collective-permute-start
  51.8 2.2 %collective-permute-start.1 = (f32[2,272,128]{2,1,0:T(8,128)S(1)}, f32[2,272,128]{2,1,0:T(8,128)S(1)}, u32[]{:S(2)}, u32[]{:S(2)}) collective-permute-start(f32[2,272,128]{2,1,0:T(8,128)S(1)} %get-tuple-element.18), channel_id=1, source_target_pairs={{0,128},{64,192},{128,0},{192,64},{1,129},{65,193},{129,1},{193,65... | collective-permute-start | bytes 835592 | tf_op jit(solution)/shard_map/ppermute | solution.py:189
  54.0 2.9 %collective-permute-start.2 = (f32[2,272,128]{2,1,0:T(8,128)S(1)}, f32[2,272,128]{2,1,0:T(8,128)S(1)}, u32[]{:S(2)}, u32[]{:S(2)}) collective-permute-start(f32[2,272,128]{2,1,0:T(8,128)S(1)} %get-tuple-element.19), channel_id=1, source_target_pairs={{0,192},{64,0},{128,64},{192,128},{1,193},{65,1},{129,65},{193,129... | collective-permute-start | bytes 835592 | tf_op jit(solution)/shard_map/ppermute | solution.py:189
  56.9 4.7 %collective-permute-done.y1 = f32[2,272,128]{2,1,0:T(8,128)S(1)} collective-permute-done((f32[2,272,128]{2,1,0:T(8,128)S(1)}, f32[2,272,128]{2,1,0:T(8,128)S(1)}, u32[]{:S(2)}, u32[]{:S(2)}) %collective-permute-start) | collective-permute-done | bytes 278560 | tf_op jit(solution)/shard_map/ppermute | solution.py:189
  61.6 1.3 %collective-permute-done.1.y2 = f32[2,272,128]{2,1,0:T(8,128)S(1)} collective-permute-done((f32[2,272,128]{2,1,0:T(8,128)S(1)}, f32[2,272,128]{2,1,0:T(8,128)S(1)}, u32[]{:S(2)}, u32[]{:S(2)}) %collective-permute-start.1) | collective-permute-done | bytes 278560 | tf_op jit(solution)/shard_map/ppermute | solution.py:189
  62.8 3.5 %collective-permute-done.2.y3 = f32[2,272,128]{2,1,0:T(8,128)S(1)} collective-permute-done((f32[2,272,128]{2,1,0:T(8,128)S(1)}, f32[2,272,128]{2,1,0:T(8,128)S(1)}, u32[]{:S(2)}, u32[]{:S(2)}) %collective-permute-start.2) | collective-permute-done | bytes 278560 | tf_op jit(solution)/shard_map/ppermute | solution.py:189
  66.3 0.0 copy-done
  66.3 0.9 %fore_aft.1 = (f32[4,272,128]{2,1,0:T(8,128)S(1)}, f32[32,384]{1,0:T(8,128)S(1)}, f32[32,384]{1,0:T(8,128)S(1)}) custom-call(s32[4]{0:T(128)S(1)} %copy-done, f32[2,272,128]{2,1,0:T(8,128)S(1)} %get-tuple-element.16.y0, f32[2,272,128]{2,1,0:T(8,128)S(1)} %collective-permute-done.y1, f32[2,272,128]{2,1,0:T(8,128)S(1)} %collective-permute-done.1.y2, ...), custom_call_target="tpu_custom_call" | custom-call | flops 1000000 | bytes 2097152 | tf_op jit(solution)/shard_map/fore_aft/pallas_call | solution.py:190
  67.2 4.8 %collective-permute-start.3 = (f32[32,384]{1,0:T(8,128)S(1)}, f32[32,384]{1,0:T(8,128)S(1)}, u32[]{:S(2)}, u32[]{:S(2)}) collective-permute-start(f32[32,384]{1,0:T(8,128)S(1)} %get-tuple-element.21), channel_id=1, source_target_pairs={{0,1},{1,2},{2,3},{3,4},{4,5},{5,6},{6,7},{7,8},{8,9},{9,10},{10,1... | collective-permute-start | bytes 147464 | tf_op jit(solution)/shard_map/ppermute | solution.py:195
  72.0 1.9 %collective-permute-start.4 = (f32[32,384]{1,0:T(8,128)S(1)}, f32[32,384]{1,0:T(8,128)S(1)}, u32[]{:S(2)}, u32[]{:S(2)}) collective-permute-start(f32[32,384]{1,0:T(8,128)S(1)} %get-tuple-element.22), channel_id=1, source_target_pairs={{1,0},{2,1},{3,2},{4,3},{5,4},{6,5},{7,6},{8,7},{9,8},{10,9},{11,1... | collective-permute-start | bytes 147464 | tf_op jit(solution)/shard_map/ppermute | solution.py:196
  74.0 0.0 copy-done.6
  74.0 0.1 copy.6.offsets_ref
  74.0 0.0 collective-permute-done.3.before_ref
  74.0 7.3 %collective-permute-done.4.after_ref = f32[32,384]{1,0:T(8,128)S(1)} collective-permute-done((f32[32,384]{1,0:T(8,128)S(1)}, f32[32,384]{1,0:T(8,128)S(1)}, u32[]{:S(2)}, u32[]{:S(2)}) %collective-permute-start.4) | collective-permute-done | bytes 49184 | tf_op jit(solution)/shard_map/ppermute | solution.py:196
  81.4 2.8 %coherence.1 = f32[2,256,128]{2,1,0:T(8,128)} custom-call(s32[8,2]{1,0:T(8,128)S(1)} %copy.6.offsets_ref, f32[4,272,128]{2,1,0:T(8,128)S(1)} %get-tuple-element.20.sums_ref, f32[32,384]{1,0:T(8,128)S(1)} %collective-permute-done.3.before_ref, f32[32,384]{1,0:T(8,128)S(1)} %collective-permute-done.4.after_ref), custom_call_target="tpu_custom_call" | custom-call | flops 1000000000 | bytes 1048576 | tf_op jit(solution)/shard_map/coherence/pallas_call | solution.py:197
Async XLA Ops:
  0.0 1.2 %copy-start.1 = (f32[2,1,16,8192]{3,2,1,0:T(8,128)S(1)}, f32[2,1,16,8192]{3,2,1,0:T(8,128)}, u32[]{:S(2)}) copy-start(f32[2,1,16,8192]{3,2,1,0:T(8,128)} %param.5) | copy-start | bytes 3145732
  1.2 0.7 copy-start.3
  6.2 12.9 %copy-start.2 = (f32[2,1,1024]{2,1,0:T(1,128)S(1)}, f32[2,1,1024]{2,1,0:T(1,128)}, u32[]{:S(2)}) copy-start(f32[2,1,1024]{2,1,0:T(1,128)} %taps_ref.1) | copy-start | bytes 24580
  6.2 40.9 %all-to-all-start = ((f32[64,32,128]{2,1,0:T(8,128)}), f32[64,32,128]{2,1,0:T(8,128)S(1)}, u32[]{:S(2)}, u32[]{:S(2)}) async-start(f32[64,32,128]{2,1,0:T(8,128)} %range_filter.1), calls=%async_computation | async-start | bytes 2097152 | tf_op jit(solution)/shard_map/all_to_all | solution.py:181
  19.5 1.1 %copy-start.4 = (bf16[512,1280]{1,0:T(8,128)(2,1)}, bf16[512,1280]{1,0:T(8,128)(2,1)S(1)}, u32[]{:S(2)}) copy-start(bf16[512,1280]{1,0:T(8,128)(2,1)S(1)} %get-tuple-element.15.t_lo) | copy-start | bytes 3932164
  47.0 1.3 %copy-start.5 = (bf16[512,1280]{1,0:T(8,128)(2,1)S(1)}, bf16[512,1280]{1,0:T(8,128)(2,1)}, u32[]{:S(2)}) copy-start(bf16[512,1280]{1,0:T(8,128)(2,1)} %copy-done.4) | copy-start | bytes 3932164
  48.4 18.0 %copy-start = (s32[4]{0:T(128)S(1)}, s32[4]{0:T(128)}, u32[]{:S(2)}) copy-start(s32[4]{0:T(128)} %pairing_ref.1) | copy-start | bytes 52
  48.4 25.6 %copy-start.6 = (s32[8,2]{0,1:T(2,128)S(1)}, s32[8,2]{0,1:T(2,128)}, u32[]{:S(2)}) copy-start(s32[8,2]{0,1:T(2,128)} %param.9) | copy-start | bytes 196
  51.7 9.9 %collective-permute-start = (f32[2,272,128]{2,1,0:T(8,128)S(1)}, f32[2,272,128]{2,1,0:T(8,128)S(1)}, u32[]{:S(2)}, u32[]{:S(2)}) collective-permute-start(f32[2,272,128]{2,1,0:T(8,128)S(1)} %get-tuple-element.17), channel_id=1, source_target_pairs={{0,64},{64,128},{128,192},{192,0},{1,65},{65,129},{129,193},{193,1... | collective-permute-start | bytes 835592 | tf_op jit(solution)/shard_map/ppermute | solution.py:189
  51.8 11.1 %collective-permute-start.1 = (f32[2,272,128]{2,1,0:T(8,128)S(1)}, f32[2,272,128]{2,1,0:T(8,128)S(1)}, u32[]{:S(2)}, u32[]{:S(2)}) collective-permute-start(f32[2,272,128]{2,1,0:T(8,128)S(1)} %get-tuple-element.18), channel_id=1, source_target_pairs={{0,128},{64,192},{128,0},{192,64},{1,129},{65,193},{129,1},{193,65... | collective-permute-start | bytes 835592 | tf_op jit(solution)/shard_map/ppermute | solution.py:189
  54.0 12.3 %collective-permute-start.2 = (f32[2,272,128]{2,1,0:T(8,128)S(1)}, f32[2,272,128]{2,1,0:T(8,128)S(1)}, u32[]{:S(2)}, u32[]{:S(2)}) collective-permute-start(f32[2,272,128]{2,1,0:T(8,128)S(1)} %get-tuple-element.19), channel_id=1, source_target_pairs={{0,192},{64,0},{128,64},{192,128},{1,193},{65,1},{129,65},{193,129... | collective-permute-start | bytes 835592 | tf_op jit(solution)/shard_map/ppermute | solution.py:189
  67.2 6.8 %collective-permute-start.3 = (f32[32,384]{1,0:T(8,128)S(1)}, f32[32,384]{1,0:T(8,128)S(1)}, u32[]{:S(2)}, u32[]{:S(2)}) collective-permute-start(f32[32,384]{1,0:T(8,128)S(1)} %get-tuple-element.21), channel_id=1, source_target_pairs={{0,1},{1,2},{2,3},{3,4},{4,5},{5,6},{6,7},{7,8},{8,9},{9,10},{10,1... | collective-permute-start | bytes 147464 | tf_op jit(solution)/shard_map/ppermute | solution.py:195
  72.0 9.4 %collective-permute-start.4 = (f32[32,384]{1,0:T(8,128)S(1)}, f32[32,384]{1,0:T(8,128)S(1)}, u32[]{:S(2)}, u32[]{:S(2)}) collective-permute-start(f32[32,384]{1,0:T(8,128)S(1)} %get-tuple-element.22), channel_id=1, source_target_pairs={{1,0},{2,1},{3,2},{4,3},{5,4},{6,5},{7,6},{8,7},{9,8},{10,9},{11,1... | collective-permute-start | bytes 147464 | tf_op jit(solution)/shard_map/ppermute | solution.py:196

commit v2 on v1

v2 whole, which is shorter than its diff:
```python
import jax
import jax.numpy as jnp
from jax import lax
from jax.experimental import pallas as pl
from jax.experimental.pallas import tpu as pltpu
from jax.sharding import PartitionSpec as P

RADIUS = 4
REACH = 2 * RADIUS
F32 = jnp.float32
BF16 = jnp.bfloat16
VMEM_LIMIT = 24 * 1024 * 1024


def split(x):
    hi = x.astype(BF16)
    return hi, (x - hi.astype(F32)).astype(BF16)


def dot_nn(a, b):
    return lax.dot_general(a, b, (((1,), (0,)), ((), ())), preferred_element_type=F32)


def dot_nt(a, b):
    return lax.dot_general(a, b, (((1,), (1,)), ((), ())), preferred_element_type=F32)


def toeplitz(taps, rows, width):
    line = jnp.concatenate([taps, jnp.zeros((1, width - taps.shape[1]), F32)], 1)
    return pltpu.roll(jnp.broadcast_to(line, (rows, width)), 0, 1, stride=1, stride_axis=0)


def range_kernel(echo_hbm, chirp_hbm, out_ref, echo, chirp, e_hi, e_lo, w_hi, w_lo, sems):
    taps_copy = pltpu.make_async_copy(chirp_hbm, chirp, sems.at[4])
    taps_copy.start()
    copies = []
    for m in range(4):
        bins = pl.ds(2048 * m, 2048)
        copies.append(pltpu.make_async_copy(echo_hbm.at[:, :, bins], echo.at[:, :, bins], sems.at[m]))
        copies[m].start()
    e_hi[1024:1088, :] = jnp.zeros((64, 256), BF16)
    e_lo[1024:1088, :] = jnp.zeros((64, 256), BF16)
    taps_copy.wait()
    real = split(toeplitz(chirp[0], 128, 640))
    imag = split(toeplitz(chirp[1], 128, 640))
    for w_ref, re, im in ((w_hi, real[0], imag[0]), (w_lo, real[1], imag[1])):
        for j in range(5):
            cols = slice(128 * j, 128 * j + 128)
            w_ref[0:128, 256 * j:256 * j + 128] = re[:, cols]
            w_ref[0:128, 256 * j + 128:256 * j + 256] = -im[:, cols]
            w_ref[128:256, 256 * j:256 * j + 128] = im[:, cols]
            w_ref[128:256, 256 * j + 128:256 * j + 256] = re[:, cols]

    def fill(m):
        copies[m].wait()
        for n in range(16 * m, 16 * m + 16):
            for part in range(2):
                hi, lo = split(echo[part, :, 128 * n:128 * n + 128])
                e_hi[16 * n:16 * n + 16, 128 * part:128 * part + 128] = hi
                e_lo[16 * n:16 * n + 16, 128 * part:128 * part + 128] = lo

    fill(0)
    early = lax.broadcasted_iota(jnp.int32, (256, 128), 1) < REACH
    last = [jnp.zeros((16, 128), F32)] * 2
    for m in range(4):
        if m < 3:
            fill(m + 1)
        starts = [256 * m + 16 * j for j in range(5)]
        hi = jnp.concatenate([e_hi[s:s + 256, :] for s in starts], 1)
        lo = jnp.concatenate([e_lo[s:s + 256, :] for s in starts], 1)
        acc = dot_nt(hi, w_hi[...]) + dot_nt(hi, w_lo[...]) + dot_nt(lo, w_hi[...])
        for part in range(2):
            turned = pltpu.roll(acc[:, 128 * part:128 * part + 128], REACH, 1)
            before = jnp.concatenate([last[part], turned[0:240]], 0)
            out_ref[16 * m:16 * m + 16, 16 * part:16 * part + 16, :] = jnp.where(early, before, turned).reshape(16, 16, 128)
            last[part] = turned[240:256]
    for part in range(2):
        out_ref[0, 16 * part:16 * part + 16, 0:REACH] = last[part][:, 0:REACH]


def azimuth_kernel(x_ref, taps_ref, o0, o1, o2, o3, t_hi, t_lo, x_hi, x_lo, y_ref):
    for part in range(2):
        hi, lo = split(toeplitz(taps_ref[part], 256, 1280))
        t_hi[256 * part:256 * part + 256, :] = hi
        t_lo[256 * part:256 * part + 256, :] = lo
        hi, lo = split(x_ref[:, 16 * part:16 * part + 16, :].reshape(1024, 128))
        x_hi[:, 128 * part:128 * part + 128] = hi
        x_lo[:, 128 * part:128 * part + 128] = lo
        y_ref[part, 0:8, :] = jnp.zeros((8, 128), F32)
        y_ref[part, 1032:1040, :] = jnp.zeros((8, 128), F32)
    for q in range(4):
        first, last = max(q - 2, 0), min(q + 2, 3)
        taps = slice(256 * (first - q + 2), 256 * (last - q + 3))
        rows = slice(256 * first, 256 * last + 256)
        g = (
            dot_nn(t_hi[:, taps], x_hi[rows, :])
            + dot_nn(t_hi[:, taps], x_lo[rows, :])
            + dot_nn(t_lo[:, taps], x_hi[rows, :])
        )
        y_ref[0, 8 + 256 * q:264 + 256 * q, :] = g[0:256, 0:128] - g[256:512, 128:256]
        y_ref[1, 8 + 256 * q:264 + 256 * q, :] = g[0:256, 128:256] + g[256:512, 0:128]
    me = lax.axis_index("chan")
    for k, o_ref in enumerate((o0, o1, o2, o3)):
        start = pl.multiple_of((me ^ k) * 256, 8)
        o_ref[...] = y_ref[:, pl.ds(start, 272), :]


def sum_kernel(pairing_ref, y0, y1, y2, y3, sums_ref, edge_ref):
    me = lax.axis_index("chan")
    lane = lax.broadcasted_iota(jnp.int32, (272, 128), 1)
    edge = jnp.zeros((272, 128), F32)
    for part in range(2):
        fore = jnp.zeros((272, 128), F32)
        aft = jnp.zeros((272, 128), F32)
        for k, y_ref in enumerate((y0, y1, y2, y3)):
            channel = me ^ k
            member = (pairing_ref[0] == channel) | (pairing_ref[1] == channel)
            fore = fore + jnp.where(member, y_ref[part], 0.0)
            aft = aft + jnp.where(member, 0.0, y_ref[part])
        for plane, value in ((part, fore), (2 + part, aft)):
            sums_ref[plane] = value
            at = 16 * plane
            moved = pltpu.roll(value, at, 1) if at else value
            edge = jnp.where((lane >= at) & (lane < at + 16), moved, edge)
    edge_ref[...] = edge[0:136] + pltpu.roll(edge[136:272], 64, 1)


def quantities(fr, fi, ar, ai):
    return fr * ar + fi * ai, fi * ar - fr * ai, fr * fr + fi * fi, ar * ar + ai * ai


def row_window(oa):
    row = lax.broadcasted_iota(jnp.int32, (128, 256), 0)
    src = lax.broadcasted_iota(jnp.int32, (128, 256), 1)
    return jnp.where(jnp.abs(src - REACH - row - oa) <= RADIUS, 1.0, 0.0).astype(BF16)


def bin_window(orr, shift, wanted):
    lane = lax.broadcasted_iota(jnp.int32, (128, 128), 0)
    bin_out = lax.broadcasted_iota(jnp.int32, (128, 128), 1)
    near = (jnp.abs(lane + shift - bin_out - orr) <= RADIUS) & wanted(lane)
    return jnp.where(near, 1.0, 0.0).astype(BF16)


def main_kernel(offsets_ref, sums_ref, out_ref, p_hi, p_lo):
    me = lax.axis_index("chan")
    first = lax.axis_index("wide") == 0
    for q, value in enumerate(quantities(*[sums_ref[i] for i in range(4)])):
        hi, lo = split(value)
        p_hi[0:272, 128 * q:128 * q + 128] = hi
        p_lo[0:272, 128 * q:128 * q + 128] = lo
    p_hi[272:384, :] = jnp.zeros((112, 512), BF16)
    p_lo[272:384, :] = jnp.zeros((112, 512), BF16)
    for g in range(2):
        rows = row_window(offsets_ref[2 * me + g, 0])
        sums = dot_nn(rows, p_hi[128 * g:128 * g + 256, :]) + dot_nn(rows, p_lo[128 * g:128 * g + 256, :])
        cols = bin_window(offsets_ref[2 * me + g, 1], -REACH, lambda lane: (lane >= REACH) | jnp.logical_not(first))
        hi, lo = split(jnp.concatenate([sums[:, 128 * q:128 * q + 128] for q in range(4)], 0))
        out_ref[g] = dot_nn(hi, cols) + dot_nn(lo, cols)


def coherence_kernel(offsets_ref, main_ref, edge_ref, out_ref, p_hi, p_lo):
    me = lax.axis_index("chan")
    final = lax.axis_index("wide") == lax.axis_size("wide") - 1
    packed = edge_ref[...]
    edge = jnp.concatenate([packed, pltpu.roll(packed, 64, 1)], 0)
    lane = lax.broadcasted_iota(jnp.int32, (272, 128), 1)
    planes = [edge] + [pltpu.roll(edge, 128 - 16 * i, 1) for i in range(1, 4)]
    both = jnp.zeros((272, 128), F32)
    for q, value in enumerate(quantities(*planes)):
        moved = pltpu.roll(value, 16 * q, 1) if q else value
        both = jnp.where((lane >= 16 * q) & (lane < 16 * q + 16), moved, both)
    hi, lo = split(both)
    p_hi[0:272, :] = hi
    p_lo[0:272, :] = lo
    p_hi[272:384, :] = jnp.zeros((112, 128), BF16)
    p_lo[272:384, :] = jnp.zeros((112, 128), BF16)
    for g in range(2):
        rows = row_window(offsets_ref[2 * me + g, 0])
        sums = dot_nn(rows, p_hi[128 * g:128 * g + 256, :]) + dot_nn(rows, p_lo[128 * g:128 * g + 256, :])
        cols = bin_window(
            offsets_ref[2 * me + g, 1], 128 - REACH,
            lambda lane: (lane < REACH) | ((lane < 2 * REACH) & jnp.logical_not(final)),
        )
        hi, lo = split(jnp.concatenate([sums] + [pltpu.roll(sums, 128 - 16 * q, 1) for q in range(1, 4)], 0))
        window = main_ref[g] + dot_nn(hi, cols) + dot_nn(lo, cols)
        scale = jnp.sqrt(jnp.maximum(window[256:384], 1.0) * jnp.maximum(window[384:512], 1.0))
        out_ref[0, 128 * g:128 * g + 128, :] = window[0:128] / scale
        out_ref[1, 128 * g:128 * g + 128, :] = window[128:256] / scale


def call(kernel, name, out_shape, scratch, n_in, smem=(), hbm=(), flops=0, moved=0, vmem=VMEM_LIMIT):
    spaces = [pltpu.SMEM if i in smem else pltpu.HBM if i in hbm else pltpu.VMEM for i in range(n_in)]
    return pl.pallas_call(
        kernel,
        out_shape=out_shape,
        in_specs=[pl.BlockSpec(memory_space=space) for space in spaces],
        out_specs=jax.tree.map(lambda _: pl.BlockSpec(memory_space=pltpu.VMEM), out_shape),
        scratch_shapes=scratch,
        compiler_params=pltpu.CompilerParams(vmem_limit_bytes=vmem),
        cost_estimate=pl.CostEstimate(flops=flops, bytes_accessed=moved, transcendentals=0),
        name=name,
    )


def shape(*dims, dtype=F32):
    return jax.ShapeDtypeStruct(dims, dtype)


def body(echoes, range_chirp, azimuth_filter, pairing, offsets):
    signal = echoes[:, 0]
    chirp = range_chirp.reshape(2, 1, 512)
    taps = azimuth_filter.reshape(2, 1, 1024)
    parted = call(
        range_kernel, "range_filter", shape(64, 32, 128),
        [pltpu.VMEM((2, 16, 8192), F32), pltpu.VMEM((2, 1, 512), F32)]
        + [pltpu.VMEM((1088, 256), BF16)] * 2 + [pltpu.VMEM((256, 1280), BF16)] * 2
        + [pltpu.SemaphoreType.DMA((5,))],
        2, hbm=(0, 1), flops=2_000_000_000, moved=2 << 20, vmem=60 << 20,
    )(signal, chirp)
    turned = lax.all_to_all(parted, "wide", split_axis=0, concat_axis=0, tiled=True)
    pieces = call(
        azimuth_kernel, "azimuth_filter", (shape(2, 272, 128),) * 4,
        [pltpu.VMEM((512, 1280), BF16)] * 2 + [pltpu.VMEM((1024, 256), BF16)] * 2
        + [pltpu.VMEM((2, 1040, 128), F32)],
        2, flops=3_000_000_000, moved=4 << 20,
    )(turned, taps)
    got = [pieces[0]] + [
        lax.ppermute(pieces[k], "chan", [(i, i ^ k) for i in range(4)]) for k in range(1, 4)
    ]
    sums, edge = call(
        sum_kernel, "fore_aft", (shape(4, 272, 128), shape(136, 128)), [],
        5, smem=(0,), flops=1_000_000, moved=2 << 20,
    )(pairing, *got)
    after = lax.ppermute(edge, "wide", [(i, (i - 1) % 64) for i in range(64)])
    main = call(
        main_kernel, "window_sums", shape(2, 512, 128), [pltpu.VMEM((384, 512), BF16)] * 2,
        2, smem=(0,), flops=500_000_000, moved=1 << 20,
    )(offsets, sums)
    return call(
        coherence_kernel, "coherence", shape(2, 256, 128), [pltpu.VMEM((384, 128), BF16)] * 2,
        3, smem=(0,), flops=500_000_000, moved=1 << 20,
    )(offsets, main, after)


def solution(mesh):
    placed = (P(None, "chan", "wide", None), P(None, "chan", None), P(None, "chan", None), P(), P())
    return jax.shard_map(
        body, mesh=mesh, in_specs=placed, out_specs=P(None, "chan", "wide"), check_vma=False
    )
```

time: 84.7 us -> 77 us (0.909)
  blocking collectives: 0 us -> 40.7 us
  waiting for transfers between devices: 43.3 us -> 17.9 us
  starting transfers between devices: 24.8 us -> 4.1 us
  local copies, waits for them, and re-layouts: 4.38 us -> 0.13 us
  Pallas kernels: 11.6 us -> 13.8 us
    all_to_all x0 -> x1, blocking collectives: none -> 40.7 us  [body(): lax.all_to_all(parted, 'wide', split_axis=0, concat_axis=0, tiled=True)]
    all_to_all x1 -> x0, waiting for transfers between devices: 26.5 us -> none  [body(): lax.all_to_all(parted, 'wide', split_axis=0, concat_axis=0, tiled=True)]
    all_to_all x1 -> x0, starting transfers between devices: 12.9 us -> none  [body(): lax.all_to_all(parted, 'wide', split_axis=0, concat_axis=0, tiled=True)]
    ppermute x5 -> x4, starting transfers between devices: 11.9 us -> 4.1 us  [the longest x3 3.46 us: body(): lax.ppermute(pieces[k], 'chan', [(i, i ^ k) for i in range(4)])]
    unnamed x15 -> x7, local copies, waits for them, and re-layouts: 4.38 us -> 0.13 us
    pallas_call x4, Pallas kernels: 8.3 us -> 10.5 us  [the longest x1 5.95 us: body(): call(range_kernel, 'range_filter', shape(64, 32, 128), [pltpu.VMEM((2, 16...]
    ppermute x5 -> x4, waiting for transfers between devices: 16.8 us -> 17.9 us  [the longest x3 12.7 us: body(): lax.ppermute(pieces[k], 'chan', [(i, i ^ k) for i in range(4)])]
  transfers between devices with their start and end apart: 6 -> 4, of which waited for: 5 -> 3; matrix products, arithmetic and copies ran while one was open for 0% -> 0% of each run, Pallas kernels for 0% -> 2%
where the time goes in v2:
time: 77 us; the launch traced here: 76.8 us
  blocking collectives  40.7 us (53%)
  waiting for transfers between devices  17.9 us (23%)
  Pallas kernels  13.8 us (18%)
  starting transfers between devices  4.1 us (5%)
    all_to_all x1, blocking collectives, body(): lax.all_to_all(parted, 'wide', split_axis=0, concat_axis=0, tiled=True)  40.7 us
    ppermute x3, waiting for transfers between devices, body(): lax.ppermute(pieces[k], 'chan', [(i, i ^ k) for i in range(4)])  12.7 us
    pallas_call x1, Pallas kernels, body(): call(range_kernel, 'range_filter', shape(64, 32, 128), [pltpu.VMEM((2, 16...  5.95 us
    ppermute x1, waiting for transfers between devices, body(): after = lax.ppermute(edge, 'wide', [(i, (i - 1) % 64) for i in range(64)])  5.21 us
    ppermute x3, starting transfers between devices, body(): lax.ppermute(pieces[k], 'chan', [(i, i ^ k) for i in range(4)])  3.46 us
    pallas_call x1, Pallas kernels, body(): call(azimuth_kernel, 'azimuth_filter', (shape(2, 272, 128),) * 4, [pltpu....  3.33 us
    pallas_call x1, Pallas kernels, body(): call(coherence_kernel, 'coherence', shape(2, 256, 128), [pltpu.VMEM((384,...  2.26 us
  transfers between devices with their start and end apart: 4, of which 3 were waited for; matrix products, arithmetic and copies ran while one was open for 0% of the time, Pallas kernels for 2%

profile of v2, /device:TPU:26, one launch (start us, length us, event | category | flops | bytes accessed | tf_op | source)
XLA Modules:
  0.0 76.8 jit_solution(16575641453856135080)
XLA Ops:
  0.0 5.9 %range_filter.1 = f32[64,32,128]{2,1,0:T(8,128)} custom-call(f32[2,16,8192]{2,1,0:T(8,128)} %bitcast.1, f32[2,1,512]{2,1,0:T(1,128)} %chirp_hbm.1), custom_call_target="tpu_custom_call" | custom-call | flops 2000000000 | bytes 2097152 | tf_op jit(solution)/shard_map/range_filter/pallas_call | solution.py:214
  6.0 0.0 copy-start.1
  6.0 40.7 %all_to_all.5.x_ref = f32[64,32,128]{2,1,0:T(8,128)S(1)} all-to-all(f32[64,32,128]{2,1,0:T(8,128)} %range_filter.1), channel_id=1, replica_groups=mesh['chan'=4,'wide'=64] {'wide'}, dimensions={0} | all-to-all | bytes 2097152 | tf_op jit(solution)/shard_map/all_to_all | solution.py:221
  46.7 0.0 copy-done.1
  46.7 3.3 %azimuth_filter.1 = (f32[2,272,128]{2,1,0:T(8,128)S(1)}, f32[2,272,128]{2,1,0:T(8,128)S(1)}, f32[2,272,128]{2,1,0:T(8,128)S(1)}, f32[2,272,128]{2,1,0:T(8,128)S(1)}) custom-call(f32[64,32,128]{2,1,0:T(8,128)S(1)} %all_to_all.5.x_ref, f32[2,1,1024]{2,1,0:T(1,128)S(1)} %copy-done.1), custom_call_target="tpu_custom_call" | custom-call | flops 3000000000 | bytes 4194304 | tf_op jit(solution)/shard_map/azimuth_filter/pallas_call | solution.py:222
  50.0 0.1 collective-permute-start
  50.1 2.2 %collective-permute-start.1 = (f32[2,272,128]{2,1,0:T(8,128)S(1)}, f32[2,272,128]{2,1,0:T(8,128)S(1)}, u32[]{:S(2)}, u32[]{:S(2)}) collective-permute-start(f32[2,272,128]{2,1,0:T(8,128)S(1)} %get-tuple-element.13), channel_id=1, source_target_pairs={{0,128},{64,192},{128,0},{192,64},{1,129},{65,193},{129,1},{193,65... | collective-permute-start | bytes 835592 | tf_op jit(solution)/shard_map/ppermute | solution.py:229
  52.3 0.0 copy-start
  52.3 1.2 %collective-permute-start.2 = (f32[2,272,128]{2,1,0:T(8,128)S(1)}, f32[2,272,128]{2,1,0:T(8,128)S(1)}, u32[]{:S(2)}, u32[]{:S(2)}) collective-permute-start(f32[2,272,128]{2,1,0:T(8,128)S(1)} %get-tuple-element.14), channel_id=1, source_target_pairs={{0,192},{64,128},{128,64},{192,0},{1,193},{65,129},{129,65},{193,1... | collective-permute-start | bytes 835592 | tf_op jit(solution)/shard_map/ppermute | solution.py:229
  53.5 0.0 collective-permute-done.y1
  53.5 7.7 %collective-permute-done.1.y2 = f32[2,272,128]{2,1,0:T(8,128)S(1)} collective-permute-done((f32[2,272,128]{2,1,0:T(8,128)S(1)}, f32[2,272,128]{2,1,0:T(8,128)S(1)}, u32[]{:S(2)}, u32[]{:S(2)}) %collective-permute-start.1) | collective-permute-done | bytes 278560 | tf_op jit(solution)/shard_map/ppermute | solution.py:229
  61.2 5.0 %collective-permute-done.2.y3 = f32[2,272,128]{2,1,0:T(8,128)S(1)} collective-permute-done((f32[2,272,128]{2,1,0:T(8,128)S(1)}, f32[2,272,128]{2,1,0:T(8,128)S(1)}, u32[]{:S(2)}, u32[]{:S(2)}) %collective-permute-start.2) | collective-permute-done | bytes 278560 | tf_op jit(solution)/shard_map/ppermute | solution.py:229
  66.2 0.0 copy-done
  66.2 0.8 %fore_aft.1 = (f32[4,272,128]{2,1,0:T(8,128)S(1)}, f32[136,128]{1,0:T(8,128)S(1)}) custom-call(s32[4]{0:T(128)S(1)} %copy-done, f32[2,272,128]{2,1,0:T(8,128)S(1)} %get-tuple-element.11.y0, f32[2,272,128]{2,1,0:T(8,128)S(1)} %collective-permute-done.y1, f32[2,272,128]{2,1,0:T(8,128)S(1)} %collective-permute-done.1.y2, ...), custom_call_target="tpu_custom_call" | custom-call | flops 1000000 | bytes 2097152 | tf_op jit(solution)/shard_map/fore_aft/pallas_call | solution.py:231
  67.0 0.0 copy-start.2
  67.0 0.6 collective-permute-start.3
  67.7 0.0 copy-done.2
  67.7 0.1 copy.7.offsets_ref
  67.8 1.5 %window_sums.1.main_ref = f32[2,512,128]{2,1,0:T(8,128)S(1)} custom-call(s32[8,2]{1,0:T(8,128)S(1)} %copy.7.offsets_ref, f32[4,272,128]{2,1,0:T(8,128)S(1)} %get-tuple-element.15.sums_ref), custom_call_target="tpu_custom_call" | custom-call | flops 500000000 | bytes 1048576 | tf_op jit(solution)/shard_map/window_sums/pallas_call | solution.py:236
  69.3 5.2 %collective-permute-done.3.edge_ref = f32[136,128]{1,0:T(8,128)S(1)} collective-permute-done((f32[136,128]{1,0:T(8,128)S(1)}, f32[136,128]{1,0:T(8,128)S(1)}, u32[]{:S(2)}, u32[]{:S(2)}) %collective-permute-start.3) | collective-permute-done | bytes 69664 | tf_op jit(solution)/shard_map/ppermute | solution.py:235
  74.5 2.3 %coherence.1 = f32[2,256,128]{2,1,0:T(8,128)} custom-call(s32[8,2]{1,0:T(8,128)S(1)} %copy.7.offsets_ref, f32[2,512,128]{2,1,0:T(8,128)S(1)} %window_sums.1.main_ref, f32[136,128]{1,0:T(8,128)S(1)} %collective-permute-done.3.edge_ref), custom_call_target="tpu_custom_call" | custom-call | flops 500000000 | bytes 1048576 | tf_op jit(solution)/shard_map/coherence/pallas_call | solution.py:240
Async XLA Ops:
  6.0 40.8 %copy-start.1 = (f32[2,1,1024]{2,1,0:T(1,128)S(1)}, f32[2,1,1024]{2,1,0:T(1,128)}, u32[]{:S(2)}) copy-start(f32[2,1,1024]{2,1,0:T(1,128)} %taps_ref.1) | copy-start | bytes 24580
  50.0 3.5 %collective-permute-start = (f32[2,272,128]{2,1,0:T(8,128)S(1)}, f32[2,272,128]{2,1,0:T(8,128)S(1)}, u32[]{:S(2)}, u32[]{:S(2)}) collective-permute-start(f32[2,272,128]{2,1,0:T(8,128)S(1)} %get-tuple-element.12), channel_id=1, source_target_pairs={{0,64},{64,0},{128,192},{192,128},{1,65},{65,1},{129,193},{193,129... | collective-permute-start | bytes 835592 | tf_op jit(solution)/shard_map/ppermute | solution.py:229
  50.1 11.1 %collective-permute-start.1 = (f32[2,272,128]{2,1,0:T(8,128)S(1)}, f32[2,272,128]{2,1,0:T(8,128)S(1)}, u32[]{:S(2)}, u32[]{:S(2)}) collective-permute-start(f32[2,272,128]{2,1,0:T(8,128)S(1)} %get-tuple-element.13), channel_id=1, source_target_pairs={{0,128},{64,192},{128,0},{192,64},{1,129},{65,193},{129,1},{193,65... | collective-permute-start | bytes 835592 | tf_op jit(solution)/shard_map/ppermute | solution.py:229
  52.3 13.9 %copy-start = (s32[4]{0:T(128)S(1)}, s32[4]{0:T(128)}, u32[]{:S(2)}) copy-start(s32[4]{0:T(128)} %pairing_ref.1) | copy-start | bytes 52
  52.3 13.9 %collective-permute-start.2 = (f32[2,272,128]{2,1,0:T(8,128)S(1)}, f32[2,272,128]{2,1,0:T(8,128)S(1)}, u32[]{:S(2)}, u32[]{:S(2)}) collective-permute-start(f32[2,272,128]{2,1,0:T(8,128)S(1)} %get-tuple-element.14), channel_id=1, source_target_pairs={{0,192},{64,128},{128,64},{192,0},{1,193},{65,129},{129,65},{193,1... | collective-permute-start | bytes 835592 | tf_op jit(solution)/shard_map/ppermute | solution.py:229
  67.0 0.7 copy-start.2
  67.0 7.5 %collective-permute-start.3 = (f32[136,128]{1,0:T(8,128)S(1)}, f32[136,128]{1,0:T(8,128)S(1)}, u32[]{:S(2)}, u32[]{:S(2)}) collective-permute-start(f32[136,128]{1,0:T(8,128)S(1)} %get-tuple-element.16), channel_id=1, source_target_pairs={{0,63},{1,0},{2,1},{3,2},{4,3},{5,4},{6,5},{7,6},{8,7},{9,8},{10,9... | collective-permute-start | bytes 208904 | tf_op jit(solution)/shard_map/ppermute | solution.py:235

commit v3 on v2

v3 whole, which is shorter than its diff:
```python
import functools

import jax
import jax.numpy as jnp
from jax import lax
from jax.experimental import pallas as pl
from jax.experimental.pallas import tpu as pltpu
from jax.sharding import PartitionSpec as P

RADIUS = 4
REACH = 2 * RADIUS
XOR_ORDER = (0, 2, 3, 1)
F32 = jnp.float32
BF16 = jnp.bfloat16
VMEM_LIMIT = 24 * 1024 * 1024


def split(x):
    hi = x.astype(BF16)
    return hi, (x - hi.astype(F32)).astype(BF16)


def dot_nn(a, b):
    return lax.dot_general(a, b, (((1,), (0,)), ((), ())), preferred_element_type=F32)


def dot_nt(a, b):
    return lax.dot_general(a, b, (((1,), (1,)), ((), ())), preferred_element_type=F32)


def toeplitz(taps, rows, width, start=0):
    line = jnp.concatenate([taps, jnp.zeros((1, width - taps.shape[1]), F32)], 1)
    return pltpu.roll(jnp.broadcast_to(line, (rows, width)), start, 1, stride=1, stride_axis=0)


def range_kernel(echo_hbm, chirp_hbm, out_ref, echo, chirp, e_hi, e_lo, w_hi, w_lo, sems):
    taps_copy = pltpu.make_async_copy(chirp_hbm, chirp, sems.at[4])
    taps_copy.start()
    copies = []
    for m in range(4):
        bins = pl.ds(2048 * m, 2048)
        copies.append(pltpu.make_async_copy(echo_hbm.at[:, :, bins], echo.at[:, :, bins], sems.at[m]))
        copies[m].start()
    e_hi[1024:1088, :] = jnp.zeros((64, 256), BF16)
    e_lo[1024:1088, :] = jnp.zeros((64, 256), BF16)
    taps_copy.wait()
    real = split(toeplitz(chirp[0], 128, 640))
    imag = split(toeplitz(chirp[1], 128, 640))
    for w_ref, re, im in ((w_hi, real[0], imag[0]), (w_lo, real[1], imag[1])):
        for j in range(5):
            cols = slice(128 * j, 128 * j + 128)
            w_ref[0:128, 256 * j:256 * j + 128] = re[:, cols]
            w_ref[0:128, 256 * j + 128:256 * j + 256] = -im[:, cols]
            w_ref[128:256, 256 * j:256 * j + 128] = im[:, cols]
            w_ref[128:256, 256 * j + 128:256 * j + 256] = re[:, cols]

    def fill(m):
        copies[m].wait()
        for n in range(16 * m, 16 * m + 16):
            for part in range(2):
                hi, lo = split(echo[part, :, 128 * n:128 * n + 128])
                e_hi[16 * n:16 * n + 16, 128 * part:128 * part + 128] = hi
                e_lo[16 * n:16 * n + 16, 128 * part:128 * part + 128] = lo

    fill(0)
    early = lax.broadcasted_iota(jnp.int32, (256, 128), 1) < REACH
    last = [jnp.zeros((16, 128), F32)] * 2
    for m in range(4):
        if m < 3:
            fill(m + 1)
        starts = [256 * m + 16 * j for j in range(5)]
        hi = jnp.concatenate([e_hi[s:s + 256, :] for s in starts], 1)
        lo = jnp.concatenate([e_lo[s:s + 256, :] for s in starts], 1)
        acc = dot_nt(hi, w_hi[...]) + dot_nt(hi, w_lo[...]) + dot_nt(lo, w_hi[...])
        for part in range(2):
            turned = pltpu.roll(acc[:, 128 * part:128 * part + 128], REACH, 1)
            before = jnp.concatenate([last[part], turned[0:240]], 0)
            out_ref[16 * m:16 * m + 16, 16 * part:16 * part + 16, :] = jnp.where(early, before, turned).reshape(16, 16, 128)
            last[part] = turned[240:256]
    for part in range(2):
        out_ref[0, 16 * part:16 * part + 16, 0:REACH] = last[part][:, 0:REACH]


def prepare_kernel(pairing_ref, offsets_ref, weight_ref, rows_ref, near_ref, far_ref):
    me = lax.axis_index("chan")
    first = lax.axis_index("wide") == 0
    final = lax.axis_index("wide") == lax.axis_size("wide") - 1
    for i, k in enumerate(XOR_ORDER):
        member = (pairing_ref[0] == (me ^ k)) | (pairing_ref[1] == (me ^ k))
        weight_ref[i] = jnp.full((8, 128), jnp.where(member, 1.0, 0.0), F32)
    row = lax.broadcasted_iota(jnp.int32, (128, 256), 0)
    src = lax.broadcasted_iota(jnp.int32, (128, 256), 1)
    lane = lax.broadcasted_iota(jnp.int32, (128, 128), 0)
    bin_out = lax.broadcasted_iota(jnp.int32, (128, 128), 1)
    for g in range(2):
        oa = offsets_ref[2 * me + g, 0]
        orr = offsets_ref[2 * me + g, 1]
        rows_ref[g] = jnp.where(jnp.abs(src - REACH - row - oa) <= RADIUS, 1.0, 0.0).astype(BF16)
        near = (jnp.abs(lane - REACH - bin_out - orr) <= RADIUS) & ((lane >= REACH) | jnp.logical_not(first))
        near_ref[g] = jnp.where(near, 1.0, 0.0).astype(BF16)
        far = (jnp.abs(lane + 128 - REACH - bin_out - orr) <= RADIUS) & (
            (lane < REACH) | ((lane < 2 * REACH) & jnp.logical_not(final))
        )
        far_ref[g] = jnp.where(far, 1.0, 0.0).astype(BF16)


def azimuth_half(flip, x_ref, taps_ref, order_ref, o0, o1, done_ref, t_hi, t_lo, x_hi, x_lo, y_ref):
    done_ref[...] = jnp.zeros((8, 128), F32)
    for part in range(2):
        hi, lo = split(toeplitz(taps_ref[part], 272, 1280, 1280 - REACH))
        t_hi[part] = hi
        t_lo[part] = lo
        hi, lo = split(x_ref[:, 16 * part:16 * part + 16, :].reshape(1024, 128))
        x_hi[:, 128 * part:128 * part + 128] = hi
        x_lo[:, 128 * part:128 * part + 128] = lo
    me = lax.axis_index("chan")

    def quarter(q):
        first, last = max(q - 2, 0), min(q + 2, 3)
        cols = slice(256 * (first - q + 2), 256 * (last - q + 3))
        rows = slice(256 * first, 256 * last + 256)
        t = [ref[part, :, cols] for ref in (t_hi, t_lo) for part in range(2)]
        g = [dot_nn(t[i], x_hi[rows, :]) + dot_nn(t[i], x_lo[rows, :]) + dot_nn(t[2 + i], x_hi[rows, :]) for i in range(2)]
        return g[0][:, 0:128] - g[1][:, 128:256], g[0][:, 128:256] + g[1][:, 0:128]

    for half in range(2):
        @pl.when((me // 2) ^ flip == half)
        def _(half=half):
            for i in range(2):
                for part, value in enumerate(quarter(2 * half + i)):
                    y_ref[i, part] = value
            for part in range(2):
                y_ref[0, part, 264:272, :] = y_ref[1, part, 8:16, :]
                y_ref[1, part, 0:8, :] = y_ref[0, part, 256:264, :]
                if half == 0:
                    y_ref[0, part, 0:8, :] = jnp.zeros((8, 128), F32)
                else:
                    y_ref[1, part, 264:272, :] = jnp.zeros((8, 128), F32)

    o0[...] = y_ref[me % 2]
    o1[...] = y_ref[1 - me % 2]


def partial_kernel(weight_ref, y0, y2, y3, part_ref):
    for part in range(2):
        fore = aft = 0.0
        for k, y_ref in enumerate((y0, y2, y3)):
            weight = weight_ref[k, 0:1, :]
            y = y_ref[part]
            fore = fore + y * weight
            aft = aft + y * (1.0 - weight)
        part_ref[part] = fore
        part_ref[2 + part] = aft


def whole_sums(weight_ref, part_ref, y1):
    weight = weight_ref[3, 0:1, :]
    fore = [part_ref[part] + y1[part] * weight for part in range(2)]
    return fore + [part_ref[2 + part] + y1[part] * (1.0 - weight) for part in range(2)]


def edge_kernel(weight_ref, part_ref, y1, edge_ref):
    lane = lax.broadcasted_iota(jnp.int32, (272, 128), 1)
    edge = jnp.zeros((272, 128), F32)
    for plane, value in enumerate(whole_sums(weight_ref, part_ref, y1)):
        at = 16 * plane
        moved = pltpu.roll(value, at, 1) if at else value
        edge = jnp.where((lane >= at) & (lane < at + 16), moved, edge)
    edge_ref[...] = edge[0:136] + pltpu.roll(edge[136:272], 64, 1)


def quantities(fr, fi, ar, ai):
    return fr * ar + fi * ai, fi * ar - fr * ai, fr * fr + fi * fi, ar * ar + ai * ai


def main_kernel(weight_ref, rows_ref, near_ref, part_ref, y1, out_ref, p_hi, p_lo):
    for q, value in enumerate(quantities(*whole_sums(weight_ref, part_ref, y1))):
        hi, lo = split(value)
        p_hi[0:272, 128 * q:128 * q + 128] = hi
        p_lo[0:272, 128 * q:128 * q + 128] = lo
    p_hi[272:384, :] = jnp.zeros((112, 512), BF16)
    p_lo[272:384, :] = jnp.zeros((112, 512), BF16)
    for g in range(2):
        sums = dot_nn(rows_ref[g], p_hi[128 * g:128 * g + 256, :]) + dot_nn(rows_ref[g], p_lo[128 * g:128 * g + 256, :])
        hi, lo = split(jnp.concatenate([sums[:, 128 * q:128 * q + 128] for q in range(4)], 0))
        out_ref[g] = dot_nn(hi, near_ref[g]) + dot_nn(lo, near_ref[g])


def coherence_kernel(rows_ref, far_ref, main_ref, edge_ref, out_ref, p_hi, p_lo):
    packed = edge_ref[...]
    edge = jnp.concatenate([packed, pltpu.roll(packed, 64, 1)], 0)
    lane = lax.broadcasted_iota(jnp.int32, (272, 128), 1)
    planes = [edge] + [pltpu.roll(edge, 128 - 16 * i, 1) for i in range(1, 4)]
    both = jnp.zeros((272, 128), F32)
    for q, value in enumerate(quantities(*planes)):
        moved = pltpu.roll(value, 16 * q, 1) if q else value
        both = jnp.where((lane >= 16 * q) & (lane < 16 * q + 16), moved, both)
    hi, lo = split(both)
    p_hi[0:272, :] = hi
    p_lo[0:272, :] = lo
    p_hi[272:384, :] = jnp.zeros((112, 128), BF16)
    p_lo[272:384, :] = jnp.zeros((112, 128), BF16)
    for g in range(2):
        sums = dot_nn(rows_ref[g], p_hi[128 * g:128 * g + 256, :]) + dot_nn(rows_ref[g], p_lo[128 * g:128 * g + 256, :])
        hi, lo = split(jnp.concatenate([sums] + [pltpu.roll(sums, 128 - 16 * q, 1) for q in range(1, 4)], 0))
        window = main_ref[g] + dot_nn(hi, far_ref[g]) + dot_nn(lo, far_ref[g])
        scale = 1.0 / jnp.sqrt(jnp.maximum(window[256:384], 1.0) * jnp.maximum(window[384:512], 1.0))
        out_ref[0, 128 * g:128 * g + 128, :] = window[0:128] * scale
        out_ref[1, 128 * g:128 * g + 128, :] = window[128:256] * scale


def call(kernel, name, out_shape, scratch, n_in, smem=(), hbm=(), flops=0, moved=0, vmem=VMEM_LIMIT):
    spaces = [pltpu.SMEM if i in smem else pltpu.HBM if i in hbm else pltpu.VMEM for i in range(n_in)]
    return pl.pallas_call(
        kernel,
        out_shape=out_shape,
        in_specs=[pl.BlockSpec(memory_space=space) for space in spaces],
        out_specs=jax.tree.map(lambda _: pl.BlockSpec(memory_space=pltpu.VMEM), out_shape),
        scratch_shapes=scratch,
        compiler_params=pltpu.CompilerParams(vmem_limit_bytes=vmem),
        cost_estimate=pl.CostEstimate(flops=flops, bytes_accessed=moved, transcendentals=0),
        name=name,
    )


def shape(*dims, dtype=F32):
    return jax.ShapeDtypeStruct(dims, dtype)


def body(echoes, range_chirp, azimuth_filter, pairing, offsets):
    signal = echoes[:, 0]
    chirp = range_chirp.reshape(2, 1, 512)
    taps = azimuth_filter.reshape(2, 1, 1024)
    parted = call(
        range_kernel, "range_filter", shape(64, 32, 128),
        [pltpu.VMEM((2, 16, 8192), F32), pltpu.VMEM((2, 1, 512), F32)]
        + [pltpu.VMEM((1088, 256), BF16)] * 2 + [pltpu.VMEM((256, 1280), BF16)] * 2
        + [pltpu.SemaphoreType.DMA((5,))],
        2, hbm=(0, 1), flops=2_000_000_000, moved=2 << 20, vmem=60 << 20,
    )(signal, chirp)
    turned = lax.all_to_all(parted, "wide", split_axis=0, concat_axis=0, tiled=True)
    weight, rows, near, far = call(
        prepare_kernel, "prepare",
        (shape(4, 8, 128), shape(2, 128, 256, dtype=BF16)) + (shape(2, 128, 128, dtype=BF16),) * 2, [],
        2, smem=(0, 1), flops=1_000_000_000, moved=1 << 20,
    )(pairing, offsets)
    order = weight.reshape(32, 128)
    pieces = []
    for flip in (1, 0):
        *pair, order = call(
            functools.partial(azimuth_half, flip), "azimuth_" + ("own", "other")[flip],
            (shape(2, 272, 128),) * 2 + (shape(8, 128),),
            [pltpu.VMEM((2, 272, 1280), BF16)] * 2 + [pltpu.VMEM((1024, 256), BF16)] * 2
            + [pltpu.VMEM((2, 2, 272, 128), F32)],
            3, flops=1_500_000_000, moved=4 << 20,
        )(turned, taps, order)
        pieces.append(pair)
    (p2, p3), (p0, p1) = pieces
    y2, y3, y1 = [lax.ppermute(p, "chan", [(i, i ^ k) for i in range(4)]) for k, p in zip(XOR_ORDER[1:], (p2, p3, p1))]
    part = call(
        partial_kernel, "three_receivers", shape(4, 272, 128), [], 4, flops=1_000_000, moved=2 << 20,
    )(weight, p0, y2, y3)
    edge = call(
        edge_kernel, "edge", shape(136, 128), [], 3, flops=1_000_000, moved=2 << 20,
    )(weight, part, y1)
    after = lax.ppermute(edge, "wide", [(i, (i - 1) % 64) for i in range(64)])
    main = call(
        main_kernel, "window_sums", shape(2, 512, 128), [pltpu.VMEM((384, 512), BF16)] * 2,
        5, flops=500_000_000, moved=1 << 20,
    )(weight, rows, near, part, y1)
    return call(
        coherence_kernel, "coherence", shape(2, 256, 128), [pltpu.VMEM((384, 128), BF16)] * 2,
        4, flops=500_000_000, moved=1 << 20,
    )(rows, far, main, after)


def solution(mesh):
    placed = (P(None, "chan", "wide", None), P(None, "chan", None), P(None, "chan", None), P(), P())
    return jax.shard_map(
        body, mesh=mesh, in_specs=placed, out_specs=P(None, "chan", "wide"), check_vma=False
    )
```

time: 77 us -> 72.3 us (0.939)
  blocking collectives: 40.7 us -> 0 us
  waiting for transfers between devices: 17.9 us -> 38.4 us
  starting transfers between devices: 4.1 us -> 17.8 us
  Pallas kernels: 13.8 us -> 14.8 us
    all_to_all x1 -> x0, blocking collectives: 40.7 us -> none  [body(): lax.all_to_all(parted, 'wide', split_axis=0, concat_axis=0, tiled=True)]
    all_to_all x0 -> x1, waiting for transfers between devices: none -> 26.6 us  [body(): lax.all_to_all(parted, 'wide', split_axis=0, concat_axis=0, tiled=True)]
    all_to_all x0 -> x1, starting transfers between devices: none -> 12.8 us  [body(): lax.all_to_all(parted, 'wide', split_axis=0, concat_axis=0, tiled=True)]
    ppermute x3, waiting for transfers between devices: 12.7 us -> 6.07 us  [body(): lax.ppermute(p, 'chan', [(i, i ^ k) for i in range(4)])]
    pallas_call x2 -> x5, Pallas kernels: 4.13 us -> 6.32 us  [the longest x2 5.29 us: body(): call(functools.partial(azimuth_half, flip), 'azimuth_' + ('own', 'other')...]
  transfers between devices with their start and end apart: 4 -> 5, of which waited for: 3 -> 4; matrix products, arithmetic and copies ran while one was open for 0% -> 0% of each run, Pallas kernels for 2% -> 6%
where the time goes in v3:
time: 72.3 us; the launch traced here: 71.7 us
  waiting for transfers between devices  38.4 us (53%)
  starting transfers between devices  17.8 us (25%)
  Pallas kernels  14.8 us (20%)
    all_to_all x1, waiting for transfers between devices, body(): lax.all_to_all(parted, 'wide', split_axis=0, concat_axis=0, tiled=True)  26.6 us
    all_to_all x1, starting transfers between devices, body(): lax.all_to_all(parted, 'wide', split_axis=0, concat_axis=0, tiled=True)  12.8 us
    ppermute x3, waiting for transfers between devices, body(): lax.ppermute(p, 'chan', [(i, i ^ k) for i in range(4)])  6.07 us
    pallas_call x1, Pallas kernels, body(): call(range_kernel, 'range_filter', shape(64, 32, 128), [pltpu.VMEM((2, 16...  5.95 us
    ppermute x1, waiting for transfers between devices, body(): after = lax.ppermute(edge, 'wide', [(i, (i - 1) % 64) for i in range(64)])  5.73 us
    pallas_call x2, Pallas kernels, body(): call(functools.partial(azimuth_half, flip), 'azimuth_' + ('own', 'other')...  5.29 us
    ppermute x3, starting transfers between devices, body(): lax.ppermute(p, 'chan', [(i, i ^ k) for i in range(4)])  3.73 us
    pallas_call x1, Pallas kernels, body(): call(coherence_kernel, 'coherence', shape(2, 256, 128), [pltpu.VMEM((384,...  1.66 us
  transfers between devices with their start and end apart: 5, of which 4 were waited for; matrix products, arithmetic and copies ran while one was open for 0% of the time, Pallas kernels for 6%

profile of v3, /device:TPU:26, one launch (start us, length us, event | category | flops | bytes accessed | tf_op | source)
XLA Modules:
  0.0 71.7 jit_solution(12889594301123649669)
XLA Ops:
  0.0 6.0 %range_filter.1 = f32[64,32,128]{2,1,0:T(8,128)} custom-call(f32[2,16,8192]{2,1,0:T(8,128)} %bitcast.3, f32[2,1,512]{2,1,0:T(1,128)} %chirp_hbm.1), custom_call_target="tpu_custom_call" | custom-call | flops 2000000000 | bytes 2097152 | tf_op jit(solution)/shard_map/range_filter/pallas_call | solution.py:234
  6.0 0.0 copy-start.2
  6.0 12.8 %all-to-all-start = ((f32[64,32,128]{2,1,0:T(8,128)}), f32[64,32,128]{2,1,0:T(8,128)S(1)}, u32[]{:S(2)}, u32[]{:S(2)}) async-start(f32[64,32,128]{2,1,0:T(8,128)} %range_filter.1), calls=%async_computation | async-start | bytes 2097152 | tf_op jit(solution)/shard_map/all_to_all | solution.py:241
  18.8 0.0 copy-done.2
  18.8 0.0 copy-start.1
  18.8 0.1 copy.6.offsets_ref
  18.9 0.6 copy-done.1
  19.4 0.0 copy-start
  19.4 0.7 prepare.1
  20.1 26.6 %all-to-all-done.x_ref = f32[64,32,128]{2,1,0:T(8,128)S(1)} async-done(((f32[64,32,128]{2,1,0:T(8,128)}), f32[64,32,128]{2,1,0:T(8,128)S(1)}, u32[]{:S(2)}, u32[]{:S(2)}) %all-to-all-start) | async-done | bytes 1048608 | tf_op jit(solution)/shard_map/all_to_all | solution.py:241
  46.7 0.0 copy-done
  46.7 2.4 %azimuth_other.1 = (f32[2,272,128]{2,1,0:T(8,128)S(1)}, f32[2,272,128]{2,1,0:T(8,128)S(1)}, f32[8,128]{1,0:T(8,128)S(1)}) custom-call(f32[64,32,128]{2,1,0:T(8,128)S(1)} %all-to-all-done.x_ref, f32[2,1,1024]{2,1,0:T(1,128)S(1)} %copy-done, f32[32,128]{1,0:T(8,128)S(1)} %bitcast.2), custom_call_target="tpu_custom_call" | custom-call | flops 1500000000 | bytes 4194304 | tf_op jit(solution)/shard_map/azimuth_other/pallas_call | solution.py:250
  49.1 2.2 %collective-permute-start = (f32[2,272,128]{2,1,0:T(8,128)S(1)}, f32[2,272,128]{2,1,0:T(8,128)S(1)}, u32[]{:S(2)}, u32[]{:S(2)}) collective-permute-start(f32[2,272,128]{2,1,0:T(8,128)S(1)} %get-tuple-element.20), channel_id=1, source_target_pairs={{0,128},{64,192},{128,0},{192,64},{1,129},{65,193},{129,1},{193,65... | collective-permute-start | bytes 835592 | tf_op jit(solution)/shard_map/ppermute | solution.py:259
  51.3 0.0 collective-permute-start.1
  51.3 2.9 %azimuth_own.1 = (f32[2,272,128]{2,1,0:T(8,128)S(1)}, f32[2,272,128]{2,1,0:T(8,128)S(1)}, f32[8,128]{1,0:T(8,128)}) custom-call(f32[64,32,128]{2,1,0:T(8,128)S(1)} %all-to-all-done.x_ref, f32[2,1,1024]{2,1,0:T(1,128)S(1)} %copy-done, f32[8,128]{1,0:T(8,128)S(1)} %get-tuple-element.18.order_ref), custom_call_target="tpu_custom_call" | custom-call | flops 1500000000 | bytes 4194304 | tf_op jit(solution)/shard_map/azimuth_own/pallas_call | solution.py:250
  54.2 1.5 %collective-permute-start.2 = (f32[2,272,128]{2,1,0:T(8,128)S(1)}, f32[2,272,128]{2,1,0:T(8,128)S(1)}, u32[]{:S(2)}, u32[]{:S(2)}) collective-permute-start(f32[2,272,128]{2,1,0:T(8,128)S(1)} %get-tuple-element.22), channel_id=1, source_target_pairs={{0,64},{64,0},{128,192},{192,128},{1,65},{65,1},{129,193},{193,129... | collective-permute-start | bytes 835592 | tf_op jit(solution)/shard_map/ppermute | solution.py:259
  55.8 2.9 %collective-permute-done.y2 = f32[2,272,128]{2,1,0:T(8,128)S(1)} collective-permute-done((f32[2,272,128]{2,1,0:T(8,128)S(1)}, f32[2,272,128]{2,1,0:T(8,128)S(1)}, u32[]{:S(2)}, u32[]{:S(2)}) %collective-permute-start) | collective-permute-done | bytes 278560 | tf_op jit(solution)/shard_map/ppermute | solution.py:259
  58.6 3.2 %collective-permute-done.1.y3 = f32[2,272,128]{2,1,0:T(8,128)S(1)} collective-permute-done((f32[2,272,128]{2,1,0:T(8,128)S(1)}, f32[2,272,128]{2,1,0:T(8,128)S(1)}, u32[]{:S(2)}, u32[]{:S(2)}) %collective-permute-start.1) | collective-permute-done | bytes 278560 | tf_op jit(solution)/shard_map/ppermute | solution.py:259
  61.8 0.1 three_receivers.1.part_ref
  61.9 0.0 collective-permute-done.2.y1
  62.0 0.2 edge.1
  62.2 1.2 %collective-permute-start.3 = (f32[136,128]{1,0:T(8,128)S(1)}, f32[136,128]{1,0:T(8,128)S(1)}, u32[]{:S(2)}, u32[]{:S(2)}) collective-permute-start(f32[136,128]{1,0:T(8,128)S(1)} %edge.1), channel_id=1, source_target_pairs={{0,63},{1,0},{2,1},{3,2},{4,3},{5,4},{6,5},{7,6},{8,7},{9,8},{10,9... | collective-permute-start | bytes 208904 | tf_op jit(solution)/shard_map/ppermute | solution.py:266
  63.4 0.9 %window_sums.1.main_ref = f32[2,512,128]{2,1,0:T(8,128)S(1)} custom-call(f32[4,8,128]{2,1,0:T(8,128)S(1)} %get-tuple-element.16.weight_ref, bf16[2,128,256]{2,1,0:T(8,128)(2,1)S(1)} %get-tuple-element.14.rows_ref, bf16[2,128,128]{2,1,0:T(8,128)(2,1)S(1)} %get-tuple-element.17.near_ref, f32[4,272,128]{2,1,0:T(8,128)S(1)} %three_receivers.1.part_ref, ...), custom_call_target="tpu_custom_call" | custom-call | flops 500000000 | bytes 1048576 | tf_op jit(solution)/shard_map/window_sums/pallas_call | solution.py:267
  64.3 5.7 %collective-permute-done.3.edge_ref = f32[136,128]{1,0:T(8,128)S(1)} collective-permute-done((f32[136,128]{1,0:T(8,128)S(1)}, f32[136,128]{1,0:T(8,128)S(1)}, u32[]{:S(2)}, u32[]{:S(2)}) %collective-permute-start.3) | collective-permute-done | bytes 69664 | tf_op jit(solution)/shard_map/ppermute | solution.py:266
  70.1 1.7 %coherence.1 = f32[2,256,128]{2,1,0:T(8,128)} custom-call(bf16[2,128,256]{2,1,0:T(8,128)(2,1)S(1)} %get-tuple-element.14.rows_ref, bf16[2,128,128]{2,1,0:T(8,128)(2,1)S(1)} %get-tuple-element.15.far_ref, f32[2,512,128]{2,1,0:T(8,128)S(1)} %window_sums.1.main_ref, f32[136,128]{1,0:T(8,128)S(1)} %collective-permute-done.3.edge_ref), custom_call_target="tpu_custom_call" | custom-call | flops 500000000 | bytes 1048576 | tf_op jit(solution)/shard_map/coherence/pallas_call | solution.py:271
Async XLA Ops:
  6.0 12.8 %copy-start.2 = (s32[8,2]{0,1:T(2,128)S(1)}, s32[8,2]{0,1:T(2,128)}, u32[]{:S(2)}) copy-start(s32[8,2]{0,1:T(2,128)} %param.9) | copy-start | bytes 196
  6.0 40.7 %all-to-all-start = ((f32[64,32,128]{2,1,0:T(8,128)}), f32[64,32,128]{2,1,0:T(8,128)S(1)}, u32[]{:S(2)}, u32[]{:S(2)}) async-start(f32[64,32,128]{2,1,0:T(8,128)} %range_filter.1), calls=%async_computation | async-start | bytes 2097152 | tf_op jit(solution)/shard_map/all_to_all | solution.py:241
  18.8 0.7 copy-start.1
  19.4 27.3 %copy-start = (f32[2,1,1024]{2,1,0:T(1,128)S(1)}, f32[2,1,1024]{2,1,0:T(1,128)}, u32[]{:S(2)}) copy-start(f32[2,1,1024]{2,1,0:T(1,128)} %taps_ref.3) | copy-start | bytes 24580
  49.1 9.5 %collective-permute-start = (f32[2,272,128]{2,1,0:T(8,128)S(1)}, f32[2,272,128]{2,1,0:T(8,128)S(1)}, u32[]{:S(2)}, u32[]{:S(2)}) collective-permute-start(f32[2,272,128]{2,1,0:T(8,128)S(1)} %get-tuple-element.20), channel_id=1, source_target_pairs={{0,128},{64,192},{128,0},{192,64},{1,129},{65,193},{129,1},{193,65... | collective-permute-start | bytes 835592 | tf_op jit(solution)/shard_map/ppermute | solution.py:259
  51.3 10.5 %collective-permute-start.1 = (f32[2,272,128]{2,1,0:T(8,128)S(1)}, f32[2,272,128]{2,1,0:T(8,128)S(1)}, u32[]{:S(2)}, u32[]{:S(2)}) collective-permute-start(f32[2,272,128]{2,1,0:T(8,128)S(1)} %get-tuple-element.21), channel_id=1, source_target_pairs={{0,192},{64,128},{128,64},{192,0},{1,193},{65,129},{129,65},{193,1... | collective-permute-start | bytes 835592 | tf_op jit(solution)/shard_map/ppermute | solution.py:259
  54.2 7.7 %collective-permute-start.2 = (f32[2,272,128]{2,1,0:T(8,128)S(1)}, f32[2,272,128]{2,1,0:T(8,128)S(1)}, u32[]{:S(2)}, u32[]{:S(2)}) collective-permute-start(f32[2,272,128]{2,1,0:T(8,128)S(1)} %get-tuple-element.22), channel_id=1, source_target_pairs={{0,64},{64,0},{128,192},{192,128},{1,65},{65,1},{129,193},{193,129... | collective-permute-start | bytes 835592 | tf_op jit(solution)/shard_map/ppermute | solution.py:259
  62.2 7.9 %collective-permute-start.3 = (f32[136,128]{1,0:T(8,128)S(1)}, f32[136,128]{1,0:T(8,128)S(1)}, u32[]{:S(2)}, u32[]{:S(2)}) collective-permute-start(f32[136,128]{1,0:T(8,128)S(1)} %edge.1), channel_id=1, source_target_pairs={{0,63},{1,0},{2,1},{3,2},{4,3},{5,4},{6,5},{7,6},{8,7},{9,8},{10,9... | collective-permute-start | bytes 208904 | tf_op jit(solution)/shard_map/ppermute | solution.py:266

commit v4 on v3

v4 whole, which is shorter than its diff:
```python
import functools

import jax
import jax.numpy as jnp
from jax import lax
from jax.experimental import pallas as pl
from jax.experimental.pallas import tpu as pltpu
from jax.sharding import PartitionSpec as P

RADIUS = 4
REACH = 2 * RADIUS
XOR_ORDER = (0, 2, 3, 1)
F32 = jnp.float32
BF16 = jnp.bfloat16
VMEM_LIMIT = 24 * 1024 * 1024


def split(x):
    hi = x.astype(BF16)
    return hi, (x - hi.astype(F32)).astype(BF16)


def dot_nn(a, b):
    return lax.dot_general(a, b, (((1,), (0,)), ((), ())), preferred_element_type=F32)


def dot_nt(a, b):
    return lax.dot_general(a, b, (((1,), (1,)), ((), ())), preferred_element_type=F32)


def toeplitz(taps, rows, width, start=0):
    line = jnp.concatenate([taps, jnp.zeros((1, width - taps.shape[1]), F32)], 1)
    return pltpu.roll(jnp.broadcast_to(line, (rows, width)), start, 1, stride=1, stride_axis=0)


def range_kernel(echo_hbm, chirp_hbm, out_hbm, echo, chirp, out, e_hi, e_lo, w_hi, w_lo, sems, out_sems):
    taps_copy = pltpu.make_async_copy(chirp_hbm, chirp, sems.at[4])
    taps_copy.start()
    copies = []
    for m in range(4):
        bins = pl.ds(2048 * m, 2048)
        copies.append(pltpu.make_async_copy(echo_hbm.at[:, :, bins], echo.at[:, :, bins], sems.at[m]))
        copies[m].start()
    e_hi[1024:1088, :] = jnp.zeros((64, 256), BF16)
    e_lo[1024:1088, :] = jnp.zeros((64, 256), BF16)
    taps_copy.wait()
    real = split(toeplitz(chirp[0], 128, 640))
    imag = split(toeplitz(chirp[1], 128, 640))
    for w_ref, re, im in ((w_hi, real[0], imag[0]), (w_lo, real[1], imag[1])):
        for j in range(5):
            cols = slice(128 * j, 128 * j + 128)
            w_ref[0:128, 256 * j:256 * j + 128] = re[:, cols]
            w_ref[0:128, 256 * j + 128:256 * j + 256] = -im[:, cols]
            w_ref[128:256, 256 * j:256 * j + 128] = im[:, cols]
            w_ref[128:256, 256 * j + 128:256 * j + 256] = re[:, cols]
    for copy in copies:
        copy.wait()

    def fill(first, end):
        for n in range(first, min(end, 64)):
            for part in range(2):
                hi, lo = split(echo[part, :, 128 * n:128 * n + 128])
                e_hi[16 * n:16 * n + 16, 128 * part:128 * part + 128] = hi
                e_lo[16 * n:16 * n + 16, 128 * part:128 * part + 128] = lo

    def send(sem, first, count):
        copy = pltpu.make_async_copy(out.at[pl.ds(first, count)], out_hbm.at[pl.ds(first, count)], out_sems.at[sem])
        copy.start()
        return copy

    fill(0, 4)
    early = lax.broadcasted_iota(jnp.int32, (256, 128), 1) < REACH
    last = [jnp.zeros((16, 128), F32)] * 2
    sent = []
    for m in range(4):
        fill(16 * m + 4, 16 * m + 20)
        starts = [256 * m + 16 * j for j in range(5)]
        hi = [e_hi[s:s + 256, :] for s in starts]
        lo = [e_lo[s:s + 256, :] for s in starts]
        acc = dot_nt(
            jnp.concatenate(hi + hi + lo, 1), jnp.concatenate([w_hi[...], w_lo[...], w_hi[...]], 1)
        )
        for part in range(2):
            turned = pltpu.roll(acc[:, 128 * part:128 * part + 128], REACH, 1)
            before = jnp.concatenate([last[part], turned[0:240]], 0)
            out[16 * m:16 * m + 16, 16 * part:16 * part + 16, :] = jnp.where(early, before, turned).reshape(16, 16, 128)
            last[part] = turned[240:256]
        if m == 3:
            for part in range(2):
                out[0, 16 * part:16 * part + 16, 0:REACH] = last[part][:, 0:REACH]
            sent.append(send(4, 0, 1))
        sent.append(send(m, max(16 * m, 1), 16 if m else 15))
    for copy in sent:
        copy.wait()


def prepare_kernel(pairing_ref, offsets_ref, weight_ref, rows_ref, cols_ref):
    me = lax.axis_index("chan")
    first = lax.axis_index("wide") == 0
    final = lax.axis_index("wide") == lax.axis_size("wide") - 1
    for i, k in enumerate(XOR_ORDER):
        member = (pairing_ref[0] == (me ^ k)) | (pairing_ref[1] == (me ^ k))
        weight_ref[i] = jnp.full((8, 128), jnp.where(member, 1.0, 0.0), F32)
    row = lax.broadcasted_iota(jnp.int32, (128, 256), 0)
    src = lax.broadcasted_iota(jnp.int32, (128, 256), 1)
    lane = lax.broadcasted_iota(jnp.int32, (128, 128), 0)
    bin_out = lax.broadcasted_iota(jnp.int32, (128, 128), 1)
    for g in range(2):
        oa = offsets_ref[2 * me + g, 0]
        orr = offsets_ref[2 * me + g, 1]
        rows_ref[g] = jnp.where(jnp.abs(src - REACH - row - oa) <= RADIUS, 1.0, 0.0).astype(BF16)
        near = (jnp.abs(lane - REACH - bin_out - orr) <= RADIUS) & ((lane >= REACH) | jnp.logical_not(first))
        cols_ref[g, 0:128] = jnp.where(near, 1.0, 0.0).astype(BF16)
        far = (jnp.abs(lane + 128 - REACH - bin_out - orr) <= RADIUS) & (
            (lane < REACH) | ((lane < 2 * REACH) & jnp.logical_not(final))
        )
        cols_ref[g, 128:256] = jnp.where(far, 1.0, 0.0).astype(BF16)


def azimuth_half(flip, x_ref, taps_ref, order_ref, o0, o1, e0, e1, done_ref, t_hi, t_lo, x_hi, x_lo, y_ref):
    done_ref[...] = jnp.zeros((8, 128), F32)
    for part in range(2):
        hi, lo = split(toeplitz(taps_ref[part], 272, 1280, 1280 - REACH))
        t_hi[part] = hi
        t_lo[part] = lo
        hi, lo = split(x_ref[:, 16 * part:16 * part + 16, :].reshape(1024, 128))
        x_hi[:, 128 * part:128 * part + 128] = hi
        x_lo[:, 128 * part:128 * part + 128] = lo
    me = lax.axis_index("chan")

    def quarter(q):
        first, last = max(q - 2, 0), min(q + 2, 3)
        cols = slice(256 * (first - q + 2), 256 * (last - q + 3))
        rows = slice(256 * first, 256 * last + 256)
        t = [ref[part, :, cols] for ref in (t_hi, t_lo) for part in range(2)]
        g = [dot_nn(t[i], x_hi[rows, :]) + dot_nn(t[i], x_lo[rows, :]) + dot_nn(t[2 + i], x_hi[rows, :]) for i in range(2)]
        return g[0][:, 0:128] - g[1][:, 128:256], g[0][:, 128:256] + g[1][:, 0:128]

    for half in range(2):
        @pl.when((me // 2) ^ flip == half)
        def _(half=half):
            for i in range(2):
                for part, value in enumerate(quarter(2 * half + i)):
                    y_ref[i, part] = value
            for part in range(2):
                y_ref[0, part, 264:272, :] = y_ref[1, part, 8:16, :]
                y_ref[1, part, 0:8, :] = y_ref[0, part, 256:264, :]
                if half == 0:
                    y_ref[0, part, 0:8, :] = jnp.zeros((8, 128), F32)
                else:
                    y_ref[1, part, 264:272, :] = jnp.zeros((8, 128), F32)

    for i, o_ref, e_ref in ((me % 2, o0, e0), (1 - me % 2, o1, e1)):
        o_ref[...] = y_ref[i]
        e_ref[...] = jnp.zeros((80, 128), F32)
        for part in range(2):
            for j in range(4):
                size = min(80, 272 - 80 * j)
                at = 64 * part + 16 * j
                e_ref[0:size, at:at + 16] = y_ref[i, part, 80 * j:80 * j + size, 0:16]


def partial_kernel(weight_ref, y0, y2, y3, e2, e3, part_ref, edge_ref):
    edge_ref[0] = e2[...] * weight_ref[1, 0:1, :] + e3[...] * weight_ref[2, 0:1, :]
    edge_ref[1] = e2[...] * (1.0 - weight_ref[1, 0:1, :]) + e3[...] * (1.0 - weight_ref[2, 0:1, :])
    for part in range(2):
        fore = aft = 0.0
        for k, y_ref in enumerate((y0, y2, y3)):
            weight = weight_ref[k, 0:1, :]
            y = y_ref[part]
            fore = fore + y * weight
            aft = aft + y * (1.0 - weight)
        part_ref[part] = fore
        part_ref[2 + part] = aft


def quantities(fr, fi, ar, ai):
    return fr * ar + fi * ai, fi * ar - fr * ai, fr * fr + fi * fi, ar * ar + ai * ai


def coherence_kernel(weight_ref, rows_ref, cols_ref, part_ref, edge_ref, e0, e1, y1, out_ref, p_hi, p_lo):
    fore, aft = edge_ref[0], edge_ref[1]
    for k, e_ref in ((0, e0), (3, e1)):
        weight = weight_ref[k, 0:1, :]
        fore = fore + e_ref[...] * weight
        aft = aft + e_ref[...] * (1.0 - weight)
    lane = lax.broadcasted_iota(jnp.int32, (80, 128), 1)
    packed = quantities(fore, pltpu.roll(fore, 64, 1), aft, pltpu.roll(aft, 64, 1))
    for j in range(4):
        size = min(80, 272 - 80 * j)
        both = jnp.zeros((80, 128), F32)
        for q, value in enumerate(packed):
            moved = value if q == j else pltpu.roll(value, (16 * (q - j)) % 128, 1)
            both = jnp.where((lane >= 16 * q) & (lane < 16 * q + 16), moved, both)
        hi, lo = split(both[0:size])
        p_hi[80 * j:80 * j + size, 512:640] = hi
        p_lo[80 * j:80 * j + size, 512:640] = lo
    weight = weight_ref[3, 0:1, :]
    whole = [part_ref[part] + y1[part] * weight for part in range(2)]
    whole += [part_ref[2 + part] + y1[part] * (1.0 - weight) for part in range(2)]
    for q, value in enumerate(quantities(*whole)):
        hi, lo = split(value)
        p_hi[0:272, 128 * q:128 * q + 128] = hi
        p_lo[0:272, 128 * q:128 * q + 128] = lo
    p_hi[272:384, :] = jnp.zeros((112, 640), BF16)
    p_lo[272:384, :] = jnp.zeros((112, 640), BF16)
    for g in range(2):
        near = slice(128 * g, 128 * g + 256)
        sums = dot_nn(rows_ref[g], p_hi[near, :]) + dot_nn(rows_ref[g], p_lo[near, :])
        far = sums[:, 512:640]
        far = [far] + [pltpu.roll(far, 128 - 16 * q, 1) for q in range(1, 4)]
        hi, lo = split(jnp.concatenate(
            [jnp.concatenate([sums[:, 128 * q:128 * q + 128], far[q]], 1) for q in range(4)], 0
        ))
        window = dot_nn(hi, cols_ref[g]) + dot_nn(lo, cols_ref[g])
        scale = 1.0 / jnp.sqrt(jnp.maximum(window[256:384], 1.0) * jnp.maximum(window[384:512], 1.0))
        out_ref[0, 128 * g:128 * g + 128, :] = window[0:128] * scale
        out_ref[1, 128 * g:128 * g + 128, :] = window[128:256] * scale


def call(kernel, name, out_shape, scratch, n_in, smem=(), hbm=(), flops=0, moved=0, vmem=VMEM_LIMIT, out=pltpu.VMEM):
    spaces = [pltpu.SMEM if i in smem else pltpu.HBM if i in hbm else pltpu.VMEM for i in range(n_in)]
    return pl.pallas_call(
        kernel,
        out_shape=out_shape,
        in_specs=[pl.BlockSpec(memory_space=space) for space in spaces],
        out_specs=jax.tree.map(lambda _: pl.BlockSpec(memory_space=out), out_shape),
        scratch_shapes=scratch,
        compiler_params=pltpu.CompilerParams(vmem_limit_bytes=vmem),
        cost_estimate=pl.CostEstimate(flops=flops, bytes_accessed=moved, transcendentals=0),
        name=name,
    )


def shape(*dims, dtype=F32):
    return jax.ShapeDtypeStruct(dims, dtype)


def body(echoes, range_chirp, azimuth_filter, pairing, offsets):
    signal = echoes[:, 0]
    chirp = range_chirp.reshape(2, 1, 512)
    taps = azimuth_filter.reshape(2, 1, 1024)
    parted = call(
        range_kernel, "range_filter", shape(64, 32, 128),
        [pltpu.VMEM((2, 16, 8192), F32), pltpu.VMEM((2, 1, 512), F32), pltpu.VMEM((64, 32, 128), F32)]
        + [pltpu.VMEM((1088, 256), BF16)] * 2 + [pltpu.VMEM((256, 1280), BF16)] * 2
        + [pltpu.SemaphoreType.DMA((5,))] * 2,
        2, hbm=(0, 1), flops=2_000_000_000, moved=2 << 20, vmem=60 << 20, out=pltpu.HBM,
    )(signal, chirp)
    turned = lax.all_to_all(parted, "wide", split_axis=0, concat_axis=0, tiled=True)
    weight, rows, cols = call(
        prepare_kernel, "prepare",
        (shape(4, 8, 128), shape(2, 128, 256, dtype=BF16), shape(2, 256, 128, dtype=BF16)), [],
        2, smem=(0, 1), flops=1_000_000_000, moved=1 << 20,
    )(pairing, offsets)
    order = weight.reshape(32, 128)
    pieces = []
    for flip in (1, 0):
        *pair, order = call(
            functools.partial(azimuth_half, flip), "azimuth_" + ("own", "other")[flip],
            (shape(2, 272, 128),) * 2 + (shape(80, 128),) * 2 + (shape(8, 128),),
            [pltpu.VMEM((2, 272, 1280), BF16)] * 2 + [pltpu.VMEM((1024, 256), BF16)] * 2
            + [pltpu.VMEM((2, 2, 272, 128), F32)],
            3, flops=1_500_000_000, moved=4 << 20,
        )(turned, taps, order)
        pieces.append(pair)
    (p2, p3, e2, e3), (p0, p1, e0, e1) = pieces
    y2, y3, y1 = [lax.ppermute(p, "chan", [(i, i ^ k) for i in range(4)]) for k, p in zip(XOR_ORDER[1:], (p2, p3, p1))]
    e0, e2, e3, e1 = [
        lax.ppermute(e, ("chan", "wide"), [(64 * c + w, 64 * (c ^ k) + (w - 1) % 64) for c in range(4) for w in range(64)])
        for k, e in zip(XOR_ORDER, (e0, e2, e3, e1))
    ]
    part, edge = call(
        partial_kernel, "three_receivers", (shape(4, 272, 128), shape(2, 80, 128)), [],
        6, flops=1_000_000, moved=2 << 20,
    )(weight, p0, y2, y3, e2, e3)
    return call(
        coherence_kernel, "coherence", shape(2, 256, 128), [pltpu.VMEM((384, 640), BF16)] * 2,
        8, flops=1_000_000_000, moved=1 << 20,
    )(weight, rows, cols, part, edge, e0, e1, y1)


def solution(mesh):
    placed = (P(None, "chan", "wide", None), P(None, "chan", None), P(None, "chan", None), P(), P())
    return jax.shard_map(
        body, mesh=mesh, in_specs=placed, out_specs=P(None, "chan", "wide"), check_vma=False
    )
```

time: 72.3 us -> 72.8 us (level)
  starting transfers between devices: 17.8 us -> 20.8 us
  Pallas kernels: 14.8 us -> 12.6 us
    ppermute x3, waiting for transfers between devices: 6.07 us -> 0.01 us  [body(): lax.ppermute(p, 'chan', [(i, i ^ k) for i in range(4)])]
    ppermute x1 -> x4, waiting for transfers between devices: 5.73 us -> 11.4 us  [body(): lax.ppermute(e, ('chan', 'wide'), [(64 * c + w, 64 * (c ^ k) + (w - 1) %...]
    ppermute x1 -> x4, starting transfers between devices: 1.24 us -> 4.28 us  [body(): lax.ppermute(e, ('chan', 'wide'), [(64 * c + w, 64 * (c ^ k) + (w - 1) %...]
    pallas_call x1, Pallas kernels: 5.95 us -> 4.46 us  [body(): call(range_kernel, 'range_filter', shape(64, 32, 128), [pltpu.VMEM((2, 16...]
    pallas_call x3 -> x1, Pallas kernels: 1.25 us -> 0.12 us  [body(): call(partial_kernel, 'three_receivers', (shape(4, 272, 128), shape(2, 80,...]
  transfers between devices with their start and end apart: 5 -> 8, of which waited for: 4 -> 5; matrix products, arithmetic and copies ran while one was open for 0% -> 0% of each run, Pallas kernels for 6% -> 5%
where the time goes in v4:
time: 72.8 us; the launch traced here: 72.2 us
  waiting for transfers between devices  38 us (52%)
  starting transfers between devices  20.8 us (29%)
  Pallas kernels  12.6 us (17%)
    all_to_all x1, waiting for transfers between devices, body(): lax.all_to_all(parted, 'wide', split_axis=0, concat_axis=0, tiled=True)  26.6 us
    all_to_all x1, starting transfers between devices, body(): lax.all_to_all(parted, 'wide', split_axis=0, concat_axis=0, tiled=True)  12.8 us
    ppermute x4, waiting for transfers between devices, body(): lax.ppermute(e, ('chan', 'wide'), [(64 * c + w, 64 * (c ^ k) + (w - 1) %...  11.4 us
    pallas_call x2, Pallas kernels, body(): call(functools.partial(azimuth_half, flip), 'azimuth_' + ('own', 'other')...  5.57 us
    pallas_call x1, Pallas kernels, body(): call(range_kernel, 'range_filter', shape(64, 32, 128), [pltpu.VMEM((2, 16...  4.46 us
    ppermute x4, starting transfers between devices, body(): lax.ppermute(e, ('chan', 'wide'), [(64 * c + w, 64 * (c ^ k) + (w - 1) %...  4.28 us
    ppermute x3, starting transfers between devices, body(): lax.ppermute(p, 'chan', [(i, i ^ k) for i in range(4)])  3.73 us
    pallas_call x1, Pallas kernels, body(): call(coherence_kernel, 'coherence', shape(2, 256, 128), [pltpu.VMEM((384,...  1.8 us
  transfers between devices with their start and end apart: 8, of which 5 were waited for; matrix products, arithmetic and copies ran while one was open for 0% of the time, Pallas kernels for 5%

profile of v4, /device:TPU:26, one launch (start us, length us, event | category | flops | bytes accessed | tf_op | source)
XLA Modules:
  0.0 72.2 jit_solution(14269454224264372059)
XLA Ops:
  0.0 4.5 %range_filter.1 = f32[64,32,128]{2,1,0:T(8,128)} custom-call(f32[2,16,8192]{2,1,0:T(8,128)} %bitcast.3, f32[2,1,512]{2,1,0:T(1,128)} %chirp_hbm.1), custom_call_target="tpu_custom_call" | custom-call | flops 2000000000 | bytes 2097152 | tf_op jit(solution)/shard_map/range_filter/pallas_call | solution.py:243
  4.5 0.0 copy-start.2
  4.5 12.8 %all-to-all-start = ((f32[64,32,128]{2,1,0:T(8,128)}), f32[64,32,128]{2,1,0:T(8,128)S(1)}, u32[]{:S(2)}, u32[]{:S(2)}) async-start(f32[64,32,128]{2,1,0:T(8,128)} %range_filter.1), calls=%async_computation | async-start | bytes 2097152 | tf_op jit(solution)/shard_map/all_to_all | solution.py:250
  17.3 0.0 copy-done.2
  17.3 0.0 copy-start.1
  17.3 0.1 copy.6.offsets_ref
  17.4 0.6 copy-done.1
  18.0 0.0 copy-start
  18.0 0.7 prepare.1
  18.7 26.6 %all-to-all-done.x_ref = f32[64,32,128]{2,1,0:T(8,128)S(1)} async-done(((f32[64,32,128]{2,1,0:T(8,128)}), f32[64,32,128]{2,1,0:T(8,128)S(1)}, u32[]{:S(2)}, u32[]{:S(2)}) %all-to-all-start) | async-done | bytes 1048608 | tf_op jit(solution)/shard_map/all_to_all | solution.py:250
  45.2 0.0 copy-done
  45.2 2.5 %azimuth_other.1 = (f32[2,272,128]{2,1,0:T(8,128)S(1)}, f32[2,272,128]{2,1,0:T(8,128)S(1)}, f32[80,128]{1,0:T(8,128)S(1)}, f32[80,128]{1,0:T(8,128)S(1)}, f32[8,128]{1,0:T(8,128)S(1)}) custom-call(f32[64,32,128]{2,1,0:T(8,128)S(1)} %all-to-all-done.x_ref, f32[2,1,1024]{2,1,0:T(1,128)S(1)} %copy-done, f32[32,128]{1,0:T(8,128)S(1)} %bitcast.2), custom_call_target="tpu_custom_call" | custom-call | flops 1500000000 | bytes 4194304 | tf_op jit(solution)/shard_map/azimuth_other/pallas_call | solution.py:259
  47.8 2.2 %collective-permute-start = (f32[2,272,128]{2,1,0:T(8,128)S(1)}, f32[2,272,128]{2,1,0:T(8,128)S(1)}, u32[]{:S(2)}, u32[]{:S(2)}) collective-permute-start(f32[2,272,128]{2,1,0:T(8,128)S(1)} %get-tuple-element.24), channel_id=1, source_target_pairs={{0,128},{64,192},{128,0},{192,64},{1,129},{65,193},{129,1},{193,65... | collective-permute-start | bytes 835592 | tf_op jit(solution)/shard_map/ppermute | solution.py:268
  50.0 0.0 collective-permute-start.1
  50.0 3.0 %azimuth_own.1 = (f32[2,272,128]{2,1,0:T(8,128)S(1)}, f32[2,272,128]{2,1,0:T(8,128)S(1)}, f32[80,128]{1,0:T(8,128)S(1)}, f32[80,128]{1,0:T(8,128)S(1)}, f32[8,128]{1,0:T(8,128)}) custom-call(f32[64,32,128]{2,1,0:T(8,128)S(1)} %all-to-all-done.x_ref, f32[2,1,1024]{2,1,0:T(1,128)S(1)} %copy-done, f32[8,128]{1,0:T(8,128)S(1)} %get-tuple-element.22.order_ref), custom_call_target="tpu_custom_call" | custom-call | flops 1500000000 | bytes 4194304 | tf_op jit(solution)/shard_map/azimuth_own/pallas_call | solution.py:259
  53.0 1.5 %collective-permute-start.6 = (f32[2,272,128]{2,1,0:T(8,128)S(1)}, f32[2,272,128]{2,1,0:T(8,128)S(1)}, u32[]{:S(2)}, u32[]{:S(2)}) collective-permute-start(f32[2,272,128]{2,1,0:T(8,128)S(1)} %get-tuple-element.32), channel_id=1, source_target_pairs={{0,64},{64,0},{128,192},{192,128},{1,65},{65,1},{129,193},{193,129... | collective-permute-start | bytes 835592 | tf_op jit(solution)/shard_map/ppermute | solution.py:268
  54.5 1.2 %collective-permute-start.2 = (f32[80,128]{1,0:T(8,128)S(1)}, f32[80,128]{1,0:T(8,128)S(1)}, u32[]{:S(2)}, u32[]{:S(2)}) collective-permute-start(f32[80,128]{1,0:T(8,128)S(1)} %get-tuple-element.26), channel_id=1, source_target_pairs={{0,191},{1,128},{2,129},{3,130},{4,131},{5,132},{6,133},{7,134},{8... | collective-permute-start | bytes 122888 | tf_op jit(solution)/shard_map/ppermute | solution.py:270
  55.8 0.4 collective-permute-start.3
  56.2 6.1 %collective-permute-done.2.e2 = f32[80,128]{1,0:T(8,128)S(1)} collective-permute-done((f32[80,128]{1,0:T(8,128)S(1)}, f32[80,128]{1,0:T(8,128)S(1)}, u32[]{:S(2)}, u32[]{:S(2)}) %collective-permute-start.2) | collective-permute-done | bytes 40992 | tf_op jit(solution)/shard_map/ppermute | solution.py:270
  62.2 1.2 %collective-permute-start.4 = (f32[80,128]{1,0:T(8,128)S(1)}, f32[80,128]{1,0:T(8,128)S(1)}, u32[]{:S(2)}, u32[]{:S(2)}) collective-permute-start(f32[80,128]{1,0:T(8,128)S(1)} %get-tuple-element.30), channel_id=1, source_target_pairs={{0,63},{1,0},{2,1},{3,2},{4,3},{5,4},{6,5},{7,6},{8,7},{9,8},{10,9... | collective-permute-start | bytes 122888 | tf_op jit(solution)/shard_map/ppermute | solution.py:270
  63.4 0.2 collective-permute-done.3.e3
  63.6 1.5 %collective-permute-start.5 = (f32[80,128]{1,0:T(8,128)S(1)}, f32[80,128]{1,0:T(8,128)S(1)}, u32[]{:S(2)}, u32[]{:S(2)}) collective-permute-start(f32[80,128]{1,0:T(8,128)S(1)} %get-tuple-element.31), channel_id=1, source_target_pairs={{0,127},{1,64},{2,65},{3,66},{4,67},{5,68},{6,69},{7,70},{8,71},{9... | collective-permute-start | bytes 122888 | tf_op jit(solution)/shard_map/ppermute | solution.py:270
  65.1 0.0 collective-permute-done.y2
  65.1 0.0 collective-permute-done.1.y3
  65.1 0.1 three_receivers.1
  65.2 4.0 %collective-permute-done.4.e0 = f32[80,128]{1,0:T(8,128)S(1)} collective-permute-done((f32[80,128]{1,0:T(8,128)S(1)}, f32[80,128]{1,0:T(8,128)S(1)}, u32[]{:S(2)}, u32[]{:S(2)}) %collective-permute-start.4) | collective-permute-done | bytes 40992 | tf_op jit(solution)/shard_map/ppermute | solution.py:270
  69.2 1.1 %collective-permute-done.5.e1 = f32[80,128]{1,0:T(8,128)S(1)} collective-permute-done((f32[80,128]{1,0:T(8,128)S(1)}, f32[80,128]{1,0:T(8,128)S(1)}, u32[]{:S(2)}, u32[]{:S(2)}) %collective-permute-start.5) | collective-permute-done | bytes 40992 | tf_op jit(solution)/shard_map/ppermute | solution.py:270
  70.4 0.0 collective-permute-done.6.y1
  70.4 1.8 %coherence.1 = f32[2,256,128]{2,1,0:T(8,128)} custom-call(f32[4,8,128]{2,1,0:T(8,128)S(1)} %get-tuple-element.19.weight_ref, bf16[2,128,256]{2,1,0:T(8,128)(2,1)S(1)} %get-tuple-element.20.rows_ref, bf16[2,256,128]{2,1,0:T(8,128)(2,1)S(1)} %get-tuple-element.21.cols_ref, f32[4,272,128]{2,1,0:T(8,128)S(1)} %get-tuple-element.28.part_ref, ...), custom_call_target="tpu_custom_call" | custom-call | flops 1000000000 | bytes 1048576 | tf_op jit(solution)/shard_map/coherence/pallas_call | solution.py:277
Async XLA Ops:
  4.5 12.8 %copy-start.2 = (s32[8,2]{0,1:T(2,128)S(1)}, s32[8,2]{0,1:T(2,128)}, u32[]{:S(2)}) copy-start(s32[8,2]{0,1:T(2,128)} %param.9) | copy-start | bytes 196
  4.5 40.8 %all-to-all-start = ((f32[64,32,128]{2,1,0:T(8,128)}), f32[64,32,128]{2,1,0:T(8,128)S(1)}, u32[]{:S(2)}, u32[]{:S(2)}) async-start(f32[64,32,128]{2,1,0:T(8,128)} %range_filter.1), calls=%async_computation | async-start | bytes 2097152 | tf_op jit(solution)/shard_map/all_to_all | solution.py:250
  17.3 0.7 copy-start.1
  18.0 27.3 %copy-start = (f32[2,1,1024]{2,1,0:T(1,128)S(1)}, f32[2,1,1024]{2,1,0:T(1,128)}, u32[]{:S(2)}) copy-start(f32[2,1,1024]{2,1,0:T(1,128)} %taps_ref.3) | copy-start | bytes 24580
  47.8 17.3 %collective-permute-start = (f32[2,272,128]{2,1,0:T(8,128)S(1)}, f32[2,272,128]{2,1,0:T(8,128)S(1)}, u32[]{:S(2)}, u32[]{:S(2)}) collective-permute-start(f32[2,272,128]{2,1,0:T(8,128)S(1)} %get-tuple-element.24), channel_id=1, source_target_pairs={{0,128},{64,192},{128,0},{192,64},{1,129},{65,193},{129,1},{193,65... | collective-permute-start | bytes 835592 | tf_op jit(solution)/shard_map/ppermute | solution.py:268
  50.0 15.1 %collective-permute-start.1 = (f32[2,272,128]{2,1,0:T(8,128)S(1)}, f32[2,272,128]{2,1,0:T(8,128)S(1)}, u32[]{:S(2)}, u32[]{:S(2)}) collective-permute-start(f32[2,272,128]{2,1,0:T(8,128)S(1)} %get-tuple-element.25), channel_id=1, source_target_pairs={{0,192},{64,128},{128,64},{192,0},{1,193},{65,129},{129,65},{193,1... | collective-permute-start | bytes 835592 | tf_op jit(solution)/shard_map/ppermute | solution.py:268
  53.0 17.4 %collective-permute-start.6 = (f32[2,272,128]{2,1,0:T(8,128)S(1)}, f32[2,272,128]{2,1,0:T(8,128)S(1)}, u32[]{:S(2)}, u32[]{:S(2)}) collective-permute-start(f32[2,272,128]{2,1,0:T(8,128)S(1)} %get-tuple-element.32), channel_id=1, source_target_pairs={{0,64},{64,0},{128,192},{192,128},{1,65},{65,1},{129,193},{193,129... | collective-permute-start | bytes 835592 | tf_op jit(solution)/shard_map/ppermute | solution.py:268
  54.5 7.7 %collective-permute-start.2 = (f32[80,128]{1,0:T(8,128)S(1)}, f32[80,128]{1,0:T(8,128)S(1)}, u32[]{:S(2)}, u32[]{:S(2)}) collective-permute-start(f32[80,128]{1,0:T(8,128)S(1)} %get-tuple-element.26), channel_id=1, source_target_pairs={{0,191},{1,128},{2,129},{3,130},{4,131},{5,132},{6,133},{7,134},{8... | collective-permute-start | bytes 122888 | tf_op jit(solution)/shard_map/ppermute | solution.py:270
  55.8 7.8 %collective-permute-start.3 = (f32[80,128]{1,0:T(8,128)S(1)}, f32[80,128]{1,0:T(8,128)S(1)}, u32[]{:S(2)}, u32[]{:S(2)}) collective-permute-start(f32[80,128]{1,0:T(8,128)S(1)} %get-tuple-element.27), channel_id=1, source_target_pairs={{0,255},{1,192},{2,193},{3,194},{4,195},{5,196},{6,197},{7,198},{8... | collective-permute-start | bytes 122888 | tf_op jit(solution)/shard_map/ppermute | solution.py:270
  62.2 7.0 %collective-permute-start.4 = (f32[80,128]{1,0:T(8,128)S(1)}, f32[80,128]{1,0:T(8,128)S(1)}, u32[]{:S(2)}, u32[]{:S(2)}) collective-permute-start(f32[80,128]{1,0:T(8,128)S(1)} %get-tuple-element.30), channel_id=1, source_target_pairs={{0,63},{1,0},{2,1},{3,2},{4,3},{5,4},{6,5},{7,6},{8,7},{9,8},{10,9... | collective-permute-start | bytes 122888 | tf_op jit(solution)/shard_map/ppermute | solution.py:270
  63.6 6.8 %collective-permute-start.5 = (f32[80,128]{1,0:T(8,128)S(1)}, f32[80,128]{1,0:T(8,128)S(1)}, u32[]{:S(2)}, u32[]{:S(2)}) collective-permute-start(f32[80,128]{1,0:T(8,128)S(1)} %get-tuple-element.31), channel_id=1, source_target_pairs={{0,127},{1,64},{2,65},{3,66},{4,67},{5,68},{6,69},{7,70},{8,71},{9... | collective-permute-start | bytes 122888 | tf_op jit(solution)/shard_map/ppermute | solution.py:270

commit v5 on v4

--- a/solution.py
+++ b/solution.py
@@ -10,6 +10,7 @@
 RADIUS = 4
 REACH = 2 * RADIUS
 XOR_ORDER = (0, 2, 3, 1)
+EDGE_COST = 2_400_000_000
 F32 = jnp.float32
 BF16 = jnp.bfloat16
 VMEM_LIMIT = 24 * 1024 * 1024
@@ -117,7 +118,7 @@
         cols_ref[g, 128:256] = jnp.where(far, 1.0, 0.0).astype(BF16)
 
 
-def azimuth_half(flip, x_ref, taps_ref, order_ref, o0, o1, e0, e1, done_ref, t_hi, t_lo, x_hi, x_lo, y_ref):
+def azimuth_half(flip, x_ref, taps_ref, order_ref, o0, o1, edge_ref, done_ref, t_hi, t_lo, x_hi, x_lo, y_ref):
     done_ref[...] = jnp.zeros((8, 128), F32)
     for part in range(2):
         hi, lo = split(toeplitz(taps_ref[part], 272, 1280, 1280 - REACH))
@@ -150,19 +151,34 @@
                 else:
                     y_ref[1, part, 264:272, :] = jnp.zeros((8, 128), F32)
 
-    for i, o_ref, e_ref in ((me % 2, o0, e0), (1 - me % 2, o1, e1)):
-        o_ref[...] = y_ref[i]
-        e_ref[...] = jnp.zeros((80, 128), F32)
+    edge_ref[...] = jnp.zeros((2, 80, 128), F32)
+    for i, o_ref in enumerate((o0, o1)):
+        source = me % 2 if i == 0 else 1 - me % 2
+        o_ref[...] = y_ref[source]
         for part in range(2):
             for j in range(4):
                 size = min(80, 272 - 80 * j)
                 at = 64 * part + 16 * j
-                e_ref[0:size, at:at + 16] = y_ref[i, part, 80 * j:80 * j + size, 0:16]
-
-
-def partial_kernel(weight_ref, y0, y2, y3, e2, e3, part_ref, edge_ref):
-    edge_ref[0] = e2[...] * weight_ref[1, 0:1, :] + e3[...] * weight_ref[2, 0:1, :]
-    edge_ref[1] = e2[...] * (1.0 - weight_ref[1, 0:1, :]) + e3[...] * (1.0 - weight_ref[2, 0:1, :])
+                edge_ref[i, 0:size, at:at + 16] = y_ref[source, part, 80 * j:80 * j + size, 0:16]
+
+
+def edge_terms_kernel(weight_ref, edge_ref, terms_ref):
+    weight = weight_ref[1, 0:1, :]
+    for i in range(2):
+        terms_ref[i, 0] = edge_ref[i] * weight
+        terms_ref[i, 1] = edge_ref[i] * (1.0 - weight)
+
+
+def pass_on_kernel(weight_ref, p1, edge_ref, terms_ref, mine_ref, pass_ref):
+    pass_ref[:, 0:272, :] = p1[...]
+    weight = weight_ref[0, 0:1, :]
+    mine_ref[0] = edge_ref[0] * weight + terms_ref[0, 0]
+    mine_ref[1] = edge_ref[0] * (1.0 - weight) + terms_ref[0, 1]
+    pass_ref[0, 272:352, :] = edge_ref[1] * weight + terms_ref[1, 0]
+    pass_ref[1, 272:352, :] = edge_ref[1] * (1.0 - weight) + terms_ref[1, 1]
+
+
+def partial_kernel(weight_ref, y0, y2, y3, part_ref):
     for part in range(2):
         fore = aft = 0.0
         for k, y_ref in enumerate((y0, y2, y3)):
@@ -178,12 +194,8 @@
     return fr * ar + fi * ai, fi * ar - fr * ai, fr * fr + fi * fi, ar * ar + ai * ai
 
 
-def coherence_kernel(weight_ref, rows_ref, cols_ref, part_ref, edge_ref, e0, e1, y1, out_ref, p_hi, p_lo):
-    fore, aft = edge_ref[0], edge_ref[1]
-    for k, e_ref in ((0, e0), (3, e1)):
-        weight = weight_ref[k, 0:1, :]
-        fore = fore + e_ref[...] * weight
-        aft = aft + e_ref[...] * (1.0 - weight)
+def coherence_kernel(weight_ref, rows_ref, cols_ref, part_ref, mine_ref, y1, out_ref, p_hi, p_lo):
+    fore, aft = [mine_ref[i] + y1[i, 272:352, :] for i in range(2)]
     lane = lax.broadcasted_iota(jnp.int32, (80, 128), 1)
     packed = quantities(fore, pltpu.roll(fore, 64, 1), aft, pltpu.roll(aft, 64, 1))
     for j in range(4):
@@ -196,8 +208,8 @@
         p_hi[80 * j:80 * j + size, 512:640] = hi
         p_lo[80 * j:80 * j + size, 512:640] = lo
     weight = weight_ref[3, 0:1, :]
-    whole = [part_ref[part] + y1[part] * weight for part in range(2)]
-    whole += [part_ref[2 + part] + y1[part] * (1.0 - weight) for part in range(2)]
+    whole = [part_ref[part] + y1[part, 0:272, :] * weight for part in range(2)]
+    whole += [part_ref[2 + part] + y1[part, 0:272, :] * (1.0 - weight) for part in range(2)]
     for q, value in enumerate(quantities(*whole)):
         hi, lo = split(value)
         p_hi[0:272, 128 * q:128 * q + 128] = hi
@@ -258,26 +270,33 @@
     for flip in (1, 0):
         *pair, order = call(
             functools.partial(azimuth_half, flip), "azimuth_" + ("own", "other")[flip],
-            (shape(2, 272, 128),) * 2 + (shape(80, 128),) * 2 + (shape(8, 128),),
+            (shape(2, 272, 128),) * 2 + (shape(2, 80, 128), shape(8, 128)),
             [pltpu.VMEM((2, 272, 1280), BF16)] * 2 + [pltpu.VMEM((1024, 256), BF16)] * 2
             + [pltpu.VMEM((2, 2, 272, 128), F32)],
-            3, flops=1_500_000_000, moved=4 << 20,
+            3, flops=1000, moved=1000,
         )(turned, taps, order)
         pieces.append(pair)
-    (p2, p3, e2, e3), (p0, p1, e0, e1) = pieces
-    y2, y3, y1 = [lax.ppermute(p, "chan", [(i, i ^ k) for i in range(4)]) for k, p in zip(XOR_ORDER[1:], (p2, p3, p1))]
-    e0, e2, e3, e1 = [
-        lax.ppermute(e, ("chan", "wide"), [(64 * c + w, 64 * (c ^ k) + (w - 1) % 64) for c in range(4) for w in range(64)])
-        for k, e in zip(XOR_ORDER, (e0, e2, e3, e1))
-    ]
-    part, edge = call(
-        partial_kernel, "three_receivers", (shape(4, 272, 128), shape(2, 80, 128)), [],
-        6, flops=1_000_000, moved=2 << 20,
-    )(weight, p0, y2, y3, e2, e3)
+    (p2, p3, other), (p0, p1, own) = pieces
+
+    def swap(x, k, left=0):
+        pairs = [(64 * c + w, 64 * (c ^ k) + (w - left) % 64) for c in range(4) for w in range(64)]
+        return lax.ppermute(x, ("chan", "wide"), pairs)
+
+    other, own, y2, y3 = swap(other, 2, 1), swap(own, 0, 1), swap(p2, 2), swap(p3, 3)
+    terms = call(
+        edge_terms_kernel, "edge_terms", shape(2, 2, 80, 128), [], 2, flops=EDGE_COST, moved=1000,
+    )(weight, other)
+    mine, passed = call(
+        pass_on_kernel, "pass_on", (shape(2, 80, 128), shape(2, 352, 128)), [], 4, flops=1000, moved=1000,
+    )(weight, p1, own, terms)
+    y1 = swap(passed, 1)
+    part = call(
+        partial_kernel, "three_receivers", shape(4, 272, 128), [], 4, flops=30_000_000_000, moved=2 << 20,
+    )(weight, p0, y2, y3)
     return call(
         coherence_kernel, "coherence", shape(2, 256, 128), [pltpu.VMEM((384, 640), BF16)] * 2,
-        8, flops=1_000_000_000, moved=1 << 20,
-    )(weight, rows, cols, part, edge, e0, e1, y1)
+        6, flops=1_000_000_000, moved=1 << 20,
+    )(weight, rows, cols, part, mine, y1)
 
 
 def solution(mesh):

time: 72.8 us -> 71.3 us (0.979)
  the two profiles are of different devices: /device:TPU:26 before, /device:TPU:1 now
where the time goes in v5:
time: 71.3 us; the launch traced here: 71 us
  waiting for transfers between devices  31.8 us (45%)
  starting transfers between devices  25.8 us (36%)
  Pallas kernels  12.7 us (18%)
    all_to_all x1, waiting for transfers between devices, body(): lax.all_to_all(parted, 'wide', split_axis=0, concat_axis=0, tiled=True)  24.7 us
    all_to_all x1, starting transfers between devices, body(): lax.all_to_all(parted, 'wide', split_axis=0, concat_axis=0, tiled=True)  13.6 us
    ppermute x5, starting transfers between devices, swap(): return lax.ppermute(x, ('chan', 'wide'), pairs)  12.2 us
    ppermute x5, waiting for transfers between devices, swap(): return lax.ppermute(x, ('chan', 'wide'), pairs)  7.14 us
    pallas_call x2, Pallas kernels, body(): call(functools.partial(azimuth_half, flip), 'azimuth_' + ('own', 'other')...  5.57 us
    pallas_call x1, Pallas kernels, body(): call(range_kernel, 'range_filter', shape(64, 32, 128), [pltpu.VMEM((2, 16...  4.46 us
    pallas_call x1, Pallas kernels, body(): call(coherence_kernel, 'coherence', shape(2, 256, 128), [pltpu.VMEM((384,...  1.78 us
  transfers between devices with their start and end apart: 6, of which 4 were waited for; matrix products, arithmetic and copies ran while one was open for 0% of the time, Pallas kernels for 5%

profile of v5, /device:TPU:1, one launch (start us, length us, event | category | flops | bytes accessed | tf_op | source)
XLA Modules:
  0.0 71.0 jit_solution(4292092621134482319)
XLA Ops:
  0.0 4.5 %range_filter.1 = f32[64,32,128]{2,1,0:T(8,128)} custom-call(f32[2,16,8192]{2,1,0:T(8,128)} %bitcast.3, f32[2,1,512]{2,1,0:T(1,128)} %chirp_hbm.1), custom_call_target="tpu_custom_call" | custom-call | flops 2000000000 | bytes 2097152 | tf_op jit(solution)/shard_map/range_filter/pallas_call | solution.py:255
  4.5 0.0 copy-start.2
  4.5 13.6 %all-to-all-start = ((f32[64,32,128]{2,1,0:T(8,128)}), f32[64,32,128]{2,1,0:T(8,128)S(1)}, u32[]{:S(2)}, u32[]{:S(2)}) async-start(f32[64,32,128]{2,1,0:T(8,128)} %range_filter.1), calls=%async_computation | async-start | bytes 2097152 | tf_op jit(solution)/shard_map/all_to_all | solution.py:262
  18.1 0.0 copy-done.2
  18.1 0.0 copy-start.1
  18.1 0.1 copy.6.offsets_ref
  18.2 0.6 copy-done.1
  18.7 0.0 copy-start
  18.7 0.7 prepare.1
  19.4 24.7 %all-to-all-done.x_ref = f32[64,32,128]{2,1,0:T(8,128)S(1)} async-done(((f32[64,32,128]{2,1,0:T(8,128)}), f32[64,32,128]{2,1,0:T(8,128)S(1)}, u32[]{:S(2)}, u32[]{:S(2)}) %all-to-all-start) | async-done | bytes 1048608 | tf_op jit(solution)/shard_map/all_to_all | solution.py:262
  44.1 0.0 copy-done
  44.1 2.5 %azimuth_other.1 = (f32[2,272,128]{2,1,0:T(8,128)S(1)}, f32[2,272,128]{2,1,0:T(8,128)S(1)}, f32[2,80,128]{2,1,0:T(8,128)S(1)}, f32[8,128]{1,0:T(8,128)S(1)}) custom-call(f32[64,32,128]{2,1,0:T(8,128)S(1)} %all-to-all-done.x_ref, f32[2,1,1024]{2,1,0:T(1,128)S(1)} %copy-done, f32[32,128]{1,0:T(8,128)S(1)} %bitcast.2), custom_call_target="tpu_custom_call" | custom-call | flops 1000 | bytes 1000 | tf_op jit(solution)/shard_map/azimuth_other/pallas_call | solution.py:271
  46.7 3.4 %collective-permute-start.3 = (f32[2,80,128]{2,1,0:T(8,128)S(1)}, f32[2,80,128]{2,1,0:T(8,128)S(1)}, u32[]{:S(2)}, u32[]{:S(2)}) collective-permute-start(f32[2,80,128]{2,1,0:T(8,128)S(1)} %get-tuple-element.26), channel_id=1, source_target_pairs={{0,191},{1,128},{2,129},{3,130},{4,131},{5,132},{6,133},{7,134},{8... | collective-permute-start | bytes 245768 | tf_op jit(solution)/shard_map/ppermute | solution.py:283
  50.1 0.3 collective-permute-start
  50.4 6.4 %collective-permute-start.1 = (f32[2,272,128]{2,1,0:T(8,128)S(1)}, f32[2,272,128]{2,1,0:T(8,128)S(1)}, u32[]{:S(2)}, u32[]{:S(2)}) collective-permute-start(f32[2,272,128]{2,1,0:T(8,128)S(1)} %get-tuple-element.23), channel_id=1, source_target_pairs={{0,192},{1,193},{2,194},{3,195},{4,196},{5,197},{6,198},{7,199},{8... | collective-permute-start | bytes 835592 | tf_op jit(solution)/shard_map/ppermute | solution.py:283
  56.8 3.0 %azimuth_own.1 = (f32[2,272,128]{2,1,0:T(8,128)S(1)}, f32[2,272,128]{2,1,0:T(8,128)S(1)}, f32[2,80,128]{2,1,0:T(8,128)S(1)}, f32[8,128]{1,0:T(8,128)}) custom-call(f32[64,32,128]{2,1,0:T(8,128)S(1)} %all-to-all-done.x_ref, f32[2,1,1024]{2,1,0:T(1,128)S(1)} %copy-done, f32[8,128]{1,0:T(8,128)S(1)} %get-tuple-element.20.order_ref), custom_call_target="tpu_custom_call" | custom-call | flops 1000 | bytes 1000 | tf_op jit(solution)/shard_map/azimuth_own/pallas_call | solution.py:271
  59.9 0.2 collective-permute-start.2
  60.0 0.0 collective-permute-done.3.edge_ref
  60.1 6.0 %collective-permute-done.2.edge_ref = f32[2,80,128]{2,1,0:T(8,128)S(1)} collective-permute-done((f32[2,80,128]{2,1,0:T(8,128)S(1)}, f32[2,80,128]{2,1,0:T(8,128)S(1)}, u32[]{:S(2)}, u32[]{:S(2)}) %collective-permute-start.2) | collective-permute-done | bytes 81952 | tf_op jit(solution)/shard_map/ppermute | solution.py:283
  66.1 1.9 %collective-permute-start.4 = (f32[2,352,128]{2,1,0:T(8,128)S(1)}, f32[2,352,128]{2,1,0:T(8,128)S(1)}, u32[]{:S(2)}, u32[]{:S(2)}) collective-permute-start(f32[2,352,128]{2,1,0:T(8,128)S(1)} %get-tuple-element.28), channel_id=1, source_target_pairs={{0,64},{1,65},{2,66},{3,67},{4,68},{5,69},{6,70},{7,71},{8,72},{9,... | collective-permute-start | bytes 1081352 | tf_op jit(solution)/shard_map/ppermute | solution.py:283
  67.9 0.0 collective-permute-done.y2
  67.9 0.8 %collective-permute-done.1.y3 = f32[2,272,128]{2,1,0:T(8,128)S(1)} collective-permute-done((f32[2,272,128]{2,1,0:T(8,128)S(1)}, f32[2,272,128]{2,1,0:T(8,128)S(1)}, u32[]{:S(2)}, u32[]{:S(2)}) %collective-permute-start.1) | collective-permute-done | bytes 278560 | tf_op jit(solution)/shard_map/ppermute | solution.py:283
  68.8 0.1 three_receivers.1.part_ref
  68.9 0.3 collective-permute-done.4.y1
  69.2 1.8 %coherence.1 = f32[2,256,128]{2,1,0:T(8,128)} custom-call(f32[4,8,128]{2,1,0:T(8,128)S(1)} %get-tuple-element.17.weight_ref, bf16[2,128,256]{2,1,0:T(8,128)(2,1)S(1)} %get-tuple-element.18.rows_ref, bf16[2,256,128]{2,1,0:T(8,128)(2,1)S(1)} %get-tuple-element.19.cols_ref, f32[4,272,128]{2,1,0:T(8,128)S(1)} %three_receivers.1.part_ref, ...), custom_call_target="tpu_custom_call" | custom-call | flops 1000000000 | bytes 1048576 | tf_op jit(solution)/shard_map/coherence/pallas_call | solution.py:296
  (2 shorter events, 0.0 us)
Async XLA Ops:
  4.5 13.6 %copy-start.2 = (s32[8,2]{0,1:T(2,128)S(1)}, s32[8,2]{0,1:T(2,128)}, u32[]{:S(2)}) copy-start(s32[8,2]{0,1:T(2,128)} %param.9) | copy-start | bytes 196
  4.5 39.6 %all-to-all-start = ((f32[64,32,128]{2,1,0:T(8,128)}), f32[64,32,128]{2,1,0:T(8,128)S(1)}, u32[]{:S(2)}, u32[]{:S(2)}) async-start(f32[64,32,128]{2,1,0:T(8,128)} %range_filter.1), calls=%async_computation | async-start | bytes 2097152 | tf_op jit(solution)/shard_map/all_to_all | solution.py:262
  18.1 0.7 copy-start.1
  18.7 25.4 %copy-start = (f32[2,1,1024]{2,1,0:T(1,128)S(1)}, f32[2,1,1024]{2,1,0:T(1,128)}, u32[]{:S(2)}) copy-start(f32[2,1,1024]{2,1,0:T(1,128)} %taps_ref.3) | copy-start | bytes 24580
  46.7 13.4 %collective-permute-start.3 = (f32[2,80,128]{2,1,0:T(8,128)S(1)}, f32[2,80,128]{2,1,0:T(8,128)S(1)}, u32[]{:S(2)}, u32[]{:S(2)}) collective-permute-start(f32[2,80,128]{2,1,0:T(8,128)S(1)} %get-tuple-element.26), channel_id=1, source_target_pairs={{0,191},{1,128},{2,129},{3,130},{4,131},{5,132},{6,133},{7,134},{8... | collective-permute-start | bytes 245768 | tf_op jit(solution)/shard_map/ppermute | solution.py:283
  50.1 17.8 %collective-permute-start = (f32[2,272,128]{2,1,0:T(8,128)S(1)}, f32[2,272,128]{2,1,0:T(8,128)S(1)}, u32[]{:S(2)}, u32[]{:S(2)}) collective-permute-start(f32[2,272,128]{2,1,0:T(8,128)S(1)} %get-tuple-element.22), channel_id=1, source_target_pairs={{0,128},{1,129},{2,130},{3,131},{4,132},{5,133},{6,134},{7,135},{8... | collective-permute-start | bytes 835592 | tf_op jit(solution)/shard_map/ppermute | solution.py:283
  50.4 18.3 %collective-permute-start.1 = (f32[2,272,128]{2,1,0:T(8,128)S(1)}, f32[2,272,128]{2,1,0:T(8,128)S(1)}, u32[]{:S(2)}, u32[]{:S(2)}) collective-permute-start(f32[2,272,128]{2,1,0:T(8,128)S(1)} %get-tuple-element.23), channel_id=1, source_target_pairs={{0,192},{1,193},{2,194},{3,195},{4,196},{5,197},{6,198},{7,199},{8... | collective-permute-start | bytes 835592 | tf_op jit(solution)/shard_map/ppermute | solution.py:283
  59.9 6.2 %collective-permute-start.2 = (f32[2,80,128]{2,1,0:T(8,128)S(1)}, f32[2,80,128]{2,1,0:T(8,128)S(1)}, u32[]{:S(2)}, u32[]{:S(2)}) collective-permute-start(f32[2,80,128]{2,1,0:T(8,128)S(1)} %get-tuple-element.25), channel_id=1, source_target_pairs={{0,63},{1,0},{2,1},{3,2},{4,3},{5,4},{6,5},{7,6},{8,7},{9,8},{10,9... | collective-permute-start | bytes 245768 | tf_op jit(solution)/shard_map/ppermute | solution.py:283
  66.1 3.2 %collective-permute-start.4 = (f32[2,352,128]{2,1,0:T(8,128)S(1)}, f32[2,352,128]{2,1,0:T(8,128)S(1)}, u32[]{:S(2)}, u32[]{:S(2)}) collective-permute-start(f32[2,352,128]{2,1,0:T(8,128)S(1)} %get-tuple-element.28), channel_id=1, source_target_pairs={{0,64},{1,65},{2,66},{3,67},{4,68},{5,69},{6,70},{7,71},{8,72},{9,... | collective-permute-start | bytes 1081352 | tf_op jit(solution)/shard_map/ppermute | solution.py:283

commit v6 on v3

--- a/solution.py
+++ b/solution.py
@@ -33,7 +33,7 @@
     return pltpu.roll(jnp.broadcast_to(line, (rows, width)), start, 1, stride=1, stride_axis=0)
 
 
-def range_kernel(echo_hbm, chirp_hbm, out_ref, echo, chirp, e_hi, e_lo, w_hi, w_lo, sems):
+def range_kernel(echo_hbm, chirp_hbm, out_hbm, echo, chirp, out, e_hi, e_lo, w_hi, w_lo, sems, out_sems):
     taps_copy = pltpu.make_async_copy(chirp_hbm, chirp, sems.at[4])
     taps_copy.start()
     copies = []
@@ -53,32 +53,45 @@
             w_ref[0:128, 256 * j + 128:256 * j + 256] = -im[:, cols]
             w_ref[128:256, 256 * j:256 * j + 128] = im[:, cols]
             w_ref[128:256, 256 * j + 128:256 * j + 256] = re[:, cols]
-
-    def fill(m):
-        copies[m].wait()
-        for n in range(16 * m, 16 * m + 16):
+    for copy in copies:
+        copy.wait()
+
+    def fill(first, end):
+        for n in range(first, min(end, 64)):
             for part in range(2):
                 hi, lo = split(echo[part, :, 128 * n:128 * n + 128])
                 e_hi[16 * n:16 * n + 16, 128 * part:128 * part + 128] = hi
                 e_lo[16 * n:16 * n + 16, 128 * part:128 * part + 128] = lo
 
-    fill(0)
+    def send(sem, first, count):
+        copy = pltpu.make_async_copy(out.at[pl.ds(first, count)], out_hbm.at[pl.ds(first, count)], out_sems.at[sem])
+        copy.start()
+        return copy
+
+    fill(0, 4)
     early = lax.broadcasted_iota(jnp.int32, (256, 128), 1) < REACH
     last = [jnp.zeros((16, 128), F32)] * 2
+    sent = []
     for m in range(4):
-        if m < 3:
-            fill(m + 1)
+        fill(16 * m + 4, 16 * m + 20)
         starts = [256 * m + 16 * j for j in range(5)]
-        hi = jnp.concatenate([e_hi[s:s + 256, :] for s in starts], 1)
-        lo = jnp.concatenate([e_lo[s:s + 256, :] for s in starts], 1)
-        acc = dot_nt(hi, w_hi[...]) + dot_nt(hi, w_lo[...]) + dot_nt(lo, w_hi[...])
+        hi = [e_hi[s:s + 256, :] for s in starts]
+        lo = [e_lo[s:s + 256, :] for s in starts]
+        acc = dot_nt(
+            jnp.concatenate(hi + hi + lo, 1), jnp.concatenate([w_hi[...], w_lo[...], w_hi[...]], 1)
+        )
         for part in range(2):
             turned = pltpu.roll(acc[:, 128 * part:128 * part + 128], REACH, 1)
             before = jnp.concatenate([last[part], turned[0:240]], 0)
-            out_ref[16 * m:16 * m + 16, 16 * part:16 * part + 16, :] = jnp.where(early, before, turned).reshape(16, 16, 128)
+            out[16 * m:16 * m + 16, 16 * part:16 * part + 16, :] = jnp.where(early, before, turned).reshape(16, 16, 128)
             last[part] = turned[240:256]
-    for part in range(2):
-        out_ref[0, 16 * part:16 * part + 16, 0:REACH] = last[part][:, 0:REACH]
+        if m == 3:
+            for part in range(2):
+                out[0, 16 * part:16 * part + 16, 0:REACH] = last[part][:, 0:REACH]
+            sent.append(send(4, 0, 1))
+        sent.append(send(m, max(16 * m, 1), 16 if m else 15))
+    for copy in sent:
+        copy.wait()
 
 
 def prepare_kernel(pairing_ref, offsets_ref, weight_ref, rows_ref, near_ref, far_ref):
@@ -209,13 +222,13 @@
         out_ref[1, 128 * g:128 * g + 128, :] = window[128:256] * scale
 
 
-def call(kernel, name, out_shape, scratch, n_in, smem=(), hbm=(), flops=0, moved=0, vmem=VMEM_LIMIT):
+def call(kernel, name, out_shape, scratch, n_in, smem=(), hbm=(), flops=0, moved=0, vmem=VMEM_LIMIT, out=pltpu.VMEM):
     spaces = [pltpu.SMEM if i in smem else pltpu.HBM if i in hbm else pltpu.VMEM for i in range(n_in)]
     return pl.pallas_call(
         kernel,
         out_shape=out_shape,
         in_specs=[pl.BlockSpec(memory_space=space) for space in spaces],
-        out_specs=jax.tree.map(lambda _: pl.BlockSpec(memory_space=pltpu.VMEM), out_shape),
+        out_specs=jax.tree.map(lambda _: pl.BlockSpec(memory_space=out), out_shape),
         scratch_shapes=scratch,
         compiler_params=pltpu.CompilerParams(vmem_limit_bytes=vmem),
         cost_estimate=pl.CostEstimate(flops=flops, bytes_accessed=moved, transcendentals=0),
@@ -233,10 +246,10 @@
     taps = azimuth_filter.reshape(2, 1, 1024)
     parted = call(
         range_kernel, "range_filter", shape(64, 32, 128),
-        [pltpu.VMEM((2, 16, 8192), F32), pltpu.VMEM((2, 1, 512), F32)]
+        [pltpu.VMEM((2, 16, 8192), F32), pltpu.VMEM((2, 1, 512), F32), pltpu.VMEM((64, 32, 128), F32)]
         + [pltpu.VMEM((1088, 256), BF16)] * 2 + [pltpu.VMEM((256, 1280), BF16)] * 2
-        + [pltpu.SemaphoreType.DMA((5,))],
-        2, hbm=(0, 1), flops=2_000_000_000, moved=2 << 20, vmem=60 << 20,
+        + [pltpu.SemaphoreType.DMA((5,))] * 2,
+        2, hbm=(0, 1), flops=2_000_000_000, moved=2 << 20, vmem=60 << 20, out=pltpu.HBM,
     )(signal, chirp)
     turned = lax.all_to_all(parted, "wide", split_axis=0, concat_axis=0, tiled=True)
     weight, rows, near, far = call(

time: 72.3 us -> 70.8 us (0.979)
  Pallas kernels: 14.8 us -> 13.3 us
    pallas_call x1, Pallas kernels: 5.95 us -> 4.44 us  [body(): call(range_kernel, 'range_filter', shape(64, 32, 128), [pltpu.VMEM((2, 16...]
  transfers between devices with their start and end apart: 5 -> 5, of which waited for: 4 -> 4; matrix products, arithmetic and copies ran while one was open for 0% -> 0% of each run, Pallas kernels for 6% -> 7%
where the time goes in v6:
time: 70.8 us; the launch traced here: 70.2 us
  waiting for transfers between devices  38.4 us (54%)
  starting transfers between devices  17.8 us (25%)
  Pallas kernels  13.3 us (19%)
    all_to_all x1, waiting for transfers between devices, body(): lax.all_to_all(parted, 'wide', split_axis=0, concat_axis=0, tiled=True)  26.6 us
    all_to_all x1, starting transfers between devices, body(): lax.all_to_all(parted, 'wide', split_axis=0, concat_axis=0, tiled=True)  12.8 us
    ppermute x3, waiting for transfers between devices, body(): lax.ppermute(p, 'chan', [(i, i ^ k) for i in range(4)])  6.08 us
    ppermute x1, waiting for transfers between devices, body(): after = lax.ppermute(edge, 'wide', [(i, (i - 1) % 64) for i in range(64)])  5.71 us
    pallas_call x2, Pallas kernels, body(): call(functools.partial(azimuth_half, flip), 'azimuth_' + ('own', 'other')...  5.29 us
    pallas_call x1, Pallas kernels, body(): call(range_kernel, 'range_filter', shape(64, 32, 128), [pltpu.VMEM((2, 16...  4.44 us
    ppermute x3, starting transfers between devices, body(): lax.ppermute(p, 'chan', [(i, i ^ k) for i in range(4)])  3.73 us
    pallas_call x1, Pallas kernels, body(): call(coherence_kernel, 'coherence', shape(2, 256, 128), [pltpu.VMEM((384,...  1.66 us
  transfers between devices with their start and end apart: 5, of which 4 were waited for; matrix products, arithmetic and copies ran while one was open for 0% of the time, Pallas kernels for 7%

profile of v6, /device:TPU:26, one launch (start us, length us, event | category | flops | bytes accessed | tf_op | source)
XLA Modules:
  0.0 70.2 jit_solution(18051855921456813381)
XLA Ops:
  0.0 4.4 %range_filter.1 = f32[64,32,128]{2,1,0:T(8,128)} custom-call(f32[2,16,8192]{2,1,0:T(8,128)} %bitcast.3, f32[2,1,512]{2,1,0:T(1,128)} %chirp_hbm.1), custom_call_target="tpu_custom_call" | custom-call | flops 2000000000 | bytes 2097152 | tf_op jit(solution)/shard_map/range_filter/pallas_call | solution.py:247
  4.5 0.0 copy-start.2
  4.5 12.8 %all-to-all-start = ((f32[64,32,128]{2,1,0:T(8,128)}), f32[64,32,128]{2,1,0:T(8,128)S(1)}, u32[]{:S(2)}, u32[]{:S(2)}) async-start(f32[64,32,128]{2,1,0:T(8,128)} %range_filter.1), calls=%async_computation | async-start | bytes 2097152 | tf_op jit(solution)/shard_map/all_to_all | solution.py:254
  17.3 0.0 copy-done.2
  17.3 0.0 copy-start.1
  17.3 0.1 copy.6.offsets_ref
  17.4 0.6 copy-done.1
  17.9 0.0 copy-start
  17.9 0.7 prepare.1
  18.6 26.6 %all-to-all-done.x_ref = f32[64,32,128]{2,1,0:T(8,128)S(1)} async-done(((f32[64,32,128]{2,1,0:T(8,128)}), f32[64,32,128]{2,1,0:T(8,128)S(1)}, u32[]{:S(2)}, u32[]{:S(2)}) %all-to-all-start) | async-done | bytes 1048608 | tf_op jit(solution)/shard_map/all_to_all | solution.py:254
  45.2 0.0 copy-done
  45.2 2.4 %azimuth_other.1 = (f32[2,272,128]{2,1,0:T(8,128)S(1)}, f32[2,272,128]{2,1,0:T(8,128)S(1)}, f32[8,128]{1,0:T(8,128)S(1)}) custom-call(f32[64,32,128]{2,1,0:T(8,128)S(1)} %all-to-all-done.x_ref, f32[2,1,1024]{2,1,0:T(1,128)S(1)} %copy-done, f32[32,128]{1,0:T(8,128)S(1)} %bitcast.2), custom_call_target="tpu_custom_call" | custom-call | flops 1500000000 | bytes 4194304 | tf_op jit(solution)/shard_map/azimuth_other/pallas_call | solution.py:263
  47.6 2.2 %collective-permute-start = (f32[2,272,128]{2,1,0:T(8,128)S(1)}, f32[2,272,128]{2,1,0:T(8,128)S(1)}, u32[]{:S(2)}, u32[]{:S(2)}) collective-permute-start(f32[2,272,128]{2,1,0:T(8,128)S(1)} %get-tuple-element.20), channel_id=1, source_target_pairs={{0,128},{64,192},{128,0},{192,64},{1,129},{65,193},{129,1},{193,65... | collective-permute-start | bytes 835592 | tf_op jit(solution)/shard_map/ppermute | solution.py:272
  49.8 0.0 collective-permute-start.1
  49.8 2.9 %azimuth_own.1 = (f32[2,272,128]{2,1,0:T(8,128)S(1)}, f32[2,272,128]{2,1,0:T(8,128)S(1)}, f32[8,128]{1,0:T(8,128)}) custom-call(f32[64,32,128]{2,1,0:T(8,128)S(1)} %all-to-all-done.x_ref, f32[2,1,1024]{2,1,0:T(1,128)S(1)} %copy-done, f32[8,128]{1,0:T(8,128)S(1)} %get-tuple-element.18.order_ref), custom_call_target="tpu_custom_call" | custom-call | flops 1500000000 | bytes 4194304 | tf_op jit(solution)/shard_map/azimuth_own/pallas_call | solution.py:263
  52.7 1.5 %collective-permute-start.2 = (f32[2,272,128]{2,1,0:T(8,128)S(1)}, f32[2,272,128]{2,1,0:T(8,128)S(1)}, u32[]{:S(2)}, u32[]{:S(2)}) collective-permute-start(f32[2,272,128]{2,1,0:T(8,128)S(1)} %get-tuple-element.22), channel_id=1, source_target_pairs={{0,64},{64,0},{128,192},{192,128},{1,65},{65,1},{129,193},{193,129... | collective-permute-start | bytes 835592 | tf_op jit(solution)/shard_map/ppermute | solution.py:272
  54.3 2.9 %collective-permute-done.y2 = f32[2,272,128]{2,1,0:T(8,128)S(1)} collective-permute-done((f32[2,272,128]{2,1,0:T(8,128)S(1)}, f32[2,272,128]{2,1,0:T(8,128)S(1)}, u32[]{:S(2)}, u32[]{:S(2)}) %collective-permute-start) | collective-permute-done | bytes 278560 | tf_op jit(solution)/shard_map/ppermute | solution.py:272
  57.2 3.1 %collective-permute-done.1.y3 = f32[2,272,128]{2,1,0:T(8,128)S(1)} collective-permute-done((f32[2,272,128]{2,1,0:T(8,128)S(1)}, f32[2,272,128]{2,1,0:T(8,128)S(1)}, u32[]{:S(2)}, u32[]{:S(2)}) %collective-permute-start.1) | collective-permute-done | bytes 278560 | tf_op jit(solution)/shard_map/ppermute | solution.py:272
  60.3 0.1 three_receivers.1.part_ref
  60.4 0.0 collective-permute-done.2.y1
  60.5 0.2 edge.1
  60.7 1.2 %collective-permute-start.3 = (f32[136,128]{1,0:T(8,128)S(1)}, f32[136,128]{1,0:T(8,128)S(1)}, u32[]{:S(2)}, u32[]{:S(2)}) collective-permute-start(f32[136,128]{1,0:T(8,128)S(1)} %edge.1), channel_id=1, source_target_pairs={{0,63},{1,0},{2,1},{3,2},{4,3},{5,4},{6,5},{7,6},{8,7},{9,8},{10,9... | collective-permute-start | bytes 208904 | tf_op jit(solution)/shard_map/ppermute | solution.py:279
  61.9 0.9 %window_sums.1.main_ref = f32[2,512,128]{2,1,0:T(8,128)S(1)} custom-call(f32[4,8,128]{2,1,0:T(8,128)S(1)} %get-tuple-element.16.weight_ref, bf16[2,128,256]{2,1,0:T(8,128)(2,1)S(1)} %get-tuple-element.14.rows_ref, bf16[2,128,128]{2,1,0:T(8,128)(2,1)S(1)} %get-tuple-element.17.near_ref, f32[4,272,128]{2,1,0:T(8,128)S(1)} %three_receivers.1.part_ref, ...), custom_call_target="tpu_custom_call" | custom-call | flops 500000000 | bytes 1048576 | tf_op jit(solution)/shard_map/window_sums/pallas_call | solution.py:280
  62.8 5.7 %collective-permute-done.3.edge_ref = f32[136,128]{1,0:T(8,128)S(1)} collective-permute-done((f32[136,128]{1,0:T(8,128)S(1)}, f32[136,128]{1,0:T(8,128)S(1)}, u32[]{:S(2)}, u32[]{:S(2)}) %collective-permute-start.3) | collective-permute-done | bytes 69664 | tf_op jit(solution)/shard_map/ppermute | solution.py:279
  68.6 1.7 %coherence.1 = f32[2,256,128]{2,1,0:T(8,128)} custom-call(bf16[2,128,256]{2,1,0:T(8,128)(2,1)S(1)} %get-tuple-element.14.rows_ref, bf16[2,128,128]{2,1,0:T(8,128)(2,1)S(1)} %get-tuple-element.15.far_ref, f32[2,512,128]{2,1,0:T(8,128)S(1)} %window_sums.1.main_ref, f32[136,128]{1,0:T(8,128)S(1)} %collective-permute-done.3.edge_ref), custom_call_target="tpu_custom_call" | custom-call | flops 500000000 | bytes 1048576 | tf_op jit(solution)/shard_map/coherence/pallas_call | solution.py:284
Async XLA Ops:
  4.5 12.8 %copy-start.2 = (s32[8,2]{0,1:T(2,128)S(1)}, s32[8,2]{0,1:T(2,128)}, u32[]{:S(2)}) copy-start(s32[8,2]{0,1:T(2,128)} %param.9) | copy-start | bytes 196
  4.5 40.8 %all-to-all-start = ((f32[64,32,128]{2,1,0:T(8,128)}), f32[64,32,128]{2,1,0:T(8,128)S(1)}, u32[]{:S(2)}, u32[]{:S(2)}) async-start(f32[64,32,128]{2,1,0:T(8,128)} %range_filter.1), calls=%async_computation | async-start | bytes 2097152 | tf_op jit(solution)/shard_map/all_to_all | solution.py:254
  17.3 0.7 copy-start.1
  17.9 27.3 %copy-start = (f32[2,1,1024]{2,1,0:T(1,128)S(1)}, f32[2,1,1024]{2,1,0:T(1,128)}, u32[]{:S(2)}) copy-start(f32[2,1,1024]{2,1,0:T(1,128)} %taps_ref.3) | copy-start | bytes 24580
  47.6 9.6 %collective-permute-start = (f32[2,272,128]{2,1,0:T(8,128)S(1)}, f32[2,272,128]{2,1,0:T(8,128)S(1)}, u32[]{:S(2)}, u32[]{:S(2)}) collective-permute-start(f32[2,272,128]{2,1,0:T(8,128)S(1)} %get-tuple-element.20), channel_id=1, source_target_pairs={{0,128},{64,192},{128,0},{192,64},{1,129},{65,193},{129,1},{193,65... | collective-permute-start | bytes 835592 | tf_op jit(solution)/shard_map/ppermute | solution.py:272
  49.8 10.5 %collective-permute-start.1 = (f32[2,272,128]{2,1,0:T(8,128)S(1)}, f32[2,272,128]{2,1,0:T(8,128)S(1)}, u32[]{:S(2)}, u32[]{:S(2)}) collective-permute-start(f32[2,272,128]{2,1,0:T(8,128)S(1)} %get-tuple-element.21), channel_id=1, source_target_pairs={{0,192},{64,128},{128,64},{192,0},{1,193},{65,129},{129,65},{193,1... | collective-permute-start | bytes 835592 | tf_op jit(solution)/shard_map/ppermute | solution.py:272
  52.7 7.7 %collective-permute-start.2 = (f32[2,272,128]{2,1,0:T(8,128)S(1)}, f32[2,272,128]{2,1,0:T(8,128)S(1)}, u32[]{:S(2)}, u32[]{:S(2)}) collective-permute-start(f32[2,272,128]{2,1,0:T(8,128)S(1)} %get-tuple-element.22), channel_id=1, source_target_pairs={{0,64},{64,0},{128,192},{192,128},{1,65},{65,1},{129,193},{193,129... | collective-permute-start | bytes 835592 | tf_op jit(solution)/shard_map/ppermute | solution.py:272
  60.7 7.9 %collective-permute-start.3 = (f32[136,128]{1,0:T(8,128)S(1)}, f32[136,128]{1,0:T(8,128)S(1)}, u32[]{:S(2)}, u32[]{:S(2)}) collective-permute-start(f32[136,128]{1,0:T(8,128)S(1)} %edge.1), channel_id=1, source_target_pairs={{0,63},{1,0},{2,1},{3,2},{4,3},{5,4},{6,5},{7,6},{8,7},{9,8},{10,9... | collective-permute-start | bytes 208904 | tf_op jit(solution)/shard_map/ppermute | solution.py:279

commit v7 on v6

--- a/solution.py
+++ b/solution.py
@@ -111,9 +111,9 @@
         rows_ref[g] = jnp.where(jnp.abs(src - REACH - row - oa) <= RADIUS, 1.0, 0.0).astype(BF16)
         near = (jnp.abs(lane - REACH - bin_out - orr) <= RADIUS) & ((lane >= REACH) | jnp.logical_not(first))
         near_ref[g] = jnp.where(near, 1.0, 0.0).astype(BF16)
-        far = (jnp.abs(lane + 128 - REACH - bin_out - orr) <= RADIUS) & (
-            (lane < REACH) | ((lane < 2 * REACH) & jnp.logical_not(final))
-        )
+        bin_in = lane % 16
+        far = (jnp.abs(bin_in + REACH - bin_out % 16 - orr) <= RADIUS) & (lane // 16 == bin_out // 16) & (lane < 64)
+        far = far & ((bin_in < REACH) | jnp.logical_not(final))
         far_ref[g] = jnp.where(far, 1.0, 0.0).astype(BF16)
 
 
@@ -186,7 +186,8 @@
     return fr * ar + fi * ai, fi * ar - fr * ai, fr * fr + fi * fi, ar * ar + ai * ai
 
 
-def main_kernel(weight_ref, rows_ref, near_ref, part_ref, y1, out_ref, p_hi, p_lo):
+def main_kernel(weight_ref, rows_ref, near_ref, part_ref, y1, out_ref, last_ref, p_hi, p_lo):
+    lane = lax.broadcasted_iota(jnp.int32, (128, 128), 1)
     for q, value in enumerate(quantities(*whole_sums(weight_ref, part_ref, y1))):
         hi, lo = split(value)
         p_hi[0:272, 128 * q:128 * q + 128] = hi
@@ -196,10 +197,19 @@
     for g in range(2):
         sums = dot_nn(rows_ref[g], p_hi[128 * g:128 * g + 256, :]) + dot_nn(rows_ref[g], p_lo[128 * g:128 * g + 256, :])
         hi, lo = split(jnp.concatenate([sums[:, 128 * q:128 * q + 128] for q in range(4)], 0))
-        out_ref[g] = dot_nn(hi, near_ref[g]) + dot_nn(lo, near_ref[g])
-
-
-def coherence_kernel(rows_ref, far_ref, main_ref, edge_ref, out_ref, p_hi, p_lo):
+        window = dot_nn(hi, near_ref[g]) + dot_nn(lo, near_ref[g])
+        planes = [window[128 * q:128 * q + 128] for q in range(4)]
+        scale = 1.0 / jnp.sqrt(jnp.maximum(planes[2], 1.0) * jnp.maximum(planes[3], 1.0))
+        packed = jnp.zeros((128, 128), F32)
+        for q in range(4):
+            moved = pltpu.roll(planes[q], 16 * q + 16, 1)
+            packed = jnp.where((lane >= 16 * q) & (lane < 16 * q + 16), moved, packed)
+        last_ref[128 * g:128 * g + 128] = packed
+        for part in range(2):
+            out_ref[part, 128 * g:128 * g + 128, :] = planes[part] * scale
+
+
+def coherence_kernel(rows_ref, far_ref, most_ref, last_ref, edge_ref, out_ref, p_hi, p_lo):
     packed = edge_ref[...]
     edge = jnp.concatenate([packed, pltpu.roll(packed, 64, 1)], 0)
     lane = lax.broadcasted_iota(jnp.int32, (272, 128), 1)
@@ -213,13 +223,17 @@
     p_lo[0:272, :] = lo
     p_hi[272:384, :] = jnp.zeros((112, 128), BF16)
     p_lo[272:384, :] = jnp.zeros((112, 128), BF16)
+    keep = lax.broadcasted_iota(jnp.int32, (128, 128), 1) < 112
     for g in range(2):
         sums = dot_nn(rows_ref[g], p_hi[128 * g:128 * g + 256, :]) + dot_nn(rows_ref[g], p_lo[128 * g:128 * g + 256, :])
-        hi, lo = split(jnp.concatenate([sums] + [pltpu.roll(sums, 128 - 16 * q, 1) for q in range(1, 4)], 0))
-        window = main_ref[g] + dot_nn(hi, far_ref[g]) + dot_nn(lo, far_ref[g])
-        scale = 1.0 / jnp.sqrt(jnp.maximum(window[256:384], 1.0) * jnp.maximum(window[384:512], 1.0))
-        out_ref[0, 128 * g:128 * g + 128, :] = window[0:128] * scale
-        out_ref[1, 128 * g:128 * g + 128, :] = window[128:256] * scale
+        hi, lo = split(sums)
+        window = last_ref[128 * g:128 * g + 128] + dot_nn(hi, far_ref[g]) + dot_nn(lo, far_ref[g])
+        power = jnp.maximum(window, 1.0)
+        scale = 1.0 / jnp.sqrt(power * pltpu.roll(power, 112, 1))
+        rows = slice(128 * g, 128 * g + 128)
+        for part in range(2):
+            value = window * pltpu.roll(scale, 96 + 16 * part, 1)
+            out_ref[part, rows, :] = jnp.where(keep, most_ref[part, rows, :], pltpu.roll(value, 112 - 16 * part, 1))
 
 
 def call(kernel, name, out_shape, scratch, n_in, smem=(), hbm=(), flops=0, moved=0, vmem=VMEM_LIMIT, out=pltpu.VMEM):
@@ -277,14 +291,14 @@
         edge_kernel, "edge", shape(136, 128), [], 3, flops=1_000_000, moved=2 << 20,
     )(weight, part, y1)
     after = lax.ppermute(edge, "wide", [(i, (i - 1) % 64) for i in range(64)])
-    main = call(
-        main_kernel, "window_sums", shape(2, 512, 128), [pltpu.VMEM((384, 512), BF16)] * 2,
+    most, last = call(
+        main_kernel, "window_sums", (shape(2, 256, 128), shape(256, 128)), [pltpu.VMEM((384, 512), BF16)] * 2,
         5, flops=500_000_000, moved=1 << 20,
     )(weight, rows, near, part, y1)
     return call(
         coherence_kernel, "coherence", shape(2, 256, 128), [pltpu.VMEM((384, 128), BF16)] * 2,
-        4, flops=500_000_000, moved=1 << 20,
-    )(rows, far, main, after)
+        5, flops=500_000_000, moved=1 << 20,
+    )(rows, far, most, last, after)
 
 
 def solution(mesh):

time: 70.8 us -> 70.9 us (level)
  no operation moved by 1% of the time
where the time goes in v7:
time: 70.9 us; the launch traced here: 70.3 us
  waiting for transfers between devices  38.3 us (54%)
  starting transfers between devices  17.8 us (25%)
  Pallas kernels  13.5 us (19%)
    all_to_all x1, waiting for transfers between devices, body(): lax.all_to_all(parted, 'wide', split_axis=0, concat_axis=0, tiled=True)  26.5 us
    all_to_all x1, starting transfers between devices, body(): lax.all_to_all(parted, 'wide', split_axis=0, concat_axis=0, tiled=True)  12.8 us
    ppermute x3, waiting for transfers between devices, body(): lax.ppermute(p, 'chan', [(i, i ^ k) for i in range(4)])  6.08 us
    ppermute x1, waiting for transfers between devices, body(): after = lax.ppermute(edge, 'wide', [(i, (i - 1) % 64) for i in range(64)])  5.64 us
    pallas_call x2, Pallas kernels, body(): call(functools.partial(azimuth_half, flip), 'azimuth_' + ('own', 'other')...  5.29 us
    pallas_call x1, Pallas kernels, body(): call(range_kernel, 'range_filter', shape(64, 32, 128), [pltpu.VMEM((2, 16...  4.45 us
    ppermute x3, starting transfers between devices, body(): lax.ppermute(p, 'chan', [(i, i ^ k) for i in range(4)])  3.73 us
    pallas_call x1, Pallas kernels, body(): call(coherence_kernel, 'coherence', shape(2, 256, 128), [pltpu.VMEM((384,...  1.77 us
  transfers between devices with their start and end apart: 5, of which 4 were waited for; matrix products, arithmetic and copies ran while one was open for 0% of the time, Pallas kernels for 7%

profile of v7, /device:TPU:26, one launch (start us, length us, event | category | flops | bytes accessed | tf_op | source)
XLA Modules:
  0.0 70.3 jit_solution(15904468617028413194)
XLA Ops:
  0.0 4.5 %range_filter.1 = f32[64,32,128]{2,1,0:T(8,128)} custom-call(f32[2,16,8192]{2,1,0:T(8,128)} %bitcast.3, f32[2,1,512]{2,1,0:T(1,128)} %chirp_hbm.1), custom_call_target="tpu_custom_call" | custom-call | flops 2000000000 | bytes 2097152 | tf_op jit(solution)/shard_map/range_filter/pallas_call | solution.py:261
  4.5 0.0 copy-start.2
  4.5 12.8 %all-to-all-start = ((f32[64,32,128]{2,1,0:T(8,128)}), f32[64,32,128]{2,1,0:T(8,128)S(1)}, u32[]{:S(2)}, u32[]{:S(2)}) async-start(f32[64,32,128]{2,1,0:T(8,128)} %range_filter.1), calls=%async_computation | async-start | bytes 2097152 | tf_op jit(solution)/shard_map/all_to_all | solution.py:268
  17.3 0.0 copy-done.2
  17.3 0.0 copy-start.1
  17.3 0.1 copy.6.offsets_ref
  17.4 0.6 copy-done.1
  18.0 0.0 copy-start
  18.0 0.7 %prepare.1 = (f32[4,8,128]{2,1,0:T(8,128)S(1)}, bf16[2,128,256]{2,1,0:T(8,128)(2,1)S(1)}, bf16[2,128,128]{2,1,0:T(8,128)(2,1)S(1)}, bf16[2,128,128]{2,1,0:T(8,128)(2,1)S(1)}) custom-call(s32[4]{0:T(128)S(1)} %copy-done.1, s32[8,2]{1,0:T(8,128)S(1)} %copy.6.offsets_ref), custom_call_target="tpu_custom_call" | custom-call | flops 1000000000 | bytes 1048576 | tf_op jit(solution)/shard_map/prepare/pallas_call | solution.py:269
  18.7 26.5 %all-to-all-done.x_ref = f32[64,32,128]{2,1,0:T(8,128)S(1)} async-done(((f32[64,32,128]{2,1,0:T(8,128)}), f32[64,32,128]{2,1,0:T(8,128)S(1)}, u32[]{:S(2)}, u32[]{:S(2)}) %all-to-all-start) | async-done | bytes 1048608 | tf_op jit(solution)/shard_map/all_to_all | solution.py:268
  45.2 0.0 copy-done
  45.2 2.4 %azimuth_other.1 = (f32[2,272,128]{2,1,0:T(8,128)S(1)}, f32[2,272,128]{2,1,0:T(8,128)S(1)}, f32[8,128]{1,0:T(8,128)S(1)}) custom-call(f32[64,32,128]{2,1,0:T(8,128)S(1)} %all-to-all-done.x_ref, f32[2,1,1024]{2,1,0:T(1,128)S(1)} %copy-done, f32[32,128]{1,0:T(8,128)S(1)} %bitcast.2), custom_call_target="tpu_custom_call" | custom-call | flops 1500000000 | bytes 4194304 | tf_op jit(solution)/shard_map/azimuth_other/pallas_call | solution.py:277
  47.6 2.2 %collective-permute-start = (f32[2,272,128]{2,1,0:T(8,128)S(1)}, f32[2,272,128]{2,1,0:T(8,128)S(1)}, u32[]{:S(2)}, u32[]{:S(2)}) collective-permute-start(f32[2,272,128]{2,1,0:T(8,128)S(1)} %get-tuple-element.22), channel_id=1, source_target_pairs={{0,128},{64,192},{128,0},{192,64},{1,129},{65,193},{129,1},{193,65... | collective-permute-start | bytes 835592 | tf_op jit(solution)/shard_map/ppermute | solution.py:286
  49.8 0.0 collective-permute-start.1
  49.8 2.9 %azimuth_own.1 = (f32[2,272,128]{2,1,0:T(8,128)S(1)}, f32[2,272,128]{2,1,0:T(8,128)S(1)}, f32[8,128]{1,0:T(8,128)}) custom-call(f32[64,32,128]{2,1,0:T(8,128)S(1)} %all-to-all-done.x_ref, f32[2,1,1024]{2,1,0:T(1,128)S(1)} %copy-done, f32[8,128]{1,0:T(8,128)S(1)} %get-tuple-element.20.order_ref), custom_call_target="tpu_custom_call" | custom-call | flops 1500000000 | bytes 4194304 | tf_op jit(solution)/shard_map/azimuth_own/pallas_call | solution.py:277
  52.7 1.5 %collective-permute-start.2 = (f32[2,272,128]{2,1,0:T(8,128)S(1)}, f32[2,272,128]{2,1,0:T(8,128)S(1)}, u32[]{:S(2)}, u32[]{:S(2)}) collective-permute-start(f32[2,272,128]{2,1,0:T(8,128)S(1)} %get-tuple-element.24), channel_id=1, source_target_pairs={{0,64},{64,0},{128,192},{192,128},{1,65},{65,1},{129,193},{193,129... | collective-permute-start | bytes 835592 | tf_op jit(solution)/shard_map/ppermute | solution.py:286
  54.3 2.9 %collective-permute-done.y2 = f32[2,272,128]{2,1,0:T(8,128)S(1)} collective-permute-done((f32[2,272,128]{2,1,0:T(8,128)S(1)}, f32[2,272,128]{2,1,0:T(8,128)S(1)}, u32[]{:S(2)}, u32[]{:S(2)}) %collective-permute-start) | collective-permute-done | bytes 278560 | tf_op jit(solution)/shard_map/ppermute | solution.py:286
  57.2 3.1 %collective-permute-done.1.y3 = f32[2,272,128]{2,1,0:T(8,128)S(1)} collective-permute-done((f32[2,272,128]{2,1,0:T(8,128)S(1)}, f32[2,272,128]{2,1,0:T(8,128)S(1)}, u32[]{:S(2)}, u32[]{:S(2)}) %collective-permute-start.1) | collective-permute-done | bytes 278560 | tf_op jit(solution)/shard_map/ppermute | solution.py:286
  60.3 0.1 three_receivers.1.part_ref
  60.5 0.0 collective-permute-done.2.y1
  60.5 0.2 edge.1
  60.7 1.2 %collective-permute-start.3 = (f32[136,128]{1,0:T(8,128)S(1)}, f32[136,128]{1,0:T(8,128)S(1)}, u32[]{:S(2)}, u32[]{:S(2)}) collective-permute-start(f32[136,128]{1,0:T(8,128)S(1)} %edge.1), channel_id=1, source_target_pairs={{0,63},{1,0},{2,1},{3,2},{4,3},{5,4},{6,5},{7,6},{8,7},{9,8},{10,9... | collective-permute-start | bytes 208904 | tf_op jit(solution)/shard_map/ppermute | solution.py:293
  61.9 1.0 %window_sums.1 = (f32[2,256,128]{2,1,0:T(8,128)S(1)}, f32[256,128]{1,0:T(8,128)S(1)}) custom-call(f32[4,8,128]{2,1,0:T(8,128)S(1)} %get-tuple-element.18.weight_ref, bf16[2,128,256]{2,1,0:T(8,128)(2,1)S(1)} %get-tuple-element.16.rows_ref, bf16[2,128,128]{2,1,0:T(8,128)(2,1)S(1)} %get-tuple-element.19.near_ref, f32[4,272,128]{2,1,0:T(8,128)S(1)} %three_receivers.1.part_ref, ...), custom_call_target="tpu_custom_call" | custom-call | flops 500000000 | bytes 1048576 | tf_op jit(solution)/shard_map/window_sums/pallas_call | solution.py:294
  62.9 5.6 %collective-permute-done.3.edge_ref = f32[136,128]{1,0:T(8,128)S(1)} collective-permute-done((f32[136,128]{1,0:T(8,128)S(1)}, f32[136,128]{1,0:T(8,128)S(1)}, u32[]{:S(2)}, u32[]{:S(2)}) %collective-permute-start.3) | collective-permute-done | bytes 69664 | tf_op jit(solution)/shard_map/ppermute | solution.py:293
  68.6 1.8 %coherence.1 = f32[2,256,128]{2,1,0:T(8,128)} custom-call(bf16[2,128,256]{2,1,0:T(8,128)(2,1)S(1)} %get-tuple-element.16.rows_ref, bf16[2,128,128]{2,1,0:T(8,128)(2,1)S(1)} %get-tuple-element.17.far_ref, f32[2,256,128]{2,1,0:T(8,128)S(1)} %get-tuple-element.25.most_ref, f32[256,128]{1,0:T(8,128)S(1)} %get-tuple-element.26.last_ref, ...), custom_call_target="tpu_custom_call" | custom-call | flops 500000000 | bytes 1048576 | tf_op jit(solution)/shard_map/coherence/pallas_call | solution.py:298
Async XLA Ops:
  4.5 12.8 %copy-start.2 = (s32[8,2]{0,1:T(2,128)S(1)}, s32[8,2]{0,1:T(2,128)}, u32[]{:S(2)}) copy-start(s32[8,2]{0,1:T(2,128)} %param.9) | copy-start | bytes 196
  4.5 40.8 %all-to-all-start = ((f32[64,32,128]{2,1,0:T(8,128)}), f32[64,32,128]{2,1,0:T(8,128)S(1)}, u32[]{:S(2)}, u32[]{:S(2)}) async-start(f32[64,32,128]{2,1,0:T(8,128)} %range_filter.1), calls=%async_computation | async-start | bytes 2097152 | tf_op jit(solution)/shard_map/all_to_all | solution.py:268
  17.3 0.7 copy-start.1
  18.0 27.3 %copy-start = (f32[2,1,1024]{2,1,0:T(1,128)S(1)}, f32[2,1,1024]{2,1,0:T(1,128)}, u32[]{:S(2)}) copy-start(f32[2,1,1024]{2,1,0:T(1,128)} %taps_ref.3) | copy-start | bytes 24580
  47.6 9.6 %collective-permute-start = (f32[2,272,128]{2,1,0:T(8,128)S(1)}, f32[2,272,128]{2,1,0:T(8,128)S(1)}, u32[]{:S(2)}, u32[]{:S(2)}) collective-permute-start(f32[2,272,128]{2,1,0:T(8,128)S(1)} %get-tuple-element.22), channel_id=1, source_target_pairs={{0,128},{64,192},{128,0},{192,64},{1,129},{65,193},{129,1},{193,65... | collective-permute-start | bytes 835592 | tf_op jit(solution)/shard_map/ppermute | solution.py:286
  49.8 10.5 %collective-permute-start.1 = (f32[2,272,128]{2,1,0:T(8,128)S(1)}, f32[2,272,128]{2,1,0:T(8,128)S(1)}, u32[]{:S(2)}, u32[]{:S(2)}) collective-permute-start(f32[2,272,128]{2,1,0:T(8,128)S(1)} %get-tuple-element.23), channel_id=1, source_target_pairs={{0,192},{64,128},{128,64},{192,0},{1,193},{65,129},{129,65},{193,1... | collective-permute-start | bytes 835592 | tf_op jit(solution)/shard_map/ppermute | solution.py:286
  52.7 7.7 %collective-permute-start.2 = (f32[2,272,128]{2,1,0:T(8,128)S(1)}, f32[2,272,128]{2,1,0:T(8,128)S(1)}, u32[]{:S(2)}, u32[]{:S(2)}) collective-permute-start(f32[2,272,128]{2,1,0:T(8,128)S(1)} %get-tuple-element.24), channel_id=1, source_target_pairs={{0,64},{64,0},{128,192},{192,128},{1,65},{65,1},{129,193},{193,129... | collective-permute-start | bytes 835592 | tf_op jit(solution)/shard_map/ppermute | solution.py:286
  60.7 7.9 %collective-permute-start.3 = (f32[136,128]{1,0:T(8,128)S(1)}, f32[136,128]{1,0:T(8,128)S(1)}, u32[]{:S(2)}, u32[]{:S(2)}) collective-permute-start(f32[136,128]{1,0:T(8,128)S(1)} %edge.1), channel_id=1, source_target_pairs={{0,63},{1,0},{2,1},{3,2},{4,3},{5,4},{6,5},{7,6},{8,7},{9,8},{10,9... | collective-permute-start | bytes 208904 | tf_op jit(solution)/shard_map/ppermute | solution.py:293

commit v8 on v6

--- a/solution.py
+++ b/solution.py
@@ -10,6 +10,8 @@
 RADIUS = 4
 REACH = 2 * RADIUS
 XOR_ORDER = (0, 2, 3, 1)
+FIRST = 1
+FIRST_COST = 1_000
 F32 = jnp.float32
 BF16 = jnp.bfloat16
 VMEM_LIMIT = 24 * 1024 * 1024
@@ -117,30 +119,61 @@
         far_ref[g] = jnp.where(far, 1.0, 0.0).astype(BF16)
 
 
-def azimuth_half(flip, x_ref, taps_ref, order_ref, o0, o1, done_ref, t_hi, t_lo, x_hi, x_lo, y_ref):
-    done_ref[...] = jnp.zeros((8, 128), F32)
+def build_taps(taps_ref, t_hi, t_lo):
     for part in range(2):
         hi, lo = split(toeplitz(taps_ref[part], 272, 1280, 1280 - REACH))
         t_hi[part] = hi
         t_lo[part] = lo
+
+
+def split_pulses(x_ref, x_hi, x_lo):
+    for part in range(2):
         hi, lo = split(x_ref[:, 16 * part:16 * part + 16, :].reshape(1024, 128))
         x_hi[:, 128 * part:128 * part + 128] = hi
         x_lo[:, 128 * part:128 * part + 128] = lo
+
+
+def quarter_rows(q, picked, t_hi, t_lo, x_hi, x_lo):
+    first, last = max(q - 2, 0), min(q + 2, 3)
+    cols = slice(256 * (first - q + 2), 256 * (last - q + 3))
+    rows = slice(256 * first, 256 * last + 256)
+    t = [ref[part, picked, cols] for ref in (t_hi, t_lo) for part in range(2)]
+    g = [dot_nn(t[i], x_hi[rows, :]) + dot_nn(t[i], x_lo[rows, :]) + dot_nn(t[2 + i], x_hi[rows, :]) for i in range(2)]
+    return g[0][:, 0:128] - g[1][:, 128:256], g[0][:, 128:256] + g[1][:, 0:128]
+
+
+def azimuth_quarter(k, x_ref, taps_ref, order_ref, out_ref, done_ref, t_hi, t_lo, x_hi, x_lo):
+    done_ref[...] = jnp.zeros((8, 128), F32)
+    build_taps(taps_ref, t_hi, t_lo)
+    split_pulses(x_ref, x_hi, x_lo)
+    taps = (t_hi, t_lo, x_hi, x_lo)
     me = lax.axis_index("chan")
-
-    def quarter(q):
-        first, last = max(q - 2, 0), min(q + 2, 3)
-        cols = slice(256 * (first - q + 2), 256 * (last - q + 3))
-        rows = slice(256 * first, 256 * last + 256)
-        t = [ref[part, :, cols] for ref in (t_hi, t_lo) for part in range(2)]
-        g = [dot_nn(t[i], x_hi[rows, :]) + dot_nn(t[i], x_lo[rows, :]) + dot_nn(t[2 + i], x_hi[rows, :]) for i in range(2)]
-        return g[0][:, 0:128] - g[1][:, 128:256], g[0][:, 128:256] + g[1][:, 0:128]
-
+    for q in range(4):
+        @pl.when((me ^ k) == q)
+        def _(q=q):
+            own = quarter_rows(q, slice(0, 272), *taps)
+            shared = quarter_rows(q ^ 1, slice(256, 272) if q % 2 else slice(0, 16), *taps)
+            for part in range(2):
+                out_ref[part] = own[part]
+                if q % 2:
+                    out_ref[part, 0:8, :] = shared[part][0:8]
+                else:
+                    out_ref[part, 264:272, :] = shared[part][8:16]
+                if q == 0:
+                    out_ref[part, 0:8, :] = jnp.zeros((8, 128), F32)
+                if q == 3:
+                    out_ref[part, 264:272, :] = jnp.zeros((8, 128), F32)
+
+
+def azimuth_own(x_ref, taps_ref, order_ref, o0, o1, t_hi, t_lo, x_hi, x_lo, y_ref):
+    build_taps(taps_ref, t_hi, t_lo)
+    split_pulses(x_ref, x_hi, x_lo)
+    me = lax.axis_index("chan")
     for half in range(2):
-        @pl.when((me // 2) ^ flip == half)
+        @pl.when(me // 2 == half)
         def _(half=half):
             for i in range(2):
-                for part, value in enumerate(quarter(2 * half + i)):
+                for part, value in enumerate(quarter_rows(2 * half + i, slice(0, 272), t_hi, t_lo, x_hi, x_lo)):
                     y_ref[i, part] = value
             for part in range(2):
                 y_ref[0, part, 264:272, :] = y_ref[1, part, 8:16, :]
@@ -154,16 +187,18 @@
     o1[...] = y_ref[1 - me % 2]
 
 
-def partial_kernel(weight_ref, y0, y2, y3, part_ref):
+def first_sums_kernel(weight_ref, y0, ya, part_ref):
+    own, other = weight_ref[0, 0:1, :], weight_ref[FIRST, 0:1, :]
     for part in range(2):
-        fore = aft = 0.0
-        for k, y_ref in enumerate((y0, y2, y3)):
-            weight = weight_ref[k, 0:1, :]
-            y = y_ref[part]
-            fore = fore + y * weight
-            aft = aft + y * (1.0 - weight)
-        part_ref[part] = fore
-        part_ref[2 + part] = aft
+        part_ref[part] = y0[part] * own + ya[part] * other
+        part_ref[2 + part] = y0[part] * (1.0 - own) + ya[part] * (1.0 - other)
+
+
+def more_sums_kernel(weight_ref, first_ref, yb, part_ref):
+    weight = weight_ref[3 - FIRST, 0:1, :]
+    for part in range(2):
+        part_ref[part] = first_ref[part] + yb[part] * weight
+        part_ref[2 + part] = first_ref[2 + part] + yb[part] * (1.0 - weight)
 
 
 def whole_sums(weight_ref, part_ref, y1):
@@ -258,21 +293,26 @@
         2, smem=(0, 1), flops=1_000_000_000, moved=1 << 20,
     )(pairing, offsets)
     order = weight.reshape(32, 128)
-    pieces = []
-    for flip in (1, 0):
-        *pair, order = call(
-            functools.partial(azimuth_half, flip), "azimuth_" + ("own", "other")[flip],
-            (shape(2, 272, 128),) * 2 + (shape(8, 128),),
-            [pltpu.VMEM((2, 272, 1280), BF16)] * 2 + [pltpu.VMEM((1024, 256), BF16)] * 2
-            + [pltpu.VMEM((2, 2, 272, 128), F32)],
-            3, flops=1_500_000_000, moved=4 << 20,
-        )(turned, taps, order)
-        pieces.append(pair)
-    (p2, p3), (p0, p1) = pieces
-    y2, y3, y1 = [lax.ppermute(p, "chan", [(i, i ^ k) for i in range(4)]) for k, p in zip(XOR_ORDER[1:], (p2, p3, p1))]
+    scratch = [pltpu.VMEM((2, 272, 1280), BF16)] * 2 + [pltpu.VMEM((1024, 256), BF16)] * 2
+    pa, order = call(
+        functools.partial(azimuth_quarter, 2), "azimuth_first", (shape(2, 272, 128), shape(8, 128)), scratch,
+        3, flops=1_000_000_000, moved=1000,
+    )(turned, taps, order)
+    pb, order = call(
+        functools.partial(azimuth_quarter, 3), "azimuth_second", (shape(2, 272, 128), shape(8, 128)), scratch,
+        3, flops=1000, moved=1000,
+    )(turned, taps, order)
+    p0, p1 = call(
+        azimuth_own, "azimuth_own", (shape(2, 272, 128),) * 2, scratch + [pltpu.VMEM((2, 2, 272, 128), F32)],
+        3, flops=1000, moved=1000,
+    )(turned, taps, order)
+    ya, yb, y1 = [lax.ppermute(p, "chan", [(i, i ^ k) for i in range(4)]) for k, p in ((2, pa), (3, pb), (1, p1))]
     part = call(
-        partial_kernel, "three_receivers", shape(4, 272, 128), [], 4, flops=1_000_000, moved=2 << 20,
-    )(weight, p0, y2, y3)
+        first_sums_kernel, "two_receivers", shape(4, 272, 128), [], 3, flops=FIRST_COST, moved=1000,
+    )(weight, p0, ya)
+    part = call(
+        more_sums_kernel, "three_receivers", shape(4, 272, 128), [], 3, flops=30_000_000_000, moved=2 << 20,
+    )(weight, part, yb)
     edge = call(
         edge_kernel, "edge", shape(136, 128), [], 3, flops=1_000_000, moved=2 << 20,
     )(weight, part, y1)

time: 70.8 us -> 70.9 us (level)
  Pallas kernels: 13.3 us -> 14.3 us
    pallas_call x3 -> x5, Pallas kernels: 5.41 us -> 6.37 us  [the longest x1 2.56 us: body(): call(azimuth_own, 'azimuth_own', (shape(2, 272, 128),) * 2, scratch + [pl...]
  transfers between devices with their start and end apart: 5 -> 5, of which waited for: 4 -> 3; matrix products, arithmetic and copies ran while one was open for 0% -> 0% of each run, Pallas kernels for 7% -> 9%
where the time goes in v8:
time: 70.9 us; the launch traced here: 70.6 us
  waiting for transfers between devices  38.1 us (54%)
  starting transfers between devices  17.4 us (25%)
  Pallas kernels  14.3 us (20%)
    all_to_all x1, waiting for transfers between devices, body(): lax.all_to_all(parted, 'wide', split_axis=0, concat_axis=0, tiled=True)  26.6 us
    all_to_all x1, starting transfers between devices, body(): lax.all_to_all(parted, 'wide', split_axis=0, concat_axis=0, tiled=True)  12.8 us
    ppermute x1, waiting for transfers between devices, body(): after = lax.ppermute(edge, 'wide', [(i, (i - 1) % 64) for i in range(64)])  5.84 us
    ppermute x3, waiting for transfers between devices, body(): lax.ppermute(p, 'chan', [(i, i ^ k) for i in range(4)])  5.7 us
    pallas_call x1, Pallas kernels, body(): call(range_kernel, 'range_filter', shape(64, 32, 128), [pltpu.VMEM((2, 16...  4.46 us
    ppermute x3, starting transfers between devices, body(): lax.ppermute(p, 'chan', [(i, i ^ k) for i in range(4)])  3.95 us
    pallas_call x1, Pallas kernels, body(): call(azimuth_own, 'azimuth_own', (shape(2, 272, 128),) * 2, scratch + [pl...  2.56 us
    pallas_call x1, Pallas kernels, body(): call(functools.partial(azimuth_quarter, 2), 'azimuth_first', (shape(2, 27...  1.85 us
  transfers between devices with their start and end apart: 5, of which 3 were waited for; matrix products, arithmetic and copies ran while one was open for 0% of the time, Pallas kernels for 9%

profile of v8, /device:TPU:26, one launch (start us, length us, event | category | flops | bytes accessed | tf_op | source)
XLA Modules:
  0.0 70.6 jit_solution(7156159025830732570)
XLA Ops:
  0.0 4.5 %range_filter.1 = f32[64,32,128]{2,1,0:T(8,128)} custom-call(f32[2,16,8192]{2,1,0:T(8,128)} %bitcast.3, f32[2,1,512]{2,1,0:T(1,128)} %chirp_hbm.1), custom_call_target="tpu_custom_call" | custom-call | flops 2000000000 | bytes 2097152 | tf_op jit(solution)/shard_map/range_filter/pallas_call | solution.py:282
  4.5 0.0 copy-start.2
  4.5 12.8 %all-to-all-start = ((f32[64,32,128]{2,1,0:T(8,128)}), f32[64,32,128]{2,1,0:T(8,128)S(1)}, u32[]{:S(2)}, u32[]{:S(2)}) async-start(f32[64,32,128]{2,1,0:T(8,128)} %range_filter.1), calls=%async_computation | async-start | bytes 2097152 | tf_op jit(solution)/shard_map/all_to_all | solution.py:289
  17.3 0.0 copy-done.2
  17.3 0.0 copy-start.1
  17.3 0.1 copy.6.offsets_ref
  17.4 0.6 copy-done.1
  17.9 0.0 copy-start
  17.9 0.7 prepare.1
  18.6 26.6 %all-to-all-done.x_ref = f32[64,32,128]{2,1,0:T(8,128)S(1)} async-done(((f32[64,32,128]{2,1,0:T(8,128)}), f32[64,32,128]{2,1,0:T(8,128)S(1)}, u32[]{:S(2)}, u32[]{:S(2)}) %all-to-all-start) | async-done | bytes 1048608 | tf_op jit(solution)/shard_map/all_to_all | solution.py:289
  45.2 0.0 copy-done
  45.2 1.9 %azimuth_first.1 = (f32[2,272,128]{2,1,0:T(8,128)S(1)}, f32[8,128]{1,0:T(8,128)S(1)}) custom-call(f32[64,32,128]{2,1,0:T(8,128)S(1)} %all-to-all-done.x_ref, f32[2,1,1024]{2,1,0:T(1,128)S(1)} %copy-done, f32[32,128]{1,0:T(8,128)S(1)} %bitcast.2), custom_call_target="tpu_custom_call" | custom-call | flops 1000000000 | bytes 1000 | tf_op jit(solution)/shard_map/azimuth_first/pallas_call | solution.py:297
  47.1 2.1 %collective-permute-start = (f32[2,272,128]{2,1,0:T(8,128)S(1)}, f32[2,272,128]{2,1,0:T(8,128)S(1)}, u32[]{:S(2)}, u32[]{:S(2)}) collective-permute-start(f32[2,272,128]{2,1,0:T(8,128)S(1)} %get-tuple-element.22), channel_id=1, source_target_pairs={{0,128},{64,192},{128,0},{192,64},{1,129},{65,193},{129,1},{193,65... | collective-permute-start | bytes 835592 | tf_op jit(solution)/shard_map/ppermute | solution.py:309
  49.2 1.8 %azimuth_second.1 = (f32[2,272,128]{2,1,0:T(8,128)S(1)}, f32[8,128]{1,0:T(8,128)S(1)}) custom-call(f32[64,32,128]{2,1,0:T(8,128)S(1)} %all-to-all-done.x_ref, f32[2,1,1024]{2,1,0:T(1,128)S(1)} %copy-done, f32[8,128]{1,0:T(8,128)S(1)} %get-tuple-element.19.order_ref), custom_call_target="tpu_custom_call" | custom-call | flops 1000 | bytes 1000 | tf_op jit(solution)/shard_map/azimuth_second/pallas_call | solution.py:301
  51.0 0.0 collective-permute-start.1
  51.0 2.6 %azimuth_own.1 = (f32[2,272,128]{2,1,0:T(8,128)S(1)}, f32[2,272,128]{2,1,0:T(8,128)S(1)}) custom-call(f32[64,32,128]{2,1,0:T(8,128)S(1)} %all-to-all-done.x_ref, f32[2,1,1024]{2,1,0:T(1,128)S(1)} %copy-done, f32[8,128]{1,0:T(8,128)S(1)} %get-tuple-element.20.order_ref), custom_call_target="tpu_custom_call" | custom-call | flops 1000 | bytes 1000 | tf_op jit(solution)/shard_map/azimuth_own/pallas_call | solution.py:305
  53.6 1.8 %collective-permute-start.2 = (f32[2,272,128]{2,1,0:T(8,128)S(1)}, f32[2,272,128]{2,1,0:T(8,128)S(1)}, u32[]{:S(2)}, u32[]{:S(2)}) collective-permute-start(f32[2,272,128]{2,1,0:T(8,128)S(1)} %get-tuple-element.24), channel_id=1, source_target_pairs={{0,64},{64,0},{128,192},{192,128},{1,65},{65,1},{129,193},{193,129... | collective-permute-start | bytes 835592 | tf_op jit(solution)/shard_map/ppermute | solution.py:309
  55.5 0.0 collective-permute-done.ya
  55.5 0.1 two_receivers.1.first_ref
  55.5 5.7 %collective-permute-done.1.yb = f32[2,272,128]{2,1,0:T(8,128)S(1)} collective-permute-done((f32[2,272,128]{2,1,0:T(8,128)S(1)}, f32[2,272,128]{2,1,0:T(8,128)S(1)}, u32[]{:S(2)}, u32[]{:S(2)}) %collective-permute-start.1) | collective-permute-done | bytes 278560 | tf_op jit(solution)/shard_map/ppermute | solution.py:309
  61.3 0.0 collective-permute-done.2.y1
  61.3 0.2 edge.1
  61.5 0.6 collective-permute-start.3
  62.2 0.9 %window_sums.1.main_ref = f32[2,512,128]{2,1,0:T(8,128)S(1)} custom-call(f32[4,8,128]{2,1,0:T(8,128)S(1)} %get-tuple-element.17.weight_ref, bf16[2,128,256]{2,1,0:T(8,128)(2,1)S(1)} %get-tuple-element.15.rows_ref, bf16[2,128,128]{2,1,0:T(8,128)(2,1)S(1)} %get-tuple-element.18.near_ref, f32[4,272,128]{2,1,0:T(8,128)S(1)} %three_receivers.1.part_ref, ...), custom_call_target="tpu_custom_call" | custom-call | flops 500000000 | bytes 1048576 | tf_op jit(solution)/shard_map/window_sums/pallas_call | solution.py:320
  63.1 5.8 %collective-permute-done.3.edge_ref = f32[136,128]{1,0:T(8,128)S(1)} collective-permute-done((f32[136,128]{1,0:T(8,128)S(1)}, f32[136,128]{1,0:T(8,128)S(1)}, u32[]{:S(2)}, u32[]{:S(2)}) %collective-permute-start.3) | collective-permute-done | bytes 69664 | tf_op jit(solution)/shard_map/ppermute | solution.py:319
  68.9 1.7 %coherence.1 = f32[2,256,128]{2,1,0:T(8,128)} custom-call(bf16[2,128,256]{2,1,0:T(8,128)(2,1)S(1)} %get-tuple-element.15.rows_ref, bf16[2,128,128]{2,1,0:T(8,128)(2,1)S(1)} %get-tuple-element.16.far_ref, f32[2,512,128]{2,1,0:T(8,128)S(1)} %window_sums.1.main_ref, f32[136,128]{1,0:T(8,128)S(1)} %collective-permute-done.3.edge_ref), custom_call_target="tpu_custom_call" | custom-call | flops 500000000 | bytes 1048576 | tf_op jit(solution)/shard_map/coherence/pallas_call | solution.py:324
  (1 shorter events, 0.0 us)
Async XLA Ops:
  4.5 12.8 %copy-start.2 = (s32[8,2]{0,1:T(2,128)S(1)}, s32[8,2]{0,1:T(2,128)}, u32[]{:S(2)}) copy-start(s32[8,2]{0,1:T(2,128)} %param.9) | copy-start | bytes 196
  4.5 40.7 %all-to-all-start = ((f32[64,32,128]{2,1,0:T(8,128)}), f32[64,32,128]{2,1,0:T(8,128)S(1)}, u32[]{:S(2)}, u32[]{:S(2)}) async-start(f32[64,32,128]{2,1,0:T(8,128)} %range_filter.1), calls=%async_computation | async-start | bytes 2097152 | tf_op jit(solution)/shard_map/all_to_all | solution.py:289
  17.3 0.7 copy-start.1
  17.9 27.3 %copy-start = (f32[2,1,1024]{2,1,0:T(1,128)S(1)}, f32[2,1,1024]{2,1,0:T(1,128)}, u32[]{:S(2)}) copy-start(f32[2,1,1024]{2,1,0:T(1,128)} %taps_ref.5) | copy-start | bytes 24580
  47.1 8.4 %collective-permute-start = (f32[2,272,128]{2,1,0:T(8,128)S(1)}, f32[2,272,128]{2,1,0:T(8,128)S(1)}, u32[]{:S(2)}, u32[]{:S(2)}) collective-permute-start(f32[2,272,128]{2,1,0:T(8,128)S(1)} %get-tuple-element.22), channel_id=1, source_target_pairs={{0,128},{64,192},{128,0},{192,64},{1,129},{65,193},{129,1},{193,65... | collective-permute-start | bytes 835592 | tf_op jit(solution)/shard_map/ppermute | solution.py:309
  51.0 10.2 %collective-permute-start.1 = (f32[2,272,128]{2,1,0:T(8,128)S(1)}, f32[2,272,128]{2,1,0:T(8,128)S(1)}, u32[]{:S(2)}, u32[]{:S(2)}) collective-permute-start(f32[2,272,128]{2,1,0:T(8,128)S(1)} %get-tuple-element.23), channel_id=1, source_target_pairs={{0,192},{64,128},{128,64},{192,0},{1,193},{65,129},{129,65},{193,1... | collective-permute-start | bytes 835592 | tf_op jit(solution)/shard_map/ppermute | solution.py:309
  53.6 7.7 %collective-permute-start.2 = (f32[2,272,128]{2,1,0:T(8,128)S(1)}, f32[2,272,128]{2,1,0:T(8,128)S(1)}, u32[]{:S(2)}, u32[]{:S(2)}) collective-permute-start(f32[2,272,128]{2,1,0:T(8,128)S(1)} %get-tuple-element.24), channel_id=1, source_target_pairs={{0,64},{64,0},{128,192},{192,128},{1,65},{65,1},{129,193},{193,129... | collective-permute-start | bytes 835592 | tf_op jit(solution)/shard_map/ppermute | solution.py:309
  61.5 7.4 %collective-permute-start.3 = (f32[136,128]{1,0:T(8,128)S(1)}, f32[136,128]{1,0:T(8,128)S(1)}, u32[]{:S(2)}, u32[]{:S(2)}) collective-permute-start(f32[136,128]{1,0:T(8,128)S(1)} %edge.1), channel_id=1, source_target_pairs={{0,63},{1,0},{2,1},{3,2},{4,3},{5,4},{6,5},{7,6},{8,7},{9,8},{10,9... | collective-permute-start | bytes 208904 | tf_op jit(solution)/shard_map/ppermute | solution.py:319

commit v9 on v8

--- a/solution.py
+++ b/solution.py
@@ -142,11 +142,19 @@
     return g[0][:, 0:128] - g[1][:, 128:256], g[0][:, 128:256] + g[1][:, 0:128]
 
 
-def azimuth_quarter(k, x_ref, taps_ref, order_ref, out_ref, done_ref, t_hi, t_lo, x_hi, x_lo):
+def first_quarter(x_ref, taps_ref, order_ref, out_ref, done_ref, t_hi, t_lo, x_hi, x_lo):
     done_ref[...] = jnp.zeros((8, 128), F32)
     build_taps(taps_ref, t_hi, t_lo)
     split_pulses(x_ref, x_hi, x_lo)
-    taps = (t_hi, t_lo, x_hi, x_lo)
+    azimuth_quarter(2, (t_hi, t_lo, x_hi, x_lo), out_ref)
+
+
+def second_quarter(order_ref, t_hi, t_lo, x_hi, x_lo, out_ref, done_ref):
+    done_ref[...] = jnp.zeros((8, 128), F32)
+    azimuth_quarter(3, (t_hi, t_lo, x_hi, x_lo), out_ref)
+
+
+def azimuth_quarter(k, taps, out_ref):
     me = lax.axis_index("chan")
     for q in range(4):
         @pl.when((me ^ k) == q)
@@ -165,9 +173,7 @@
                     out_ref[part, 264:272, :] = jnp.zeros((8, 128), F32)
 
 
-def azimuth_own(x_ref, taps_ref, order_ref, o0, o1, t_hi, t_lo, x_hi, x_lo, y_ref):
-    build_taps(taps_ref, t_hi, t_lo)
-    split_pulses(x_ref, x_hi, x_lo)
+def azimuth_own(order_ref, t_hi, t_lo, x_hi, x_lo, o0, o1, y_ref):
     me = lax.axis_index("chan")
     for half in range(2):
         @pl.when(me // 2 == half)
@@ -293,19 +299,18 @@
         2, smem=(0, 1), flops=1_000_000_000, moved=1 << 20,
     )(pairing, offsets)
     order = weight.reshape(32, 128)
-    scratch = [pltpu.VMEM((2, 272, 1280), BF16)] * 2 + [pltpu.VMEM((1024, 256), BF16)] * 2
-    pa, order = call(
-        functools.partial(azimuth_quarter, 2), "azimuth_first", (shape(2, 272, 128), shape(8, 128)), scratch,
-        3, flops=1_000_000_000, moved=1000,
+    pa, order, *taps = call(
+        first_quarter, "azimuth_first",
+        (shape(2, 272, 128), shape(8, 128)) + (shape(2, 272, 1280, dtype=BF16),) * 2 + (shape(1024, 256, dtype=BF16),) * 2,
+        [], 3, flops=1_000_000_000, moved=1000,
     )(turned, taps, order)
     pb, order = call(
-        functools.partial(azimuth_quarter, 3), "azimuth_second", (shape(2, 272, 128), shape(8, 128)), scratch,
-        3, flops=1000, moved=1000,
-    )(turned, taps, order)
+        second_quarter, "azimuth_second", (shape(2, 272, 128), shape(8, 128)), [], 5, flops=1000, moved=1000,
+    )(order, *taps)
     p0, p1 = call(
-        azimuth_own, "azimuth_own", (shape(2, 272, 128),) * 2, scratch + [pltpu.VMEM((2, 2, 272, 128), F32)],
-        3, flops=1000, moved=1000,
-    )(turned, taps, order)
+        azimuth_own, "azimuth_own", (shape(2, 272, 128),) * 2, [pltpu.VMEM((2, 2, 272, 128), F32)],
+        5, flops=1000, moved=1000,
+    )(order, *taps)
     ya, yb, y1 = [lax.ppermute(p, "chan", [(i, i ^ k) for i in range(4)]) for k, p in ((2, pa), (3, pb), (1, p1))]
     part = call(
         first_sums_kernel, "two_receivers", shape(4, 272, 128), [], 3, flops=FIRST_COST, moved=1000,

time: 70.9 us -> 70.6 us (level)
  Pallas kernels: 14.3 us -> 12.8 us
  waiting for transfers between devices: 38.1 us -> 39.4 us
    pallas_call x3, Pallas kernels: 6.25 us -> 4.75 us  [the longest x1 1.85 us: body(): call(first_quarter, 'azimuth_first', (shape(2, 272, 128), shape(8, 128))...]
    ppermute x3, waiting for transfers between devices: 5.7 us -> 6.71 us  [body(): lax.ppermute(p, 'chan', [(i, i ^ k) for i in range(4)])]
  transfers between devices with their start and end apart: 5 -> 5, of which waited for: 3 -> 4; matrix products, arithmetic and copies ran while one was open for 0% -> 0% of each run, Pallas kernels for 9% -> 7%
where the time goes in v9:
time: 70.6 us; the launch traced here: 70.3 us
  waiting for transfers between devices  39.4 us (56%)
  starting transfers between devices  17.9 us (25%)
  Pallas kernels  12.8 us (18%)
    all_to_all x1, waiting for transfers between devices, body(): lax.all_to_all(parted, 'wide', split_axis=0, concat_axis=0, tiled=True)  27.2 us
    all_to_all x1, starting transfers between devices, body(): lax.all_to_all(parted, 'wide', split_axis=0, concat_axis=0, tiled=True)  12.8 us
    ppermute x3, waiting for transfers between devices, body(): lax.ppermute(p, 'chan', [(i, i ^ k) for i in range(4)])  6.71 us
    ppermute x1, waiting for transfers between devices, body(): after = lax.ppermute(edge, 'wide', [(i, (i - 1) % 64) for i in range(64)])  5.54 us
    pallas_call x1, Pallas kernels, body(): call(range_kernel, 'range_filter', shape(64, 32, 128), [pltpu.VMEM((2, 16...  4.46 us
    ppermute x3, starting transfers between devices, body(): lax.ppermute(p, 'chan', [(i, i ^ k) for i in range(4)])  4.14 us
    pallas_call x1, Pallas kernels, body(): call(first_quarter, 'azimuth_first', (shape(2, 272, 128), shape(8, 128))...  1.85 us
    pallas_call x1, Pallas kernels, body(): call(azimuth_own, 'azimuth_own', (shape(2, 272, 128),) * 2, [pltpu.VMEM((...  1.73 us
  transfers between devices with their start and end apart: 5, of which 4 were waited for; matrix products, arithmetic and copies ran while one was open for 0% of the time, Pallas kernels for 7%

profile of v9, /device:TPU:26, one launch (start us, length us, event | category | flops | bytes accessed | tf_op | source)
XLA Modules:
  0.0 70.3 jit_solution(17984947770927225584)
XLA Ops:
  0.0 4.5 %range_filter.1 = f32[64,32,128]{2,1,0:T(8,128)} custom-call(f32[2,16,8192]{2,1,0:T(8,128)} %bitcast.3, f32[2,1,512]{2,1,0:T(1,128)} %chirp_hbm.1), custom_call_target="tpu_custom_call" | custom-call | flops 2000000000 | bytes 2097152 | tf_op jit(solution)/shard_map/range_filter/pallas_call | solution.py:288
  4.5 0.0 copy-start.2
  4.5 0.0 copy-start.1
  4.5 12.8 %all-to-all-start = ((f32[64,32,128]{2,1,0:T(8,128)}), f32[64,32,128]{2,1,0:T(8,128)S(1)}, u32[]{:S(2)}, u32[]{:S(2)}) async-start(f32[64,32,128]{2,1,0:T(8,128)} %range_filter.1), calls=%async_computation | async-start | bytes 2097152 | tf_op jit(solution)/shard_map/all_to_all | solution.py:295
  17.3 0.0 copy-done.2
  17.3 0.1 copy.6.offsets_ref
  17.4 0.0 copy-done.1
  17.4 0.0 copy-start
  17.4 0.7 prepare.1
  18.1 27.2 %all-to-all-done.x_ref = f32[64,32,128]{2,1,0:T(8,128)S(1)} async-done(((f32[64,32,128]{2,1,0:T(8,128)}), f32[64,32,128]{2,1,0:T(8,128)S(1)}, u32[]{:S(2)}, u32[]{:S(2)}) %all-to-all-start) | async-done | bytes 1048608 | tf_op jit(solution)/shard_map/all_to_all | solution.py:295
  45.2 0.0 copy-done
  45.2 1.9 %azimuth_first.1 = (f32[2,272,128]{2,1,0:T(8,128)S(1)}, f32[8,128]{1,0:T(8,128)S(1)}, bf16[2,272,1280]{2,1,0:T(8,128)(2,1)S(1)}, bf16[2,272,1280]{2,1,0:T(8,128)...) custom-call(f32[64,32,128]{2,1,0:T(8,128)S(1)} %all-to-all-done.x_ref, ...), custom_call_target="tpu_custom_call" | custom-call | flops 1000000000 | bytes 1000 | tf_op jit(solution)/shard_map/azimuth_first/pallas_call | solution.py:302
  47.1 2.1 %collective-permute-start = (f32[2,272,128]{2,1,0:T(8,128)S(1)}, f32[2,272,128]{2,1,0:T(8,128)S(1)}, u32[]{:S(2)}, u32[]{:S(2)}) collective-permute-start(f32[2,272,128]{2,1,0:T(8,128)S(1)} %get-tuple-element.30), channel_id=1, source_target_pairs={{0,128},{64,192},{128,0},{192,64},{1,129},{65,193},{129,1},{193,65... | collective-permute-start | bytes 835592 | tf_op jit(solution)/shard_map/ppermute | solution.py:314
  49.2 1.2 %azimuth_second.1 = (f32[2,272,128]{2,1,0:T(8,128)S(1)}, f32[8,128]{1,0:T(8,128)S(1)}) custom-call(f32[8,128]{1,0:T(8,128)S(1)} %get-tuple-element.23.order_ref, bf16[2,272,1280]{2,1,0:T(8,128)(2,1)S(1)} %get-tuple-element.24.t_hi, bf16[2,272,1280]{2,1,0:T(8,128)(2,1)S(1)} %get-tuple-element.25.t_lo, bf16[1024,256]{1,0:T(8,128)(2,1)S(1)} %get-tuple-element.26.x_hi, ...), custom_call_target="tpu_custom_call" | custom-call | flops 1000 | bytes 1000 | tf_op jit(solution)/shard_map/azimuth_second/pallas_call | solution.py:307
  50.4 0.0 collective-permute-start.1
  50.4 1.7 %azimuth_own.1 = (f32[2,272,128]{2,1,0:T(8,128)S(1)}, f32[2,272,128]{2,1,0:T(8,128)S(1)}) custom-call(f32[8,128]{1,0:T(8,128)S(1)} %get-tuple-element.28.order_ref, bf16[2,272,1280]{2,1,0:T(8,128)(2,1)S(1)} %get-tuple-element.24.t_hi, bf16[2,272,1280]{2,1,0:T(8,128)(2,1)S(1)} %get-tuple-element.25.t_lo, bf16[1024,256]{1,0:T(8,128)(2,1)S(1)} %get-tuple-element.26.x_hi, ...), custom_call_target="tpu_custom_call" | custom-call | flops 1000 | bytes 1000 | tf_op jit(solution)/shard_map/azimuth_own/pallas_call | solution.py:310
  52.1 2.0 %collective-permute-start.2 = (f32[2,272,128]{2,1,0:T(8,128)S(1)}, f32[2,272,128]{2,1,0:T(8,128)S(1)}, u32[]{:S(2)}, u32[]{:S(2)}) collective-permute-start(f32[2,272,128]{2,1,0:T(8,128)S(1)} %get-tuple-element.32), channel_id=1, source_target_pairs={{0,64},{64,0},{128,192},{192,128},{1,65},{65,1},{129,193},{193,129... | collective-permute-start | bytes 835592 | tf_op jit(solution)/shard_map/ppermute | solution.py:314
  54.1 1.4 %collective-permute-done.ya = f32[2,272,128]{2,1,0:T(8,128)S(1)} collective-permute-done((f32[2,272,128]{2,1,0:T(8,128)S(1)}, f32[2,272,128]{2,1,0:T(8,128)S(1)}, u32[]{:S(2)}, u32[]{:S(2)}) %collective-permute-start) | collective-permute-done | bytes 278560 | tf_op jit(solution)/shard_map/ppermute | solution.py:314
  55.6 0.1 two_receivers.1.first_ref
  55.6 5.3 %collective-permute-done.1.yb = f32[2,272,128]{2,1,0:T(8,128)S(1)} collective-permute-done((f32[2,272,128]{2,1,0:T(8,128)S(1)}, f32[2,272,128]{2,1,0:T(8,128)S(1)}, u32[]{:S(2)}, u32[]{:S(2)}) %collective-permute-start.1) | collective-permute-done | bytes 278560 | tf_op jit(solution)/shard_map/ppermute | solution.py:314
  61.0 0.0 collective-permute-done.2.y1
  61.0 0.2 edge.1
  61.2 0.9 %collective-permute-start.3 = (f32[136,128]{1,0:T(8,128)S(1)}, f32[136,128]{1,0:T(8,128)S(1)}, u32[]{:S(2)}, u32[]{:S(2)}) collective-permute-start(f32[136,128]{1,0:T(8,128)S(1)} %edge.1), channel_id=1, source_target_pairs={{0,63},{1,0},{2,1},{3,2},{4,3},{5,4},{6,5},{7,6},{8,7},{9,8},{10,9... | collective-permute-start | bytes 208904 | tf_op jit(solution)/shard_map/ppermute | solution.py:324
  62.2 0.9 %window_sums.1.main_ref = f32[2,512,128]{2,1,0:T(8,128)S(1)} custom-call(f32[4,8,128]{2,1,0:T(8,128)S(1)} %get-tuple-element.21.weight_ref, bf16[2,128,256]{2,1,0:T(8,128)(2,1)S(1)} %get-tuple-element.19.rows_ref, bf16[2,128,128]{2,1,0:T(8,128)(2,1)S(1)} %get-tuple-element.22.near_ref, f32[4,272,128]{2,1,0:T(8,128)S(1)} %three_receivers.1.part_ref, ...), custom_call_target="tpu_custom_call" | custom-call | flops 500000000 | bytes 1048576 | tf_op jit(solution)/shard_map/window_sums/pallas_call | solution.py:325
  63.1 5.5 %collective-permute-done.3.edge_ref = f32[136,128]{1,0:T(8,128)S(1)} collective-permute-done((f32[136,128]{1,0:T(8,128)S(1)}, f32[136,128]{1,0:T(8,128)S(1)}, u32[]{:S(2)}, u32[]{:S(2)}) %collective-permute-start.3) | collective-permute-done | bytes 69664 | tf_op jit(solution)/shard_map/ppermute | solution.py:324
  68.6 1.7 %coherence.1 = f32[2,256,128]{2,1,0:T(8,128)} custom-call(bf16[2,128,256]{2,1,0:T(8,128)(2,1)S(1)} %get-tuple-element.19.rows_ref, bf16[2,128,128]{2,1,0:T(8,128)(2,1)S(1)} %get-tuple-element.20.far_ref, f32[2,512,128]{2,1,0:T(8,128)S(1)} %window_sums.1.main_ref, f32[136,128]{1,0:T(8,128)S(1)} %collective-permute-done.3.edge_ref), custom_call_target="tpu_custom_call" | custom-call | flops 500000000 | bytes 1048576 | tf_op jit(solution)/shard_map/coherence/pallas_call | solution.py:329
  (1 shorter events, 0.0 us)
Async XLA Ops:
  4.5 12.8 %copy-start.2 = (s32[8,2]{0,1:T(2,128)S(1)}, s32[8,2]{0,1:T(2,128)}, u32[]{:S(2)}) copy-start(s32[8,2]{0,1:T(2,128)} %param.9) | copy-start | bytes 196
  4.5 12.9 %copy-start.1 = (s32[4]{0:T(128)S(1)}, s32[4]{0:T(128)}, u32[]{:S(2)}) copy-start(s32[4]{0:T(128)} %pairing_ref.1) | copy-start | bytes 52
  4.5 40.7 %all-to-all-start = ((f32[64,32,128]{2,1,0:T(8,128)}), f32[64,32,128]{2,1,0:T(8,128)S(1)}, u32[]{:S(2)}, u32[]{:S(2)}) async-start(f32[64,32,128]{2,1,0:T(8,128)} %range_filter.1), calls=%async_computation | async-start | bytes 2097152 | tf_op jit(solution)/shard_map/all_to_all | solution.py:295
  17.4 27.9 %copy-start = (f32[2,1,1024]{2,1,0:T(1,128)S(1)}, f32[2,1,1024]{2,1,0:T(1,128)}, u32[]{:S(2)}) copy-start(f32[2,1,1024]{2,1,0:T(1,128)} %taps_ref.1) | copy-start | bytes 24580
  47.1 8.5 %collective-permute-start = (f32[2,272,128]{2,1,0:T(8,128)S(1)}, f32[2,272,128]{2,1,0:T(8,128)S(1)}, u32[]{:S(2)}, u32[]{:S(2)}) collective-permute-start(f32[2,272,128]{2,1,0:T(8,128)S(1)} %get-tuple-element.30), channel_id=1, source_target_pairs={{0,128},{64,192},{128,0},{192,64},{1,129},{65,193},{129,1},{193,65... | collective-permute-start | bytes 835592 | tf_op jit(solution)/shard_map/ppermute | solution.py:314
  50.4 10.5 %collective-permute-start.1 = (f32[2,272,128]{2,1,0:T(8,128)S(1)}, f32[2,272,128]{2,1,0:T(8,128)S(1)}, u32[]{:S(2)}, u32[]{:S(2)}) collective-permute-start(f32[2,272,128]{2,1,0:T(8,128)S(1)} %get-tuple-element.31), channel_id=1, source_target_pairs={{0,192},{64,128},{128,64},{192,0},{1,193},{65,129},{129,65},{193,1... | collective-permute-start | bytes 835592 | tf_op jit(solution)/shard_map/ppermute | solution.py:314
  52.1 8.9 %collective-permute-start.2 = (f32[2,272,128]{2,1,0:T(8,128)S(1)}, f32[2,272,128]{2,1,0:T(8,128)S(1)}, u32[]{:S(2)}, u32[]{:S(2)}) collective-permute-start(f32[2,272,128]{2,1,0:T(8,128)S(1)} %get-tuple-element.32), channel_id=1, source_target_pairs={{0,64},{64,0},{128,192},{192,128},{1,65},{65,1},{129,193},{193,129... | collective-permute-start | bytes 835592 | tf_op jit(solution)/shard_map/ppermute | solution.py:314
  61.2 7.4 %collective-permute-start.3 = (f32[136,128]{1,0:T(8,128)S(1)}, f32[136,128]{1,0:T(8,128)S(1)}, u32[]{:S(2)}, u32[]{:S(2)}) collective-permute-start(f32[136,128]{1,0:T(8,128)S(1)} %edge.1), channel_id=1, source_target_pairs={{0,63},{1,0},{2,1},{3,2},{4,3},{5,4},{6,5},{7,6},{8,7},{9,8},{10,9... | collective-permute-start | bytes 208904 | tf_op jit(solution)/shard_map/ppermute | solution.py:324

commit v10 on v9

--- a/solution.py
+++ b/solution.py
@@ -11,6 +11,7 @@
 REACH = 2 * RADIUS
 XOR_ORDER = (0, 2, 3, 1)
 FIRST = 1
+COLUMN = (256, 0)
 FIRST_COST = 1_000
 F32 = jnp.float32
 BF16 = jnp.bfloat16
@@ -96,8 +97,20 @@
         copy.wait()
 
 
-def prepare_kernel(pairing_ref, offsets_ref, weight_ref, rows_ref, near_ref, far_ref):
+def taps_rows(taps):
+    return toeplitz(taps, 272, 1280, 1280 - REACH)
+
+
+def prepare_kernel(pairing_ref, offsets_ref, taps_ref, t_ref, weight_ref, rows_ref, near_ref, far_ref):
     me = lax.axis_index("chan")
+    for part in range(2):
+        whole = taps_rows(taps_ref[part])
+        for half in range(2):
+            @pl.when(me // 2 != half)
+            def _(half=half, part=part, whole=whole):
+                hi, lo = split(whole[:, COLUMN[half]:COLUMN[half] + 1024])
+                t_ref[part] = hi
+                t_ref[2 + part] = lo
     first = lax.axis_index("wide") == 0
     final = lax.axis_index("wide") == lax.axis_size("wide") - 1
     for i, k in enumerate(XOR_ORDER):
@@ -119,11 +132,11 @@
         far_ref[g] = jnp.where(far, 1.0, 0.0).astype(BF16)
 
 
-def build_taps(taps_ref, t_hi, t_lo):
-    for part in range(2):
-        hi, lo = split(toeplitz(taps_ref[part], 272, 1280, 1280 - REACH))
-        t_hi[part] = hi
-        t_lo[part] = lo
+def build_taps(taps_ref, t_ref):
+    for part in range(2):
+        hi, lo = split(taps_rows(taps_ref[part]))
+        t_ref[part] = hi
+        t_ref[2 + part] = lo
 
 
 def split_pulses(x_ref, x_hi, x_lo):
@@ -133,25 +146,24 @@
         x_lo[:, 128 * part:128 * part + 128] = lo
 
 
-def quarter_rows(q, picked, t_hi, t_lo, x_hi, x_lo):
+def quarter_rows(q, picked, t_ref, x_hi, x_lo, column=0):
     first, last = max(q - 2, 0), min(q + 2, 3)
-    cols = slice(256 * (first - q + 2), 256 * (last - q + 3))
+    cols = slice(256 * (first - q + 2) - column, 256 * (last - q + 3) - column)
     rows = slice(256 * first, 256 * last + 256)
-    t = [ref[part, picked, cols] for ref in (t_hi, t_lo) for part in range(2)]
+    t = [t_ref[i, picked, cols] for i in range(4)]
     g = [dot_nn(t[i], x_hi[rows, :]) + dot_nn(t[i], x_lo[rows, :]) + dot_nn(t[2 + i], x_hi[rows, :]) for i in range(2)]
     return g[0][:, 0:128] - g[1][:, 128:256], g[0][:, 128:256] + g[1][:, 0:128]
 
 
-def first_quarter(x_ref, taps_ref, order_ref, out_ref, done_ref, t_hi, t_lo, x_hi, x_lo):
+def first_quarter(x_ref, t_ref, order_ref, out_ref, done_ref, x_hi, x_lo):
     done_ref[...] = jnp.zeros((8, 128), F32)
-    build_taps(taps_ref, t_hi, t_lo)
     split_pulses(x_ref, x_hi, x_lo)
-    azimuth_quarter(2, (t_hi, t_lo, x_hi, x_lo), out_ref)
-
-
-def second_quarter(order_ref, t_hi, t_lo, x_hi, x_lo, out_ref, done_ref):
+    azimuth_quarter(2, (t_ref, x_hi, x_lo), out_ref)
+
+
+def second_quarter(order_ref, t_ref, x_hi, x_lo, out_ref, done_ref):
     done_ref[...] = jnp.zeros((8, 128), F32)
-    azimuth_quarter(3, (t_hi, t_lo, x_hi, x_lo), out_ref)
+    azimuth_quarter(3, (t_ref, x_hi, x_lo), out_ref)
 
 
 def azimuth_quarter(k, taps, out_ref):
@@ -159,8 +171,8 @@
     for q in range(4):
         @pl.when((me ^ k) == q)
         def _(q=q):
-            own = quarter_rows(q, slice(0, 272), *taps)
-            shared = quarter_rows(q ^ 1, slice(256, 272) if q % 2 else slice(0, 16), *taps)
+            own = quarter_rows(q, slice(0, 272), *taps, COLUMN[q // 2])
+            shared = quarter_rows(q ^ 1, slice(256, 272) if q % 2 else slice(0, 16), *taps, COLUMN[q // 2])
             for part in range(2):
                 out_ref[part] = own[part]
                 if q % 2:
@@ -173,13 +185,14 @@
                     out_ref[part, 264:272, :] = jnp.zeros((8, 128), F32)
 
 
-def azimuth_own(order_ref, t_hi, t_lo, x_hi, x_lo, o0, o1, y_ref):
+def azimuth_own(order_ref, taps_ref, x_hi, x_lo, o0, o1, t_ref, y_ref):
+    build_taps(taps_ref, t_ref)
     me = lax.axis_index("chan")
     for half in range(2):
         @pl.when(me // 2 == half)
         def _(half=half):
             for i in range(2):
-                for part, value in enumerate(quarter_rows(2 * half + i, slice(0, 272), t_hi, t_lo, x_hi, x_lo)):
+                for part, value in enumerate(quarter_rows(2 * half + i, slice(0, 272), t_ref, x_hi, x_lo)):
                     y_ref[i, part] = value
             for part in range(2):
                 y_ref[0, part, 264:272, :] = y_ref[1, part, 8:16, :]
@@ -293,24 +306,25 @@
         2, hbm=(0, 1), flops=2_000_000_000, moved=2 << 20, vmem=60 << 20, out=pltpu.HBM,
     )(signal, chirp)
     turned = lax.all_to_all(parted, "wide", split_axis=0, concat_axis=0, tiled=True)
-    weight, rows, near, far = call(
+    t, weight, rows, near, far = call(
         prepare_kernel, "prepare",
-        (shape(4, 8, 128), shape(2, 128, 256, dtype=BF16)) + (shape(2, 128, 128, dtype=BF16),) * 2, [],
-        2, smem=(0, 1), flops=1_000_000_000, moved=1 << 20,
-    )(pairing, offsets)
+        (shape(4, 272, 1024, dtype=BF16), shape(4, 8, 128), shape(2, 128, 256, dtype=BF16))
+        + (shape(2, 128, 128, dtype=BF16),) * 2, [],
+        3, smem=(0, 1), flops=1_000_000_000, moved=1 << 20,
+    )(pairing, offsets, taps)
     order = weight.reshape(32, 128)
-    pa, order, *taps = call(
-        first_quarter, "azimuth_first",
-        (shape(2, 272, 128), shape(8, 128)) + (shape(2, 272, 1280, dtype=BF16),) * 2 + (shape(1024, 256, dtype=BF16),) * 2,
+    pa, order, *pulses = call(
+        first_quarter, "azimuth_first", (shape(2, 272, 128), shape(8, 128)) + (shape(1024, 256, dtype=BF16),) * 2,
         [], 3, flops=1_000_000_000, moved=1000,
-    )(turned, taps, order)
+    )(turned, t, order)
     pb, order = call(
-        second_quarter, "azimuth_second", (shape(2, 272, 128), shape(8, 128)), [], 5, flops=1000, moved=1000,
-    )(order, *taps)
+        second_quarter, "azimuth_second", (shape(2, 272, 128), shape(8, 128)), [], 4, flops=1000, moved=1000,
+    )(order, t, *pulses)
     p0, p1 = call(
-        azimuth_own, "azimuth_own", (shape(2, 272, 128),) * 2, [pltpu.VMEM((2, 2, 272, 128), F32)],
-        5, flops=1000, moved=1000,
-    )(order, *taps)
+        azimuth_own, "azimuth_own", (shape(2, 272, 128),) * 2,
+        [pltpu.VMEM((4, 272, 1280), BF16), pltpu.VMEM((2, 2, 272, 128), F32)],
+        4, flops=1000, moved=1000,
+    )(order, taps, *pulses)
     ya, yb, y1 = [lax.ppermute(p, "chan", [(i, i ^ k) for i in range(4)]) for k, p in ((2, pa), (3, pb), (1, p1))]
     part = call(
         first_sums_kernel, "two_receivers", shape(4, 272, 128), [], 3, flops=FIRST_COST, moved=1000,

time: 70.6 us -> 70.2 us (level)
  waiting for transfers between devices: 39.4 us -> 37.8 us
  Pallas kernels: 12.8 us -> 13.7 us
    all_to_all x1, waiting for transfers between devices: 27.2 us -> 25.9 us  [body(): lax.all_to_all(parted, 'wide', split_axis=0, concat_axis=0, tiled=True)]
  transfers between devices with their start and end apart: 5 -> 5, of which waited for: 4 -> 4; matrix products, arithmetic and copies ran while one was open for 0% -> 0% of each run, Pallas kernels for 7% -> 8%
where the time goes in v10:
time: 70.2 us; the launch traced here: 70 us
  waiting for transfers between devices  37.8 us (54%)
  starting transfers between devices  17.6 us (25%)
  Pallas kernels  13.7 us (20%)
  local copies, waits for them, and re-layouts  0.72 us (1%)
    all_to_all x1, waiting for transfers between devices, body(): lax.all_to_all(parted, 'wide', split_axis=0, concat_axis=0, tiled=True)  25.9 us
    all_to_all x1, starting transfers between devices, body(): lax.all_to_all(parted, 'wide', split_axis=0, concat_axis=0, tiled=True)  12.8 us
    ppermute x3, waiting for transfers between devices, body(): lax.ppermute(p, 'chan', [(i, i ^ k) for i in range(4)])  6.37 us
    ppermute x1, waiting for transfers between devices, body(): after = lax.ppermute(edge, 'wide', [(i, (i - 1) % 64) for i in range(64)])  5.58 us
    pallas_call x1, Pallas kernels, body(): call(range_kernel, 'range_filter', shape(64, 32, 128), [pltpu.VMEM((2, 16...  4.52 us
    ppermute x3, starting transfers between devices, body(): lax.ppermute(p, 'chan', [(i, i ^ k) for i in range(4)])  3.95 us
    pallas_call x1, Pallas kernels, body(): call(azimuth_own, 'azimuth_own', (shape(2, 272, 128),) * 2, [pltpu.VMEM((...  2.27 us
    pallas_call x1, Pallas kernels, body(): call(coherence_kernel, 'coherence', shape(2, 256, 128), [pltpu.VMEM((384,...  1.66 us
  transfers between devices with their start and end apart: 5, of which 4 were waited for; matrix products, arithmetic and copies ran while one was open for 0% of the time, Pallas kernels for 8%

profile of v10, /device:TPU:26, one launch (start us, length us, event | category | flops | bytes accessed | tf_op | source)
XLA Modules:
  0.0 70.0 jit_solution(12383062570690098531)
XLA Ops:
  0.0 0.0 copy-start.4
  0.0 0.0 copy-start
  0.0 0.0 copy-start.1
  0.0 4.5 %range_filter.1 = f32[64,32,128]{2,1,0:T(8,128)} custom-call(f32[2,16,8192]{2,1,0:T(8,128)} %bitcast.3, f32[2,1,512]{2,1,0:T(1,128)} %chirp_hbm.1), custom_call_target="tpu_custom_call" | custom-call | flops 2000000000 | bytes 2097152 | tf_op jit(solution)/shard_map/range_filter/pallas_call | solution.py:301
  4.5 12.8 %all-to-all-start = ((f32[64,32,128]{2,1,0:T(8,128)}), f32[64,32,128]{2,1,0:T(8,128)S(1)}, u32[]{:S(2)}, u32[]{:S(2)}) async-start(f32[64,32,128]{2,1,0:T(8,128)} %range_filter.1), calls=%async_computation | async-start | bytes 2097152 | tf_op jit(solution)/shard_map/all_to_all | solution.py:308
  17.3 0.0 copy-done.4
  17.3 0.1 copy.6.offsets_ref
  17.4 0.0 copy-done
  17.4 0.0 copy-done.1
  17.4 1.4 %prepare.1 = (bf16[4,272,1024]{2,1,0:T(8,128)(2,1)S(1)}, f32[4,8,128]{2,1,0:T(8,128)S(1)}, bf16[2,128,256]{2,1,0:T(8,128)(2,1)S(1)}, bf16[2,128,128]{2,1,0:T(8,128)(2,1)S(1)}, bf16[2,128,128]{2,1,0:T(8,128)(2,1)S(1)}) custom-call(s32[4]{0:T(128)S(1)} %copy-done.1, s32[8,2]{1,0:T(8,128)S(1)} %copy.6.offsets_ref, f32[2,1,1024]{2,1,0:T(1,128)S(1)} %copy-done), custom_call_target="tpu_custom_call" | custom-call | flops 1000000000 | bytes 1048576 | tf_op jit(solution)/shard_map/prepare/pallas_call | solution.py:309
  18.8 0.0 copy-start.2
  18.8 0.6 copy-done.2
  19.4 25.9 %all-to-all-done.x_ref = f32[64,32,128]{2,1,0:T(8,128)S(1)} async-done(((f32[64,32,128]{2,1,0:T(8,128)}), f32[64,32,128]{2,1,0:T(8,128)S(1)}, u32[]{:S(2)}, u32[]{:S(2)}) %all-to-all-start) | async-done | bytes 1048608 | tf_op jit(solution)/shard_map/all_to_all | solution.py:308
  45.3 1.4 %azimuth_first.1 = (f32[2,272,128]{2,1,0:T(8,128)S(1)}, f32[8,128]{1,0:T(8,128)S(1)}, bf16[1024,256]{1,0:T(8,128)(2,1)S(1)}, bf16[1024,256]{1,0:T(8,128)(2,1)S(1)}) custom-call(f32[64,32,128]{2,1,0:T(8,128)S(1)} %all-to-all-done.x_ref, bf16[4,272,1024]{2,1,0:T(8,128)(2,1)S(1)} %get-tuple-element.22.t_ref, f32[32,128]{1,0:T(8,128)S(1)} %bitcast.2), custom_call_target="tpu_custom_call" | custom-call | flops 1000000000 | bytes 1000 | tf_op jit(solution)/shard_map/azimuth_first/pallas_call | solution.py:316
  46.7 2.1 %collective-permute-start = (f32[2,272,128]{2,1,0:T(8,128)S(1)}, f32[2,272,128]{2,1,0:T(8,128)S(1)}, u32[]{:S(2)}, u32[]{:S(2)}) collective-permute-start(f32[2,272,128]{2,1,0:T(8,128)S(1)} %get-tuple-element.28), channel_id=1, source_target_pairs={{0,128},{64,192},{128,0},{192,64},{1,129},{65,193},{129,1},{193,65... | collective-permute-start | bytes 835592 | tf_op jit(solution)/shard_map/ppermute | solution.py:328
  48.9 1.2 %azimuth_second.1 = (f32[2,272,128]{2,1,0:T(8,128)S(1)}, f32[8,128]{1,0:T(8,128)S(1)}) custom-call(f32[8,128]{1,0:T(8,128)S(1)} %get-tuple-element.23.order_ref, bf16[4,272,1024]{2,1,0:T(8,128)(2,1)S(1)} %get-tuple-element.22.t_ref, bf16[1024,256]{1,0:T(8,128)(2,1)S(1)} %get-tuple-element.24.x_hi, bf16[1024,256]{1,0:T(8,128)(2,1)S(1)} %get-tuple-element.25.x_lo), custom_call_target="tpu_custom_call" | custom-call | flops 1000 | bytes 1000 | tf_op jit(solution)/shard_map/azimuth_second/pallas_call | solution.py:320
  50.0 0.0 collective-permute-start.1
  50.1 2.3 %azimuth_own.1 = (f32[2,272,128]{2,1,0:T(8,128)S(1)}, f32[2,272,128]{2,1,0:T(8,128)S(1)}) custom-call(f32[8,128]{1,0:T(8,128)S(1)} %get-tuple-element.26.order_ref, f32[2,1,1024]{2,1,0:T(1,128)S(1)} %copy-done, bf16[1024,256]{1,0:T(8,128)(2,1)S(1)} %get-tuple-element.24.x_hi, bf16[1024,256]{1,0:T(8,128)(2,1)S(1)} %get-tuple-element.25.x_lo), custom_call_target="tpu_custom_call" | custom-call | flops 1000 | bytes 1000 | tf_op jit(solution)/shard_map/azimuth_own/pallas_call | solution.py:323
  52.3 1.8 %collective-permute-start.2 = (f32[2,272,128]{2,1,0:T(8,128)S(1)}, f32[2,272,128]{2,1,0:T(8,128)S(1)}, u32[]{:S(2)}, u32[]{:S(2)}) collective-permute-start(f32[2,272,128]{2,1,0:T(8,128)S(1)} %get-tuple-element.30), channel_id=1, source_target_pairs={{0,64},{64,0},{128,192},{192,128},{1,65},{65,1},{129,193},{193,129... | collective-permute-start | bytes 835592 | tf_op jit(solution)/shard_map/ppermute | solution.py:328
  54.2 1.0 %collective-permute-done.ya = f32[2,272,128]{2,1,0:T(8,128)S(1)} collective-permute-done((f32[2,272,128]{2,1,0:T(8,128)S(1)}, f32[2,272,128]{2,1,0:T(8,128)S(1)}, u32[]{:S(2)}, u32[]{:S(2)}) %collective-permute-start) | collective-permute-done | bytes 278560 | tf_op jit(solution)/shard_map/ppermute | solution.py:328
  55.1 0.1 two_receivers.1.first_ref
  55.2 5.4 %collective-permute-done.1.yb = f32[2,272,128]{2,1,0:T(8,128)S(1)} collective-permute-done((f32[2,272,128]{2,1,0:T(8,128)S(1)}, f32[2,272,128]{2,1,0:T(8,128)S(1)}, u32[]{:S(2)}, u32[]{:S(2)}) %collective-permute-start.1) | collective-permute-done | bytes 278560 | tf_op jit(solution)/shard_map/ppermute | solution.py:328
  60.6 0.0 copy-start.3
  60.7 0.0 collective-permute-done.2.y1
  60.7 0.2 edge.1
  60.9 0.9 %collective-permute-start.3 = (f32[136,128]{1,0:T(8,128)S(1)}, f32[136,128]{1,0:T(8,128)S(1)}, u32[]{:S(2)}, u32[]{:S(2)}) collective-permute-start(f32[136,128]{1,0:T(8,128)S(1)} %edge.1), channel_id=1, source_target_pairs={{0,63},{1,0},{2,1},{3,2},{4,3},{5,4},{6,5},{7,6},{8,7},{9,8},{10,9... | collective-permute-start | bytes 208904 | tf_op jit(solution)/shard_map/ppermute | solution.py:338
  61.8 0.9 %window_sums.1.main_ref = f32[2,512,128]{2,1,0:T(8,128)S(1)} custom-call(f32[4,8,128]{2,1,0:T(8,128)S(1)} %get-tuple-element.20.weight_ref, bf16[2,128,256]{2,1,0:T(8,128)(2,1)S(1)} %get-tuple-element.18.rows_ref, bf16[2,128,128]{2,1,0:T(8,128)(2,1)S(1)} %get-tuple-element.21.near_ref, f32[4,272,128]{2,1,0:T(8,128)S(1)} %three_receivers.1.part_ref, ...), custom_call_target="tpu_custom_call" | custom-call | flops 500000000 | bytes 1048576 | tf_op jit(solution)/shard_map/window_sums/pallas_call | solution.py:339
  62.7 5.6 %collective-permute-done.3.edge_ref = f32[136,128]{1,0:T(8,128)S(1)} collective-permute-done((f32[136,128]{1,0:T(8,128)S(1)}, f32[136,128]{1,0:T(8,128)S(1)}, u32[]{:S(2)}, u32[]{:S(2)}) %collective-permute-start.3) | collective-permute-done | bytes 69664 | tf_op jit(solution)/shard_map/ppermute | solution.py:338
  68.3 0.0 copy-done.3
  68.3 1.7 %coherence.1 = f32[2,256,128]{2,1,0:T(8,128)} custom-call(bf16[2,128,256]{2,1,0:T(8,128)(2,1)S(1)} %get-tuple-element.18.rows_ref, bf16[2,128,128]{2,1,0:T(8,128)(2,1)S(1)} %copy-done.3, f32[2,512,128]{2,1,0:T(8,128)S(1)} %window_sums.1.main_ref, f32[136,128]{1,0:T(8,128)S(1)} %collective-permute-done.3.edge_ref), custom_call_target="tpu_custom_call" | custom-call | flops 500000000 | bytes 1048576 | tf_op jit(solution)/shard_map/coherence/pallas_call | solution.py:343
  (1 shorter events, 0.0 us)
Async XLA Ops:
  0.0 17.3 %copy-start.4 = (s32[8,2]{0,1:T(2,128)S(1)}, s32[8,2]{0,1:T(2,128)}, u32[]{:S(2)}) copy-start(s32[8,2]{0,1:T(2,128)} %param.9) | copy-start | bytes 196
  0.0 17.4 %copy-start = (f32[2,1,1024]{2,1,0:T(1,128)S(1)}, f32[2,1,1024]{2,1,0:T(1,128)}, u32[]{:S(2)}) copy-start(f32[2,1,1024]{2,1,0:T(1,128)} %taps_ref.3) | copy-start | bytes 24580
  0.0 17.4 %copy-start.1 = (s32[4]{0:T(128)S(1)}, s32[4]{0:T(128)}, u32[]{:S(2)}) copy-start(s32[4]{0:T(128)} %pairing_ref.1) | copy-start | bytes 52
  4.5 40.7 %all-to-all-start = ((f32[64,32,128]{2,1,0:T(8,128)}), f32[64,32,128]{2,1,0:T(8,128)S(1)}, u32[]{:S(2)}, u32[]{:S(2)}) async-start(f32[64,32,128]{2,1,0:T(8,128)} %range_filter.1), calls=%async_computation | async-start | bytes 2097152 | tf_op jit(solution)/shard_map/all_to_all | solution.py:308
  18.8 0.6 copy-start.2
  46.7 8.4 %collective-permute-start = (f32[2,272,128]{2,1,0:T(8,128)S(1)}, f32[2,272,128]{2,1,0:T(8,128)S(1)}, u32[]{:S(2)}, u32[]{:S(2)}) collective-permute-start(f32[2,272,128]{2,1,0:T(8,128)S(1)} %get-tuple-element.28), channel_id=1, source_target_pairs={{0,128},{64,192},{128,0},{192,64},{1,129},{65,193},{129,1},{193,65... | collective-permute-start | bytes 835592 | tf_op jit(solution)/shard_map/ppermute | solution.py:328
  50.0 10.5 %collective-permute-start.1 = (f32[2,272,128]{2,1,0:T(8,128)S(1)}, f32[2,272,128]{2,1,0:T(8,128)S(1)}, u32[]{:S(2)}, u32[]{:S(2)}) collective-permute-start(f32[2,272,128]{2,1,0:T(8,128)S(1)} %get-tuple-element.29), channel_id=1, source_target_pairs={{0,192},{64,128},{128,64},{192,0},{1,193},{65,129},{129,65},{193,1... | collective-permute-start | bytes 835592 | tf_op jit(solution)/shard_map/ppermute | solution.py:328
  52.3 8.3 %collective-permute-start.2 = (f32[2,272,128]{2,1,0:T(8,128)S(1)}, f32[2,272,128]{2,1,0:T(8,128)S(1)}, u32[]{:S(2)}, u32[]{:S(2)}) collective-permute-start(f32[2,272,128]{2,1,0:T(8,128)S(1)} %get-tuple-element.30), channel_id=1, source_target_pairs={{0,64},{64,0},{128,192},{192,128},{1,65},{65,1},{129,193},{193,129... | collective-permute-start | bytes 835592 | tf_op jit(solution)/shard_map/ppermute | solution.py:328
  60.6 7.7 %copy-start.3 = (bf16[2,128,128]{2,1,0:T(8,128)(2,1)S(1)}, bf16[2,128,128]{2,1,0:T(8,128)(2,1)}, u32[]{:S(2)}) copy-start(bf16[2,128,128]{2,1,0:T(8,128)(2,1)} %copy-done.2) | copy-start | bytes 196612
  60.9 7.4 %collective-permute-start.3 = (f32[136,128]{1,0:T(8,128)S(1)}, f32[136,128]{1,0:T(8,128)S(1)}, u32[]{:S(2)}, u32[]{:S(2)}) collective-permute-start(f32[136,128]{1,0:T(8,128)S(1)} %edge.1), channel_id=1, source_target_pairs={{0,63},{1,0},{2,1},{3,2},{4,3},{5,4},{6,5},{7,6},{8,7},{9,8},{10,9... | collective-permute-start | bytes 208904 | tf_op jit(solution)/shard_map/ppermute | solution.py:338

commit v11 on v10

--- a/solution.py
+++ b/solution.py
@@ -253,7 +253,7 @@
         out_ref[g] = dot_nn(hi, near_ref[g]) + dot_nn(lo, near_ref[g])
 
 
-def coherence_kernel(rows_ref, far_ref, main_ref, edge_ref, out_ref, p_hi, p_lo):
+def coherence_kernel(rows_ref, far_ref, main_ref, edge_ref, out_hbm, out_ref, sems):
     packed = edge_ref[...]
     edge = jnp.concatenate([packed, pltpu.roll(packed, 64, 1)], 0)
     lane = lax.broadcasted_iota(jnp.int32, (272, 128), 1)
@@ -262,18 +262,21 @@
     for q, value in enumerate(quantities(*planes)):
         moved = pltpu.roll(value, 16 * q, 1) if q else value
         both = jnp.where((lane >= 16 * q) & (lane < 16 * q + 16), moved, both)
-    hi, lo = split(both)
-    p_hi[0:272, :] = hi
-    p_lo[0:272, :] = lo
-    p_hi[272:384, :] = jnp.zeros((112, 128), BF16)
-    p_lo[272:384, :] = jnp.zeros((112, 128), BF16)
+    p_hi, p_lo = split(jnp.concatenate([both, jnp.zeros((112, 128), F32)], 0))
+    copies = []
     for g in range(2):
-        sums = dot_nn(rows_ref[g], p_hi[128 * g:128 * g + 256, :]) + dot_nn(rows_ref[g], p_lo[128 * g:128 * g + 256, :])
+        near = slice(128 * g, 128 * g + 256)
+        sums = dot_nn(rows_ref[g], p_hi[near]) + dot_nn(rows_ref[g], p_lo[near])
         hi, lo = split(jnp.concatenate([sums] + [pltpu.roll(sums, 128 - 16 * q, 1) for q in range(1, 4)], 0))
         window = main_ref[g] + dot_nn(hi, far_ref[g]) + dot_nn(lo, far_ref[g])
         scale = 1.0 / jnp.sqrt(jnp.maximum(window[256:384], 1.0) * jnp.maximum(window[384:512], 1.0))
         out_ref[0, 128 * g:128 * g + 128, :] = window[0:128] * scale
         out_ref[1, 128 * g:128 * g + 128, :] = window[128:256] * scale
+        rows = pl.ds(128 * g, 128)
+        copies.append(pltpu.make_async_copy(out_ref.at[:, rows, :], out_hbm.at[:, rows, :], sems.at[g]))
+        copies[g].start()
+    for copy in copies:
+        copy.wait()
 
 
 def call(kernel, name, out_shape, scratch, n_in, smem=(), hbm=(), flops=0, moved=0, vmem=VMEM_LIMIT, out=pltpu.VMEM):
@@ -341,8 +344,9 @@
         5, flops=500_000_000, moved=1 << 20,
     )(weight, rows, near, part, y1)
     return call(
-        coherence_kernel, "coherence", shape(2, 256, 128), [pltpu.VMEM((384, 128), BF16)] * 2,
-        4, flops=500_000_000, moved=1 << 20,
+        coherence_kernel, "coherence", shape(2, 256, 128),
+        [pltpu.VMEM((2, 256, 128), F32), pltpu.SemaphoreType.DMA((2,))],
+        4, flops=500_000_000, moved=1 << 20, out=pltpu.HBM,
     )(rows, far, main, after)
 
 

time: 70.2 us -> 70.3 us (level)
  no operation moved by 1% of the time
where the time goes in v11:
time: 70.3 us; the launch traced here: 70.1 us
  waiting for transfers between devices  37.8 us (54%)
  starting transfers between devices  17.6 us (25%)
  Pallas kernels  13.7 us (19%)
  local copies, waits for them, and re-layouts  0.72 us (1%)
    all_to_all x1, waiting for transfers between devices, body(): lax.all_to_all(parted, 'wide', split_axis=0, concat_axis=0, tiled=True)  25.9 us
    all_to_all x1, starting transfers between devices, body(): lax.all_to_all(parted, 'wide', split_axis=0, concat_axis=0, tiled=True)  12.8 us
    ppermute x3, waiting for transfers between devices, body(): lax.ppermute(p, 'chan', [(i, i ^ k) for i in range(4)])  6.37 us
    ppermute x1, waiting for transfers between devices, body(): after = lax.ppermute(edge, 'wide', [(i, (i - 1) % 64) for i in range(64)])  5.58 us
    pallas_call x1, Pallas kernels, body(): call(range_kernel, 'range_filter', shape(64, 32, 128), [pltpu.VMEM((2, 16...  4.52 us
    ppermute x3, starting transfers between devices, body(): lax.ppermute(p, 'chan', [(i, i ^ k) for i in range(4)])  3.95 us
    pallas_call x1, Pallas kernels, body(): call(azimuth_own, 'azimuth_own', (shape(2, 272, 128),) * 2, [pltpu.VMEM((...  2.27 us
    pallas_call x1, Pallas kernels, body(): call(coherence_kernel, 'coherence', shape(2, 256, 128), [pltpu.VMEM((2, 2...  1.63 us
  transfers between devices with their start and end apart: 5, of which 4 were waited for; matrix products, arithmetic and copies ran while one was open for 0% of the time, Pallas kernels for 8%

profile of v11, /device:TPU:26, one launch (start us, length us, event | category | flops | bytes accessed | tf_op | source)
XLA Modules:
  0.0 70.1 jit_solution(8154897011304428947)
XLA Ops:
  0.0 0.0 copy-start.4
  0.0 0.0 copy-start
  0.0 0.0 copy-start.1
  0.0 4.5 %range_filter.1 = f32[64,32,128]{2,1,0:T(8,128)} custom-call(f32[2,16,8192]{2,1,0:T(8,128)} %bitcast.3, f32[2,1,512]{2,1,0:T(1,128)} %chirp_hbm.1), custom_call_target="tpu_custom_call" | custom-call | flops 2000000000 | bytes 2097152 | tf_op jit(solution)/shard_map/range_filter/pallas_call | solution.py:304
  4.5 12.8 %all-to-all-start = ((f32[64,32,128]{2,1,0:T(8,128)}), f32[64,32,128]{2,1,0:T(8,128)S(1)}, u32[]{:S(2)}, u32[]{:S(2)}) async-start(f32[64,32,128]{2,1,0:T(8,128)} %range_filter.1), calls=%async_computation | async-start | bytes 2097152 | tf_op jit(solution)/shard_map/all_to_all | solution.py:311
  17.3 0.0 copy-done.4
  17.3 0.1 copy.6.offsets_ref
  17.4 0.0 copy-done
  17.4 0.0 copy-done.1
  17.4 1.4 %prepare.1 = (bf16[4,272,1024]{2,1,0:T(8,128)(2,1)S(1)}, f32[4,8,128]{2,1,0:T(8,128)S(1)}, bf16[2,128,256]{2,1,0:T(8,128)(2,1)S(1)}, bf16[2,128,128]{2,1,0:T(8,128)(2,1)S(1)}, bf16[2,128,128]{2,1,0:T(8,128)(2,1)S(1)}) custom-call(s32[4]{0:T(128)S(1)} %copy-done.1, s32[8,2]{1,0:T(8,128)S(1)} %copy.6.offsets_ref, f32[2,1,1024]{2,1,0:T(1,128)S(1)} %copy-done), custom_call_target="tpu_custom_call" | custom-call | flops 1000000000 | bytes 1048576 | tf_op jit(solution)/shard_map/prepare/pallas_call | solution.py:312
  18.8 0.0 copy-start.2
  18.8 0.6 copy-done.2
  19.4 25.9 %all-to-all-done.x_ref = f32[64,32,128]{2,1,0:T(8,128)S(1)} async-done(((f32[64,32,128]{2,1,0:T(8,128)}), f32[64,32,128]{2,1,0:T(8,128)S(1)}, u32[]{:S(2)}, u32[]{:S(2)}) %all-to-all-start) | async-done | bytes 1048608 | tf_op jit(solution)/shard_map/all_to_all | solution.py:311
  45.3 1.4 %azimuth_first.1 = (f32[2,272,128]{2,1,0:T(8,128)S(1)}, f32[8,128]{1,0:T(8,128)S(1)}, bf16[1024,256]{1,0:T(8,128)(2,1)S(1)}, bf16[1024,256]{1,0:T(8,128)(2,1)S(1)}) custom-call(f32[64,32,128]{2,1,0:T(8,128)S(1)} %all-to-all-done.x_ref, bf16[4,272,1024]{2,1,0:T(8,128)(2,1)S(1)} %get-tuple-element.22.t_ref, f32[32,128]{1,0:T(8,128)S(1)} %bitcast.2), custom_call_target="tpu_custom_call" | custom-call | flops 1000000000 | bytes 1000 | tf_op jit(solution)/shard_map/azimuth_first/pallas_call | solution.py:319
  46.7 2.1 %collective-permute-start = (f32[2,272,128]{2,1,0:T(8,128)S(1)}, f32[2,272,128]{2,1,0:T(8,128)S(1)}, u32[]{:S(2)}, u32[]{:S(2)}) collective-permute-start(f32[2,272,128]{2,1,0:T(8,128)S(1)} %get-tuple-element.28), channel_id=1, source_target_pairs={{0,128},{64,192},{128,0},{192,64},{1,129},{65,193},{129,1},{193,65... | collective-permute-start | bytes 835592 | tf_op jit(solution)/shard_map/ppermute | solution.py:331
  48.9 1.2 %azimuth_second.1 = (f32[2,272,128]{2,1,0:T(8,128)S(1)}, f32[8,128]{1,0:T(8,128)S(1)}) custom-call(f32[8,128]{1,0:T(8,128)S(1)} %get-tuple-element.23.order_ref, bf16[4,272,1024]{2,1,0:T(8,128)(2,1)S(1)} %get-tuple-element.22.t_ref, bf16[1024,256]{1,0:T(8,128)(2,1)S(1)} %get-tuple-element.24.x_hi, bf16[1024,256]{1,0:T(8,128)(2,1)S(1)} %get-tuple-element.25.x_lo), custom_call_target="tpu_custom_call" | custom-call | flops 1000 | bytes 1000 | tf_op jit(solution)/shard_map/azimuth_second/pallas_call | solution.py:323
  50.0 0.0 collective-permute-start.1
  50.1 2.3 %azimuth_own.1 = (f32[2,272,128]{2,1,0:T(8,128)S(1)}, f32[2,272,128]{2,1,0:T(8,128)S(1)}) custom-call(f32[8,128]{1,0:T(8,128)S(1)} %get-tuple-element.26.order_ref, f32[2,1,1024]{2,1,0:T(1,128)S(1)} %copy-done, bf16[1024,256]{1,0:T(8,128)(2,1)S(1)} %get-tuple-element.24.x_hi, bf16[1024,256]{1,0:T(8,128)(2,1)S(1)} %get-tuple-element.25.x_lo), custom_call_target="tpu_custom_call" | custom-call | flops 1000 | bytes 1000 | tf_op jit(solution)/shard_map/azimuth_own/pallas_call | solution.py:326
  52.3 1.8 %collective-permute-start.2 = (f32[2,272,128]{2,1,0:T(8,128)S(1)}, f32[2,272,128]{2,1,0:T(8,128)S(1)}, u32[]{:S(2)}, u32[]{:S(2)}) collective-permute-start(f32[2,272,128]{2,1,0:T(8,128)S(1)} %get-tuple-element.30), channel_id=1, source_target_pairs={{0,64},{64,0},{128,192},{192,128},{1,65},{65,1},{129,193},{193,129... | collective-permute-start | bytes 835592 | tf_op jit(solution)/shard_map/ppermute | solution.py:331
  54.2 1.0 %collective-permute-done.ya = f32[2,272,128]{2,1,0:T(8,128)S(1)} collective-permute-done((f32[2,272,128]{2,1,0:T(8,128)S(1)}, f32[2,272,128]{2,1,0:T(8,128)S(1)}, u32[]{:S(2)}, u32[]{:S(2)}) %collective-permute-start) | collective-permute-done | bytes 278560 | tf_op jit(solution)/shard_map/ppermute | solution.py:331
  55.1 0.1 two_receivers.1.first_ref
  55.2 5.4 %collective-permute-done.1.yb = f32[2,272,128]{2,1,0:T(8,128)S(1)} collective-permute-done((f32[2,272,128]{2,1,0:T(8,128)S(1)}, f32[2,272,128]{2,1,0:T(8,128)S(1)}, u32[]{:S(2)}, u32[]{:S(2)}) %collective-permute-start.1) | collective-permute-done | bytes 278560 | tf_op jit(solution)/shard_map/ppermute | solution.py:331
  60.6 0.0 copy-start.3
  60.7 0.0 collective-permute-done.2.y1
  60.7 0.2 edge.1
  60.9 0.9 %collective-permute-start.3 = (f32[136,128]{1,0:T(8,128)S(1)}, f32[136,128]{1,0:T(8,128)S(1)}, u32[]{:S(2)}, u32[]{:S(2)}) collective-permute-start(f32[136,128]{1,0:T(8,128)S(1)} %edge.1), channel_id=1, source_target_pairs={{0,63},{1,0},{2,1},{3,2},{4,3},{5,4},{6,5},{7,6},{8,7},{9,8},{10,9... | collective-permute-start | bytes 208904 | tf_op jit(solution)/shard_map/ppermute | solution.py:341
  61.8 0.9 %window_sums.1.main_ref = f32[2,512,128]{2,1,0:T(8,128)S(1)} custom-call(f32[4,8,128]{2,1,0:T(8,128)S(1)} %get-tuple-element.20.weight_ref, bf16[2,128,256]{2,1,0:T(8,128)(2,1)S(1)} %get-tuple-element.18.rows_ref, bf16[2,128,128]{2,1,0:T(8,128)(2,1)S(1)} %get-tuple-element.21.near_ref, f32[4,272,128]{2,1,0:T(8,128)S(1)} %three_receivers.1.part_ref, ...), custom_call_target="tpu_custom_call" | custom-call | flops 500000000 | bytes 1048576 | tf_op jit(solution)/shard_map/window_sums/pallas_call | solution.py:342
  62.7 5.6 %collective-permute-done.3.edge_ref = f32[136,128]{1,0:T(8,128)S(1)} collective-permute-done((f32[136,128]{1,0:T(8,128)S(1)}, f32[136,128]{1,0:T(8,128)S(1)}, u32[]{:S(2)}, u32[]{:S(2)}) %collective-permute-start.3) | collective-permute-done | bytes 69664 | tf_op jit(solution)/shard_map/ppermute | solution.py:341
  68.3 0.0 copy-done.3
  68.3 1.6 %coherence.1 = f32[2,256,128]{2,1,0:T(8,128)} custom-call(bf16[2,128,256]{2,1,0:T(8,128)(2,1)S(1)} %get-tuple-element.18.rows_ref, bf16[2,128,128]{2,1,0:T(8,128)(2,1)S(1)} %copy-done.3, f32[2,512,128]{2,1,0:T(8,128)S(1)} %window_sums.1.main_ref, f32[136,128]{1,0:T(8,128)S(1)} %collective-permute-done.3.edge_ref), custom_call_target="tpu_custom_call" | custom-call | flops 500000000 | bytes 1048576 | tf_op jit(solution)/shard_map/coherence/pallas_call | solution.py:346
  (1 shorter events, 0.0 us)
Async XLA Ops:
  0.0 17.3 %copy-start.4 = (s32[8,2]{0,1:T(2,128)S(1)}, s32[8,2]{0,1:T(2,128)}, u32[]{:S(2)}) copy-start(s32[8,2]{0,1:T(2,128)} %param.9) | copy-start | bytes 196
  0.0 17.4 %copy-start = (f32[2,1,1024]{2,1,0:T(1,128)S(1)}, f32[2,1,1024]{2,1,0:T(1,128)}, u32[]{:S(2)}) copy-start(f32[2,1,1024]{2,1,0:T(1,128)} %taps_ref.3) | copy-start | bytes 24580
  0.0 17.4 %copy-start.1 = (s32[4]{0:T(128)S(1)}, s32[4]{0:T(128)}, u32[]{:S(2)}) copy-start(s32[4]{0:T(128)} %pairing_ref.1) | copy-start | bytes 52
  4.5 40.7 %all-to-all-start = ((f32[64,32,128]{2,1,0:T(8,128)}), f32[64,32,128]{2,1,0:T(8,128)S(1)}, u32[]{:S(2)}, u32[]{:S(2)}) async-start(f32[64,32,128]{2,1,0:T(8,128)} %range_filter.1), calls=%async_computation | async-start | bytes 2097152 | tf_op jit(solution)/shard_map/all_to_all | solution.py:311
  18.8 0.6 copy-start.2
  46.7 8.4 %collective-permute-start = (f32[2,272,128]{2,1,0:T(8,128)S(1)}, f32[2,272,128]{2,1,0:T(8,128)S(1)}, u32[]{:S(2)}, u32[]{:S(2)}) collective-permute-start(f32[2,272,128]{2,1,0:T(8,128)S(1)} %get-tuple-element.28), channel_id=1, source_target_pairs={{0,128},{64,192},{128,0},{192,64},{1,129},{65,193},{129,1},{193,65... | collective-permute-start | bytes 835592 | tf_op jit(solution)/shard_map/ppermute | solution.py:331
  50.0 10.5 %collective-permute-start.1 = (f32[2,272,128]{2,1,0:T(8,128)S(1)}, f32[2,272,128]{2,1,0:T(8,128)S(1)}, u32[]{:S(2)}, u32[]{:S(2)}) collective-permute-start(f32[2,272,128]{2,1,0:T(8,128)S(1)} %get-tuple-element.29), channel_id=1, source_target_pairs={{0,192},{64,128},{128,64},{192,0},{1,193},{65,129},{129,65},{193,1... | collective-permute-start | bytes 835592 | tf_op jit(solution)/shard_map/ppermute | solution.py:331
  52.3 8.3 %collective-permute-start.2 = (f32[2,272,128]{2,1,0:T(8,128)S(1)}, f32[2,272,128]{2,1,0:T(8,128)S(1)}, u32[]{:S(2)}, u32[]{:S(2)}) collective-permute-start(f32[2,272,128]{2,1,0:T(8,128)S(1)} %get-tuple-element.30), channel_id=1, source_target_pairs={{0,64},{64,0},{128,192},{192,128},{1,65},{65,1},{129,193},{193,129... | collective-permute-start | bytes 835592 | tf_op jit(solution)/shard_map/ppermute | solution.py:331
  60.6 7.7 %copy-start.3 = (bf16[2,128,128]{2,1,0:T(8,128)(2,1)S(1)}, bf16[2,128,128]{2,1,0:T(8,128)(2,1)}, u32[]{:S(2)}) copy-start(bf16[2,128,128]{2,1,0:T(8,128)(2,1)} %copy-done.2) | copy-start | bytes 196612
  60.9 7.4 %collective-permute-start.3 = (f32[136,128]{1,0:T(8,128)S(1)}, f32[136,128]{1,0:T(8,128)S(1)}, u32[]{:S(2)}, u32[]{:S(2)}) collective-permute-start(f32[136,128]{1,0:T(8,128)S(1)} %edge.1), channel_id=1, source_target_pairs={{0,63},{1,0},{2,1},{3,2},{4,3},{5,4},{6,5},{7,6},{8,7},{9,8},{10,9... | collective-permute-start | bytes 208904 | tf_op jit(solution)/shard_map/ppermute | solution.py:341

commit v12 on v10

--- a/solution.py
+++ b/solution.py
@@ -155,15 +155,16 @@
     return g[0][:, 0:128] - g[1][:, 128:256], g[0][:, 128:256] + g[1][:, 0:128]
 
 
-def first_quarter(x_ref, t_ref, order_ref, out_ref, done_ref, x_hi, x_lo):
+def other_quarters(x_ref, t_ref, order_ref, oa, ob, done_ref, x_hi, x_lo):
     done_ref[...] = jnp.zeros((8, 128), F32)
     split_pulses(x_ref, x_hi, x_lo)
-    azimuth_quarter(2, (t_ref, x_hi, x_lo), out_ref)
-
-
-def second_quarter(order_ref, t_ref, x_hi, x_lo, out_ref, done_ref):
-    done_ref[...] = jnp.zeros((8, 128), F32)
-    azimuth_quarter(3, (t_ref, x_hi, x_lo), out_ref)
+    azimuth_quarter(2, (t_ref, x_hi, x_lo), oa)
+    azimuth_quarter(3, (t_ref, x_hi, x_lo), ob)
+    for part in range(2):
+        oa[part, 272:312, :] = jnp.zeros((40, 128), F32)
+        for j in range(7):
+            size = min(40, 272 - 40 * j)
+            oa[part, 272:272 + size, 16 * j:16 * j + 16] = ob[part, 40 * j:40 * j + size, 0:16]
 
 
 def azimuth_quarter(k, taps, out_ref):
@@ -174,7 +175,7 @@
             own = quarter_rows(q, slice(0, 272), *taps, COLUMN[q // 2])
             shared = quarter_rows(q ^ 1, slice(256, 272) if q % 2 else slice(0, 16), *taps, COLUMN[q // 2])
             for part in range(2):
-                out_ref[part] = own[part]
+                out_ref[part, 0:272, :] = own[part]
                 if q % 2:
                     out_ref[part, 0:8, :] = shared[part][0:8]
                 else:
@@ -209,8 +210,8 @@
 def first_sums_kernel(weight_ref, y0, ya, part_ref):
     own, other = weight_ref[0, 0:1, :], weight_ref[FIRST, 0:1, :]
     for part in range(2):
-        part_ref[part] = y0[part] * own + ya[part] * other
-        part_ref[2 + part] = y0[part] * (1.0 - own) + ya[part] * (1.0 - other)
+        part_ref[part] = y0[part] * own + ya[part, 0:272, :] * other
+        part_ref[2 + part] = y0[part] * (1.0 - own) + ya[part, 0:272, :] * (1.0 - other)
 
 
 def more_sums_kernel(weight_ref, first_ref, yb, part_ref):
@@ -226,10 +227,16 @@
     return fore + [part_ref[2 + part] + y1[part] * (1.0 - weight) for part in range(2)]
 
 
-def edge_kernel(weight_ref, part_ref, y1, edge_ref):
+def edge_kernel(weight_ref, part_ref, y1, passed, edge_ref):
     lane = lax.broadcasted_iota(jnp.int32, (272, 128), 1)
     edge = jnp.zeros((272, 128), F32)
+    far = []
+    for part in range(2):
+        groups = [passed[part] if j == 0 else pltpu.roll(passed[part], 128 - 16 * j, 1) for j in range(7)]
+        far.append(jnp.concatenate(groups[:6] + [groups[6][0:32]], 0))
+    weight = weight_ref[3 - FIRST, 0:1, :]
     for plane, value in enumerate(whole_sums(weight_ref, part_ref, y1)):
+        value = value + far[plane % 2] * (weight if plane < 2 else 1.0 - weight)
         at = 16 * plane
         moved = pltpu.roll(value, at, 1) if at else value
         edge = jnp.where((lane >= at) & (lane < at + 16), moved, edge)
@@ -313,28 +320,27 @@
         3, smem=(0, 1), flops=1_000_000_000, moved=1 << 20,
     )(pairing, offsets, taps)
     order = weight.reshape(32, 128)
-    pa, order, *pulses = call(
-        first_quarter, "azimuth_first", (shape(2, 272, 128), shape(8, 128)) + (shape(1024, 256, dtype=BF16),) * 2,
+    pa, pb, order, *pulses = call(
+        other_quarters, "azimuth_other",
+        (shape(2, 312, 128), shape(2, 272, 128), shape(8, 128)) + (shape(1024, 256, dtype=BF16),) * 2,
         [], 3, flops=1_000_000_000, moved=1000,
     )(turned, t, order)
-    pb, order = call(
-        second_quarter, "azimuth_second", (shape(2, 272, 128), shape(8, 128)), [], 4, flops=1000, moved=1000,
-    )(order, t, *pulses)
     p0, p1 = call(
         azimuth_own, "azimuth_own", (shape(2, 272, 128),) * 2,
         [pltpu.VMEM((4, 272, 1280), BF16), pltpu.VMEM((2, 2, 272, 128), F32)],
         4, flops=1000, moved=1000,
     )(order, taps, *pulses)
     ya, yb, y1 = [lax.ppermute(p, "chan", [(i, i ^ k) for i in range(4)]) for k, p in ((2, pa), (3, pb), (1, p1))]
-    part = call(
+    passed = lax.ppermute(ya[:, 272:312, :], "chan", [(i, i ^ 1) for i in range(4)])
+    first = call(
         first_sums_kernel, "two_receivers", shape(4, 272, 128), [], 3, flops=FIRST_COST, moved=1000,
     )(weight, p0, ya)
+    edge = call(
+        edge_kernel, "edge", shape(136, 128), [], 4, flops=1000, moved=1000,
+    )(weight, first, y1, passed)
     part = call(
         more_sums_kernel, "three_receivers", shape(4, 272, 128), [], 3, flops=30_000_000_000, moved=2 << 20,
-    )(weight, part, yb)
-    edge = call(
-        edge_kernel, "edge", shape(136, 128), [], 3, flops=1_000_000, moved=2 << 20,
-    )(weight, part, y1)
+    )(weight, first, yb)
     after = lax.ppermute(edge, "wide", [(i, (i - 1) % 64) for i in range(64)])
     main = call(
         main_kernel, "window_sums", shape(2, 512, 128), [pltpu.VMEM((384, 512), BF16)] * 2,

time: 70.2 us -> 69.4 us (0.989)
  the two profiles are of different devices: /device:TPU:26 before, /device:TPU:62 now
where the time goes in v12:
time: 69.4 us; the launch traced here: 69.2 us
  waiting for transfers between devices  37.8 us (54%)
  starting transfers between devices  16.5 us (24%)
  Pallas kernels  14 us (20%)
  local copies, waits for them, and re-layouts  0.73 us (1%)
    all_to_all x1, waiting for transfers between devices, body(): lax.all_to_all(parted, 'wide', split_axis=0, concat_axis=0, tiled=True)  25 us
    all_to_all x1, starting transfers between devices, body(): lax.all_to_all(parted, 'wide', split_axis=0, concat_axis=0, tiled=True)  12.3 us
    ppermute x3, waiting for transfers between devices, body(): lax.ppermute(p, 'chan', [(i, i ^ k) for i in range(4)])  6.47 us
    ppermute x1, waiting for transfers between devices, body(): after = lax.ppermute(edge, 'wide', [(i, (i - 1) % 64) for i in range(64)])  5.2 us
    pallas_call x1, Pallas kernels, body(): call(range_kernel, 'range_filter', shape(64, 32, 128), [pltpu.VMEM((2, 16...  4.52 us
    ppermute x3, starting transfers between devices, body(): lax.ppermute(p, 'chan', [(i, i ^ k) for i in range(4)])  3.84 us
    pallas_call x1, Pallas kernels, body(): call(other_quarters, 'azimuth_other', (shape(2, 312, 128), shape(2, 272,...  2.87 us
    pallas_call x1, Pallas kernels, body(): call(azimuth_own, 'azimuth_own', (shape(2, 272, 128),) * 2, [pltpu.VMEM((...  2.25 us
  transfers between devices with their start and end apart: 6, of which 5 were waited for; matrix products, arithmetic and copies ran while one was open for 0% of the time, Pallas kernels for 7%

profile of v12, /device:TPU:62, one launch (start us, length us, event | category | flops | bytes accessed | tf_op | source)
XLA Modules:
  0.0 69.2 jit_solution(9427778640082349092)
XLA Ops:
  0.0 0.0 copy-start.4
  0.0 0.0 copy-start
  0.0 0.0 copy-start.1
  0.0 4.5 %range_filter.1 = f32[64,32,128]{2,1,0:T(8,128)} custom-call(f32[2,16,8192]{2,1,0:T(8,128)} %bitcast.3, f32[2,1,512]{2,1,0:T(1,128)} %chirp_hbm.1), custom_call_target="tpu_custom_call" | custom-call | flops 2000000000 | bytes 2097152 | tf_op jit(solution)/shard_map/range_filter/pallas_call | solution.py:308
  4.5 12.3 %all-to-all-start = ((f32[64,32,128]{2,1,0:T(8,128)}), f32[64,32,128]{2,1,0:T(8,128)S(1)}, u32[]{:S(2)}, u32[]{:S(2)}) async-start(f32[64,32,128]{2,1,0:T(8,128)} %range_filter.1), calls=%async_computation | async-start | bytes 2097152 | tf_op jit(solution)/shard_map/all_to_all | solution.py:315
  16.9 0.0 copy-done.4
  16.9 0.1 copy.6.offsets_ref
  17.0 0.0 copy-done
  17.0 0.0 copy-done.1
  17.0 1.4 %prepare.1 = (bf16[4,272,1024]{2,1,0:T(8,128)(2,1)S(1)}, f32[4,8,128]{2,1,0:T(8,128)S(1)}, bf16[2,128,256]{2,1,0:T(8,128)(2,1)S(1)}, bf16[2,128,128]{2,1,0:T(8,128)(2,1)S(1)}, bf16[2,128,128]{2,1,0:T(8,128)(2,1)S(1)}) custom-call(s32[4]{0:T(128)S(1)} %copy-done.1, s32[8,2]{1,0:T(8,128)S(1)} %copy.6.offsets_ref, f32[2,1,1024]{2,1,0:T(1,128)S(1)} %copy-done), custom_call_target="tpu_custom_call" | custom-call | flops 1000000000 | bytes 1048576 | tf_op jit(solution)/shard_map/prepare/pallas_call | solution.py:316
  18.3 0.0 copy-start.2
  18.3 0.6 copy-done.2
  19.0 25.0 %all-to-all-done.x_ref = f32[64,32,128]{2,1,0:T(8,128)S(1)} async-done(((f32[64,32,128]{2,1,0:T(8,128)}), f32[64,32,128]{2,1,0:T(8,128)S(1)}, u32[]{:S(2)}, u32[]{:S(2)}) %all-to-all-start) | async-done | bytes 1048608 | tf_op jit(solution)/shard_map/all_to_all | solution.py:315
  44.0 2.9 %azimuth_other.1 = (f32[2,312,128]{2,1,0:T(8,128)S(1)}, f32[2,272,128]{2,1,0:T(8,128)S(1)}, f32[8,128]{1,0:T(8,128)S(1)}, bf16[1024,256]{1,0:T(8,128)(2,1)S(1)}, bf16[1024,256]{1,0:T(8,128)(2,1)S(1)}) custom-call(f32[64,32,128]{2,1,0:T(8,128)S(1)} %all-to-all-done.x_ref, bf16[4,272,1024]{2,1,0:T(8,128)(2,1)S(1)} %get-tuple-element.21.t_ref, ...), custom_call_target="tpu_custom_call" | custom-call | flops 1000000000 | bytes 1000 | tf_op jit(solution)/shard_map/azimuth_other/pallas_call | solution.py:323
  46.9 1.5 %collective-permute-start = (f32[2,312,128]{2,1,0:T(8,128)S(1)}, f32[2,312,128]{2,1,0:T(8,128)S(1)}, u32[]{:S(2)}, u32[]{:S(2)}) collective-permute-start(f32[2,312,128]{2,1,0:T(8,128)S(1)} %get-tuple-element.26), channel_id=1, source_target_pairs={{0,128},{64,192},{128,0},{192,64},{1,129},{65,193},{129,1},{193,65... | collective-permute-start | bytes 958472 | tf_op jit(solution)/shard_map/ppermute | solution.py:333
  48.4 2.2 %azimuth_own.1 = (f32[2,272,128]{2,1,0:T(8,128)S(1)}, f32[2,272,128]{2,1,0:T(8,128)S(1)}) custom-call(f32[8,128]{1,0:T(8,128)S(1)} %get-tuple-element.22.order_ref, f32[2,1,1024]{2,1,0:T(1,128)S(1)} %copy-done, bf16[1024,256]{1,0:T(8,128)(2,1)S(1)} %get-tuple-element.23.x_hi, bf16[1024,256]{1,0:T(8,128)(2,1)S(1)} %get-tuple-element.24.x_lo), custom_call_target="tpu_custom_call" | custom-call | flops 1000 | bytes 1000 | tf_op jit(solution)/shard_map/azimuth_own/pallas_call | solution.py:328
  50.6 0.1 collective-permute-start.2
  50.7 2.2 %collective-permute-start.1 = (f32[2,272,128]{2,1,0:T(8,128)S(1)}, f32[2,272,128]{2,1,0:T(8,128)S(1)}, u32[]{:S(2)}, u32[]{:S(2)}) collective-permute-start(f32[2,272,128]{2,1,0:T(8,128)S(1)} %get-tuple-element.27), channel_id=1, source_target_pairs={{0,192},{64,128},{128,64},{192,0},{1,193},{65,129},{129,65},{193,1... | collective-permute-start | bytes 835592 | tf_op jit(solution)/shard_map/ppermute | solution.py:333
  53.0 5.6 %collective-permute-done.ya = f32[2,312,128]{2,1,0:T(8,128)S(1)} collective-permute-done((f32[2,312,128]{2,1,0:T(8,128)S(1)}, f32[2,312,128]{2,1,0:T(8,128)S(1)}, u32[]{:S(2)}, u32[]{:S(2)}) %collective-permute-start) | collective-permute-done | bytes 319520 | tf_op jit(solution)/shard_map/ppermute | solution.py:333
  58.6 0.0 collective-permute-start.3
  58.6 0.1 two_receivers.1.first_ref.part_ref
  58.7 0.0 collective-permute-done.2.y1
  58.7 1.1 %collective-permute-done.3.passed = f32[2,40,128]{2,1,0:T(8,128)S(1)} collective-permute-done((f32[2,40,128]{2,1,0:T(8,128)S(1)}, f32[2,40,128]{2,1,0:T(8,128)S(1)}, u32[]{:S(2)}, u32[]{:S(2)}) %collective-permute-start.3) | collective-permute-done | bytes 40992 | tf_op jit(solution)/shard_map/ppermute | solution.py:334
  59.8 0.3 edge.1
  60.1 0.0 copy-start.3
  60.1 0.4 collective-permute-start.4
  60.5 0.9 %collective-permute-done.1.yb = f32[2,272,128]{2,1,0:T(8,128)S(1)} collective-permute-done((f32[2,272,128]{2,1,0:T(8,128)S(1)}, f32[2,272,128]{2,1,0:T(8,128)S(1)}, u32[]{:S(2)}, u32[]{:S(2)}) %collective-permute-start.1) | collective-permute-done | bytes 278560 | tf_op jit(solution)/shard_map/ppermute | solution.py:333
  61.4 0.9 %window_sums.1.main_ref = f32[2,512,128]{2,1,0:T(8,128)S(1)} custom-call(f32[4,8,128]{2,1,0:T(8,128)S(1)} %get-tuple-element.19.weight_ref, bf16[2,128,256]{2,1,0:T(8,128)(2,1)S(1)} %get-tuple-element.17.rows_ref, bf16[2,128,128]{2,1,0:T(8,128)(2,1)S(1)} %get-tuple-element.20.near_ref, f32[4,272,128]{2,1,0:T(8,128)S(1)} %three_receivers.1.part_ref, ...), custom_call_target="tpu_custom_call" | custom-call | flops 500000000 | bytes 1048576 | tf_op jit(solution)/shard_map/window_sums/pallas_call | solution.py:345
  62.3 5.2 %collective-permute-done.4.edge_ref = f32[136,128]{1,0:T(8,128)S(1)} collective-permute-done((f32[136,128]{1,0:T(8,128)S(1)}, f32[136,128]{1,0:T(8,128)S(1)}, u32[]{:S(2)}, u32[]{:S(2)}) %collective-permute-start.4) | collective-permute-done | bytes 69664 | tf_op jit(solution)/shard_map/ppermute | solution.py:344
  67.5 0.0 copy-done.3
  67.5 1.7 %coherence.1 = f32[2,256,128]{2,1,0:T(8,128)} custom-call(bf16[2,128,256]{2,1,0:T(8,128)(2,1)S(1)} %get-tuple-element.17.rows_ref, bf16[2,128,128]{2,1,0:T(8,128)(2,1)S(1)} %copy-done.3, f32[2,512,128]{2,1,0:T(8,128)S(1)} %window_sums.1.main_ref, f32[136,128]{1,0:T(8,128)S(1)} %collective-permute-done.4.edge_ref), custom_call_target="tpu_custom_call" | custom-call | flops 500000000 | bytes 1048576 | tf_op jit(solution)/shard_map/coherence/pallas_call | solution.py:349
  (2 shorter events, 0.1 us)
Async XLA Ops:
  0.0 16.9 %copy-start.4 = (s32[8,2]{0,1:T(2,128)S(1)}, s32[8,2]{0,1:T(2,128)}, u32[]{:S(2)}) copy-start(s32[8,2]{0,1:T(2,128)} %param.9) | copy-start | bytes 196
  0.0 17.0 %copy-start = (f32[2,1,1024]{2,1,0:T(1,128)S(1)}, f32[2,1,1024]{2,1,0:T(1,128)}, u32[]{:S(2)}) copy-start(f32[2,1,1024]{2,1,0:T(1,128)} %taps_ref.3) | copy-start | bytes 24580
  0.0 17.0 %copy-start.1 = (s32[4]{0:T(128)S(1)}, s32[4]{0:T(128)}, u32[]{:S(2)}) copy-start(s32[4]{0:T(128)} %pairing_ref.1) | copy-start | bytes 52
  4.5 39.4 %all-to-all-start = ((f32[64,32,128]{2,1,0:T(8,128)}), f32[64,32,128]{2,1,0:T(8,128)S(1)}, u32[]{:S(2)}, u32[]{:S(2)}) async-start(f32[64,32,128]{2,1,0:T(8,128)} %range_filter.1), calls=%async_computation | async-start | bytes 2097152 | tf_op jit(solution)/shard_map/all_to_all | solution.py:315
  18.3 0.6 copy-start.2
  46.9 11.7 %collective-permute-start = (f32[2,312,128]{2,1,0:T(8,128)S(1)}, f32[2,312,128]{2,1,0:T(8,128)S(1)}, u32[]{:S(2)}, u32[]{:S(2)}) collective-permute-start(f32[2,312,128]{2,1,0:T(8,128)S(1)} %get-tuple-element.26), channel_id=1, source_target_pairs={{0,128},{64,192},{128,0},{192,64},{1,129},{65,193},{129,1},{193,65... | collective-permute-start | bytes 958472 | tf_op jit(solution)/shard_map/ppermute | solution.py:333
  50.6 8.0 %collective-permute-start.2 = (f32[2,272,128]{2,1,0:T(8,128)S(1)}, f32[2,272,128]{2,1,0:T(8,128)S(1)}, u32[]{:S(2)}, u32[]{:S(2)}) collective-permute-start(f32[2,272,128]{2,1,0:T(8,128)S(1)} %get-tuple-element.28), channel_id=1, source_target_pairs={{0,64},{64,0},{128,192},{192,128},{1,65},{65,1},{129,193},{193,129... | collective-permute-start | bytes 835592 | tf_op jit(solution)/shard_map/ppermute | solution.py:333
  50.7 10.6 %collective-permute-start.1 = (f32[2,272,128]{2,1,0:T(8,128)S(1)}, f32[2,272,128]{2,1,0:T(8,128)S(1)}, u32[]{:S(2)}, u32[]{:S(2)}) collective-permute-start(f32[2,272,128]{2,1,0:T(8,128)S(1)} %get-tuple-element.27), channel_id=1, source_target_pairs={{0,192},{64,128},{128,64},{192,0},{1,193},{65,129},{129,65},{193,1... | collective-permute-start | bytes 835592 | tf_op jit(solution)/shard_map/ppermute | solution.py:333
  58.6 1.2 %collective-permute-start.3 = (f32[2,40,128]{2,1,0:T(8,128)S(1)}, f32[2,40,128]{2,1,0:T(8,128)S(1)}, u32[]{:S(2)}, u32[]{:S(2)}) collective-permute-start(f32[2,40,128]{2,1,0:T(8,128)S(1)} %slice.4), channel_id=1, source_target_pairs={{0,64},{64,0},{128,192},{192,128},{1,65},{65,1},{129,193},{193,129... | collective-permute-start | bytes 122888 | tf_op jit(solution)/shard_map/ppermute | solution.py:334
  60.1 7.4 %copy-start.3 = (bf16[2,128,128]{2,1,0:T(8,128)(2,1)S(1)}, bf16[2,128,128]{2,1,0:T(8,128)(2,1)}, u32[]{:S(2)}) copy-start(bf16[2,128,128]{2,1,0:T(8,128)(2,1)} %copy-done.2) | copy-start | bytes 196612
  60.1 7.4 %collective-permute-start.4 = (f32[136,128]{1,0:T(8,128)S(1)}, f32[136,128]{1,0:T(8,128)S(1)}, u32[]{:S(2)}, u32[]{:S(2)}) collective-permute-start(f32[136,128]{1,0:T(8,128)S(1)} %edge.1), channel_id=1, source_target_pairs={{0,63},{1,0},{2,1},{3,2},{4,3},{5,4},{6,5},{7,6},{8,7},{9,8},{10,9... | collective-permute-start | bytes 208904 | tf_op jit(solution)/shard_map/ppermute | solution.py:344

commit v13 on v12

--- a/solution.py
+++ b/solution.py
@@ -158,32 +158,28 @@
 def other_quarters(x_ref, t_ref, order_ref, oa, ob, done_ref, x_hi, x_lo):
     done_ref[...] = jnp.zeros((8, 128), F32)
     split_pulses(x_ref, x_hi, x_lo)
-    azimuth_quarter(2, (t_ref, x_hi, x_lo), oa)
-    azimuth_quarter(3, (t_ref, x_hi, x_lo), ob)
+    me = lax.axis_index("chan")
+    for q in range(4):
+        @pl.when((me ^ 2) == q)
+        def _(q=q):
+            for which, o_ref in ((q, oa), (q ^ 1, ob)):
+                value = quarter_rows(which, slice(0, 272), t_ref, x_hi, x_lo, COLUMN[which // 2])
+                for part in range(2):
+                    o_ref[part, 0:272, :] = value[part]
+            low, high = (oa, ob) if q % 2 == 0 else (ob, oa)
+            for part in range(2):
+                low[part, 264:272, :] = high[part, 8:16, :]
+                high[part, 0:8, :] = low[part, 256:264, :]
+                if q < 2:
+                    low[part, 0:8, :] = jnp.zeros((8, 128), F32)
+                else:
+                    high[part, 264:272, :] = jnp.zeros((8, 128), F32)
+
     for part in range(2):
         oa[part, 272:312, :] = jnp.zeros((40, 128), F32)
         for j in range(7):
             size = min(40, 272 - 40 * j)
             oa[part, 272:272 + size, 16 * j:16 * j + 16] = ob[part, 40 * j:40 * j + size, 0:16]
-
-
-def azimuth_quarter(k, taps, out_ref):
-    me = lax.axis_index("chan")
-    for q in range(4):
-        @pl.when((me ^ k) == q)
-        def _(q=q):
-            own = quarter_rows(q, slice(0, 272), *taps, COLUMN[q // 2])
-            shared = quarter_rows(q ^ 1, slice(256, 272) if q % 2 else slice(0, 16), *taps, COLUMN[q // 2])
-            for part in range(2):
-                out_ref[part, 0:272, :] = own[part]
-                if q % 2:
-                    out_ref[part, 0:8, :] = shared[part][0:8]
-                else:
-                    out_ref[part, 264:272, :] = shared[part][8:16]
-                if q == 0:
-                    out_ref[part, 0:8, :] = jnp.zeros((8, 128), F32)
-                if q == 3:
-                    out_ref[part, 264:272, :] = jnp.zeros((8, 128), F32)
 
 
 def azimuth_own(order_ref, taps_ref, x_hi, x_lo, o0, o1, t_ref, y_ref):

time: 69.4 us -> 68.6 us (0.988)
  Pallas kernels: 14 us -> 13 us
    pallas_call x1, Pallas kernels: 2.87 us -> 2.06 us  [body(): call(other_quarters, 'azimuth_other', (shape(2, 312, 128), shape(2, 272,...]
where the time goes in v13:
time: 68.6 us; the launch traced here: 68.4 us
  waiting for transfers between devices  37.8 us (55%)
  starting transfers between devices  16.7 us (24%)
  Pallas kernels  13 us (19%)
  local copies, waits for them, and re-layouts  0.73 us (1%)
    all_to_all x1, waiting for transfers between devices, body(): lax.all_to_all(parted, 'wide', split_axis=0, concat_axis=0, tiled=True)  25 us
    all_to_all x1, starting transfers between devices, body(): lax.all_to_all(parted, 'wide', split_axis=0, concat_axis=0, tiled=True)  12.3 us
    ppermute x3, waiting for transfers between devices, body(): lax.ppermute(p, 'chan', [(i, i ^ k) for i in range(4)])  6.44 us
    ppermute x1, waiting for transfers between devices, body(): after = lax.ppermute(edge, 'wide', [(i, (i - 1) % 64) for i in range(64)])  5.22 us
    pallas_call x1, Pallas kernels, body(): call(range_kernel, 'range_filter', shape(64, 32, 128), [pltpu.VMEM((2, 16...  4.52 us
    ppermute x3, starting transfers between devices, body(): lax.ppermute(p, 'chan', [(i, i ^ k) for i in range(4)])  4.02 us
    pallas_call x1, Pallas kernels, body(): call(azimuth_own, 'azimuth_own', (shape(2, 272, 128),) * 2, [pltpu.VMEM((...  2.07 us
    pallas_call x1, Pallas kernels, body(): call(other_quarters, 'azimuth_other', (shape(2, 312, 128), shape(2, 272,...  2.06 us
  transfers between devices with their start and end apart: 6, of which 5 were waited for; matrix products, arithmetic and copies ran while one was open for 0% of the time, Pallas kernels for 7%

profile of v13, /device:TPU:62, one launch (start us, length us, event | category | flops | bytes accessed | tf_op | source)
XLA Modules:
  0.0 68.4 jit_solution(15693292287837789350)
XLA Ops:
  0.0 0.0 copy-start.4
  0.0 0.0 copy-start
  0.0 0.0 copy-start.1
  0.0 4.5 %range_filter.1 = f32[64,32,128]{2,1,0:T(8,128)} custom-call(f32[2,16,8192]{2,1,0:T(8,128)} %bitcast.3, f32[2,1,512]{2,1,0:T(1,128)} %chirp_hbm.1), custom_call_target="tpu_custom_call" | custom-call | flops 2000000000 | bytes 2097152 | tf_op jit(solution)/shard_map/range_filter/pallas_call | solution.py:304
  4.5 12.3 %all-to-all-start = ((f32[64,32,128]{2,1,0:T(8,128)}), f32[64,32,128]{2,1,0:T(8,128)S(1)}, u32[]{:S(2)}, u32[]{:S(2)}) async-start(f32[64,32,128]{2,1,0:T(8,128)} %range_filter.1), calls=%async_computation | async-start | bytes 2097152 | tf_op jit(solution)/shard_map/all_to_all | solution.py:311
  16.9 0.0 copy-done.4
  16.9 0.1 copy.6.offsets_ref
  17.0 0.0 copy-done
  17.0 0.0 copy-done.1
  17.0 1.4 %prepare.1 = (bf16[4,272,1024]{2,1,0:T(8,128)(2,1)S(1)}, f32[4,8,128]{2,1,0:T(8,128)S(1)}, bf16[2,128,256]{2,1,0:T(8,128)(2,1)S(1)}, bf16[2,128,128]{2,1,0:T(8,128)(2,1)S(1)}, bf16[2,128,128]{2,1,0:T(8,128)(2,1)S(1)}) custom-call(s32[4]{0:T(128)S(1)} %copy-done.1, s32[8,2]{1,0:T(8,128)S(1)} %copy.6.offsets_ref, f32[2,1,1024]{2,1,0:T(1,128)S(1)} %copy-done), custom_call_target="tpu_custom_call" | custom-call | flops 1000000000 | bytes 1048576 | tf_op jit(solution)/shard_map/prepare/pallas_call | solution.py:312
  18.3 0.0 copy-start.2
  18.3 0.6 copy-done.2
  19.0 25.0 %all-to-all-done.x_ref = f32[64,32,128]{2,1,0:T(8,128)S(1)} async-done(((f32[64,32,128]{2,1,0:T(8,128)}), f32[64,32,128]{2,1,0:T(8,128)S(1)}, u32[]{:S(2)}, u32[]{:S(2)}) %all-to-all-start) | async-done | bytes 1048608 | tf_op jit(solution)/shard_map/all_to_all | solution.py:311
  44.0 2.1 %azimuth_other.1 = (f32[2,312,128]{2,1,0:T(8,128)S(1)}, f32[2,272,128]{2,1,0:T(8,128)S(1)}, f32[8,128]{1,0:T(8,128)S(1)}, bf16[1024,256]{1,0:T(8,128)(2,1)S(1)}, bf16[1024,256]{1,0:T(8,128)(2,1)S(1)}) custom-call(f32[64,32,128]{2,1,0:T(8,128)S(1)} %all-to-all-done.x_ref, bf16[4,272,1024]{2,1,0:T(8,128)(2,1)S(1)} %get-tuple-element.21.t_ref, ...), custom_call_target="tpu_custom_call" | custom-call | flops 1000000000 | bytes 1000 | tf_op jit(solution)/shard_map/azimuth_other/pallas_call | solution.py:319
  46.1 1.5 %collective-permute-start = (f32[2,312,128]{2,1,0:T(8,128)S(1)}, f32[2,312,128]{2,1,0:T(8,128)S(1)}, u32[]{:S(2)}, u32[]{:S(2)}) collective-permute-start(f32[2,312,128]{2,1,0:T(8,128)S(1)} %get-tuple-element.26), channel_id=1, source_target_pairs={{0,128},{64,192},{128,0},{192,64},{1,129},{65,193},{129,1},{193,65... | collective-permute-start | bytes 958472 | tf_op jit(solution)/shard_map/ppermute | solution.py:329
  47.5 2.1 %azimuth_own.1 = (f32[2,272,128]{2,1,0:T(8,128)S(1)}, f32[2,272,128]{2,1,0:T(8,128)S(1)}) custom-call(f32[8,128]{1,0:T(8,128)S(1)} %get-tuple-element.22.order_ref, f32[2,1,1024]{2,1,0:T(1,128)S(1)} %copy-done, bf16[1024,256]{1,0:T(8,128)(2,1)S(1)} %get-tuple-element.23.x_hi, bf16[1024,256]{1,0:T(8,128)(2,1)S(1)} %get-tuple-element.24.x_lo), custom_call_target="tpu_custom_call" | custom-call | flops 1000 | bytes 1000 | tf_op jit(solution)/shard_map/azimuth_own/pallas_call | solution.py:324
  49.6 0.3 collective-permute-start.2
  49.9 2.2 %collective-permute-start.1 = (f32[2,272,128]{2,1,0:T(8,128)S(1)}, f32[2,272,128]{2,1,0:T(8,128)S(1)}, u32[]{:S(2)}, u32[]{:S(2)}) collective-permute-start(f32[2,272,128]{2,1,0:T(8,128)S(1)} %get-tuple-element.27), channel_id=1, source_target_pairs={{0,192},{64,128},{128,64},{192,0},{1,193},{65,129},{129,65},{193,1... | collective-permute-start | bytes 835592 | tf_op jit(solution)/shard_map/ppermute | solution.py:329
  52.2 5.6 %collective-permute-done.ya = f32[2,312,128]{2,1,0:T(8,128)S(1)} collective-permute-done((f32[2,312,128]{2,1,0:T(8,128)S(1)}, f32[2,312,128]{2,1,0:T(8,128)S(1)}, u32[]{:S(2)}, u32[]{:S(2)}) %collective-permute-start) | collective-permute-done | bytes 319520 | tf_op jit(solution)/shard_map/ppermute | solution.py:329
  57.8 0.0 collective-permute-start.3
  57.8 0.1 two_receivers.1.first_ref.part_ref
  57.8 0.0 collective-permute-done.2.y1
  57.9 1.1 %collective-permute-done.3.passed = f32[2,40,128]{2,1,0:T(8,128)S(1)} collective-permute-done((f32[2,40,128]{2,1,0:T(8,128)S(1)}, f32[2,40,128]{2,1,0:T(8,128)S(1)}, u32[]{:S(2)}, u32[]{:S(2)}) %collective-permute-start.3) | collective-permute-done | bytes 40992 | tf_op jit(solution)/shard_map/ppermute | solution.py:330
  59.0 0.3 edge.1
  59.3 0.0 copy-start.3
  59.3 0.4 collective-permute-start.4
  59.7 0.8 %collective-permute-done.1.yb = f32[2,272,128]{2,1,0:T(8,128)S(1)} collective-permute-done((f32[2,272,128]{2,1,0:T(8,128)S(1)}, f32[2,272,128]{2,1,0:T(8,128)S(1)}, u32[]{:S(2)}, u32[]{:S(2)}) %collective-permute-start.1) | collective-permute-done | bytes 278560 | tf_op jit(solution)/shard_map/ppermute | solution.py:329
  60.6 0.9 %window_sums.1.main_ref = f32[2,512,128]{2,1,0:T(8,128)S(1)} custom-call(f32[4,8,128]{2,1,0:T(8,128)S(1)} %get-tuple-element.19.weight_ref, bf16[2,128,256]{2,1,0:T(8,128)(2,1)S(1)} %get-tuple-element.17.rows_ref, bf16[2,128,128]{2,1,0:T(8,128)(2,1)S(1)} %get-tuple-element.20.near_ref, f32[4,272,128]{2,1,0:T(8,128)S(1)} %three_receivers.1.part_ref, ...), custom_call_target="tpu_custom_call" | custom-call | flops 500000000 | bytes 1048576 | tf_op jit(solution)/shard_map/window_sums/pallas_call | solution.py:341
  61.5 5.2 %collective-permute-done.4.edge_ref = f32[136,128]{1,0:T(8,128)S(1)} collective-permute-done((f32[136,128]{1,0:T(8,128)S(1)}, f32[136,128]{1,0:T(8,128)S(1)}, u32[]{:S(2)}, u32[]{:S(2)}) %collective-permute-start.4) | collective-permute-done | bytes 69664 | tf_op jit(solution)/shard_map/ppermute | solution.py:340
  66.7 0.0 copy-done.3
  66.7 1.7 %coherence.1 = f32[2,256,128]{2,1,0:T(8,128)} custom-call(bf16[2,128,256]{2,1,0:T(8,128)(2,1)S(1)} %get-tuple-element.17.rows_ref, bf16[2,128,128]{2,1,0:T(8,128)(2,1)S(1)} %copy-done.3, f32[2,512,128]{2,1,0:T(8,128)S(1)} %window_sums.1.main_ref, f32[136,128]{1,0:T(8,128)S(1)} %collective-permute-done.4.edge_ref), custom_call_target="tpu_custom_call" | custom-call | flops 500000000 | bytes 1048576 | tf_op jit(solution)/shard_map/coherence/pallas_call | solution.py:345
  (2 shorter events, 0.1 us)
Async XLA Ops:
  0.0 16.9 %copy-start.4 = (s32[8,2]{0,1:T(2,128)S(1)}, s32[8,2]{0,1:T(2,128)}, u32[]{:S(2)}) copy-start(s32[8,2]{0,1:T(2,128)} %param.9) | copy-start | bytes 196
  0.0 17.0 %copy-start = (f32[2,1,1024]{2,1,0:T(1,128)S(1)}, f32[2,1,1024]{2,1,0:T(1,128)}, u32[]{:S(2)}) copy-start(f32[2,1,1024]{2,1,0:T(1,128)} %taps_ref.3) | copy-start | bytes 24580
  0.0 17.0 %copy-start.1 = (s32[4]{0:T(128)S(1)}, s32[4]{0:T(128)}, u32[]{:S(2)}) copy-start(s32[4]{0:T(128)} %pairing_ref.1) | copy-start | bytes 52
  4.5 39.4 %all-to-all-start = ((f32[64,32,128]{2,1,0:T(8,128)}), f32[64,32,128]{2,1,0:T(8,128)S(1)}, u32[]{:S(2)}, u32[]{:S(2)}) async-start(f32[64,32,128]{2,1,0:T(8,128)} %range_filter.1), calls=%async_computation | async-start | bytes 2097152 | tf_op jit(solution)/shard_map/all_to_all | solution.py:311
  18.3 0.6 copy-start.2
  46.1 11.7 %collective-permute-start = (f32[2,312,128]{2,1,0:T(8,128)S(1)}, f32[2,312,128]{2,1,0:T(8,128)S(1)}, u32[]{:S(2)}, u32[]{:S(2)}) collective-permute-start(f32[2,312,128]{2,1,0:T(8,128)S(1)} %get-tuple-element.26), channel_id=1, source_target_pairs={{0,128},{64,192},{128,0},{192,64},{1,129},{65,193},{129,1},{193,65... | collective-permute-start | bytes 958472 | tf_op jit(solution)/shard_map/ppermute | solution.py:329
  49.6 8.2 %collective-permute-start.2 = (f32[2,272,128]{2,1,0:T(8,128)S(1)}, f32[2,272,128]{2,1,0:T(8,128)S(1)}, u32[]{:S(2)}, u32[]{:S(2)}) collective-permute-start(f32[2,272,128]{2,1,0:T(8,128)S(1)} %get-tuple-element.28), channel_id=1, source_target_pairs={{0,64},{64,0},{128,192},{192,128},{1,65},{65,1},{129,193},{193,129... | collective-permute-start | bytes 835592 | tf_op jit(solution)/shard_map/ppermute | solution.py:329
  49.9 10.6 %collective-permute-start.1 = (f32[2,272,128]{2,1,0:T(8,128)S(1)}, f32[2,272,128]{2,1,0:T(8,128)S(1)}, u32[]{:S(2)}, u32[]{:S(2)}) collective-permute-start(f32[2,272,128]{2,1,0:T(8,128)S(1)} %get-tuple-element.27), channel_id=1, source_target_pairs={{0,192},{64,128},{128,64},{192,0},{1,193},{65,129},{129,65},{193,1... | collective-permute-start | bytes 835592 | tf_op jit(solution)/shard_map/ppermute | solution.py:329
  57.8 1.2 %collective-permute-start.3 = (f32[2,40,128]{2,1,0:T(8,128)S(1)}, f32[2,40,128]{2,1,0:T(8,128)S(1)}, u32[]{:S(2)}, u32[]{:S(2)}) collective-permute-start(f32[2,40,128]{2,1,0:T(8,128)S(1)} %slice.4), channel_id=1, source_target_pairs={{0,64},{64,0},{128,192},{192,128},{1,65},{65,1},{129,193},{193,129... | collective-permute-start | bytes 122888 | tf_op jit(solution)/shard_map/ppermute | solution.py:330
  59.3 7.4 %copy-start.3 = (bf16[2,128,128]{2,1,0:T(8,128)(2,1)S(1)}, bf16[2,128,128]{2,1,0:T(8,128)(2,1)}, u32[]{:S(2)}) copy-start(bf16[2,128,128]{2,1,0:T(8,128)(2,1)} %copy-done.2) | copy-start | bytes 196612
  59.3 7.4 %collective-permute-start.4 = (f32[136,128]{1,0:T(8,128)S(1)}, f32[136,128]{1,0:T(8,128)S(1)}, u32[]{:S(2)}, u32[]{:S(2)}) collective-permute-start(f32[136,128]{1,0:T(8,128)S(1)} %edge.1), channel_id=1, source_target_pairs={{0,63},{1,0},{2,1},{3,2},{4,3},{5,4},{6,5},{7,6},{8,7},{9,8},{10,9... | collective-permute-start | bytes 208904 | tf_op jit(solution)/shard_map/ppermute | solution.py:340
